TPU v7x, 256 devices: a whole 4x4x8 slice. The times are simulated.
256 devices in a mesh: gx: 8 (over z), gy: 16 (over y, x), gz: 2 (over core).
Axes of the slice: x: 4, y: 4, z: 8, core: 2. Of those that a mesh axis runs over, the one named last changes fastest.
Arguments:
- forcing: float32 [3, 128, 256, 256], P(None, 'gx', 'gy', 'gz'), may hold values from -6 to 6
- start_field: float32 [3, 128, 256, 256], P(None, 'gx', 'gy', 'gz'), may hold values from -6 to 6
- modulus: float32 [128, 256, 256], P('gx', 'gy', 'gz'), may hold values from 1 to 4
- corners: int32 [256, 3], P(('gx', 'gy', 'gz')), may hold values from 0 to 236, as said below
Outputs:
- displacement: float32 [3, 128, 256, 256], P(None, 'gx', 'gy', 'gz')
- new_modulus: float32 [128, 256, 256], P('gx', 'gy', 'gz')
Inputs may be any that keep to these rules, and one draw needn't show every extreme that they name: `corners`: subzone i is handled by device i // 1 in row-major order over (gx, gy, gz). In each dimension its corner lies within lo - 5 to lo + B + 5 - 2 * 10, where lo and B are that device's first voxel and voxel count in that dimension, and the subzone lies inside the grid.
All inputs are finite; a program needn't handle non-finite values.
Results may differ from a plain program's by a relative error of at most 0.0003.
Values sent between devices are 32-bit elements; how exact they have to be, the bound alone decides.
No kernel may reach another device: no remote copies, remote signals or barrier semaphores. Data moves between devices by JAX's collectives and lax.ppermute only.
A program may use at most 192 MiB of HBM per device.

v0:
```python
import math

import jax
import jax.numpy as jnp
from jax import lax
from jax.sharding import PartitionSpec as P

PC = 10
HALO = 6
FSWEEPS = 4


MASS_TERM = 0.5
DAMPING = 0.1
EPSILON = 1e-06
DIRECTIONS = ((0, True), (0, False), (1, True), (1, False), (2, True), (2, False))


def extended(block, sides, width):
    for axis, dim in sides:
        count = lax.axis_size(axis)
        forward = [(i, i + 1) for i in range(count - 1)]
        backward = [(target, source) for source, target in forward]
        low = lax.ppermute(
            lax.slice_in_dim(block, block.shape[dim] - width, None, axis=dim), axis, forward
        )
        high = lax.ppermute(lax.slice_in_dim(block, 0, width, axis=dim), axis, backward)
        block = jnp.concatenate([low, block, high], axis=dim)
    return block


def neighbor(values, which_axis, upward):
    index_list = [slice(1, -1), slice(1, -1), slice(1, -1)]
    index_list[which_axis] = slice(2, None) if upward else slice(0, -2)
    return values[tuple([slice(None)] * (values.ndim - 3) + index_list)]


def center(values):
    return values[tuple([slice(None)] * (values.ndim - 3) + [slice(1, -1)] * 3)]


def relax_sweep(field_pad, modulus_pad, forcing_mid):
    middle = center(modulus_pad)
    numerator = forcing_mid
    denominator = MASS_TERM
    for which_axis, upward in DIRECTIONS:
        coupling = 0.5 * (middle + neighbor(modulus_pad, which_axis, upward))
        numerator = numerator + coupling * neighbor(field_pad, which_axis, upward)
        denominator = denominator + coupling
    return numerator / denominator


def block_sum(values, coarse):
    return values.reshape(values.shape[0], coarse, 2, coarse, 2, coarse, 2).sum(axis=(2, 4, 6))


def shift_coarse(values, offset):
    padded = jnp.pad(values, 1)
    coarse = values.shape[0]
    begin = (1 - offset[0], 1 - offset[1], 1 - offset[2])
    return lax.slice(padded, begin, (begin[0] + coarse, begin[1] + coarse, begin[2] + coarse))


def zone_update(field_rim, forcing_zone, modulus_rim):
    zone_span = forcing_zone.shape[-1]
    coarse = zone_span // 2
    params = coarse**3
    field_mid = center(field_rim)
    modulus_mid = center(modulus_rim)
    applied = MASS_TERM * field_mid
    laplace = jnp.zeros_like(field_mid)
    face_flows = []
    for which_axis, upward in DIRECTIONS:
        field_next = neighbor(field_rim, which_axis, upward)
        modulus_next = neighbor(modulus_rim, which_axis, upward)
        change = field_mid - field_next
        applied = applied + 0.5 * (modulus_mid + modulus_next) * change
        laplace = laplace + change
        face_flows.append(-0.5 * modulus_next * change)
    coarse_resid = block_sum(forcing_zone - applied, coarse)
    diagonal = block_sum(-0.5 * modulus_mid * laplace, coarse)
    position = jnp.arange(coarse)
    columns = {}
    for (which_axis, upward), face_flow in zip(DIRECTIONS, face_flows):
        blocks = face_flow.reshape(3, coarse, 2, coarse, 2, coarse, 2)
        inner_pos = 0 if upward else 1
        same_part = lax.index_in_dim(blocks, inner_pos, 2 + 2 * which_axis, keepdims=True).sum(
            axis=(2, 4, 6)
        )
        cross_part = lax.index_in_dim(blocks, 1 - inner_pos, 2 + 2 * which_axis, keepdims=True).sum(
            axis=(2, 4, 6)
        )
        diagonal = diagonal + same_part
        in_range = position < coarse - 1 if upward else position > 0
        shape_list = [1, 1, 1]
        shape_list[which_axis] = coarse
        in_range = in_range.reshape(shape_list)
        step_list = [0, 0, 0]
        step_list[which_axis] = 1 if upward else -1
        columns[tuple(step_list)] = jnp.where(in_range, cross_part, 0.0)
    columns[0, 0, 0] = diagonal
    offset_list = list(columns.keys())
    gradient = jnp.zeros((coarse, coarse, coarse), jnp.float32)
    band_sums = {}
    for offset_one in offset_list:
        gradient = gradient + shift_coarse(
            jnp.sum(columns[offset_one] * coarse_resid, axis=0), offset_one
        )
        for offset_two in offset_list:
            band_key = (
                offset_two[0] - offset_one[0],
                offset_two[1] - offset_one[1],
                offset_two[2] - offset_one[2],
            )
            term_value = shift_coarse(
                jnp.sum(columns[offset_one] * columns[offset_two], axis=0), offset_one
            )
            if band_key in band_sums:
                band_sums[band_key] = band_sums[band_key] + term_value
            else:
                band_sums[band_key] = term_value
    base_rows = jnp.arange(params, dtype=jnp.int32)
    row_parts = []
    col_parts = []
    value_parts = []
    for band_key, band_value in band_sums.items():
        linear = band_key[0] * coarse * coarse + band_key[1] * coarse + band_key[2]
        target = base_rows + linear
        target = jnp.where((target >= 0) & (target < params), target, params).astype(jnp.int32)
        row_parts.append(base_rows)
        col_parts.append(target)
        value_parts.append(band_value.reshape(params))
    hessian = (
        jnp.zeros((params, params), jnp.float32)
        .at[jnp.concatenate(row_parts), jnp.concatenate(col_parts)]
        .add(jnp.concatenate(value_parts), mode="drop")
    )
    ridge = DAMPING * jnp.sum(band_sums[0, 0, 0]) / params + EPSILON
    hessian = hessian + ridge * jnp.eye(params, dtype=jnp.float32)
    factor = jnp.linalg.cholesky(hessian)
    right_hand = gradient.reshape(params, 1)
    middle_sol = lax.linalg.triangular_solve(factor, right_hand, left_side=True, lower=True)
    solution = lax.linalg.triangular_solve(
        factor, middle_sol, left_side=True, lower=True, transpose_a=True
    )
    update = -solution.reshape(coarse, coarse, coarse)
    update = jnp.repeat(jnp.repeat(jnp.repeat(update, 2, axis=0), 2, axis=1), 2, axis=2)
    ramp_curve = jnp.sin(math.pi * (jnp.arange(zone_span, dtype=jnp.float32) + 0.5) / zone_span)
    taper_weight = ramp_curve[:, None, None] * ramp_curve[None, :, None] * ramp_curve[None, None, :]
    return taper_weight * modulus_mid * update


def face_halo(values):
    return extended(values, (("gx", 1), ("gy", 2), ("gz", 3)), 1)


def pack_margins(values, which_axis, margin):
    inner = values.shape[which_axis] - 2 * margin
    return jnp.concatenate(
        [
            lax.slice_in_dim(values, 0, margin, axis=which_axis),
            lax.slice_in_dim(values, 2 * margin, inner, axis=which_axis),
            lax.slice_in_dim(values, inner + margin, inner + 2 * margin, axis=which_axis),
        ],
        axis=which_axis,
    )


def fold_margins(values, received, which_axis, margin):
    inner = values.shape[which_axis] - 2 * margin
    middle_shape = list(values.shape)
    middle_shape[which_axis] = inner - 2 * margin
    added = jnp.concatenate(
        [
            lax.slice_in_dim(received, 0, margin, axis=which_axis),
            jnp.zeros(middle_shape, jnp.float32),
            lax.slice_in_dim(received, inner + margin, inner + 2 * margin, axis=which_axis),
        ],
        axis=which_axis,
    )
    return lax.slice_in_dim(values, margin, inner + margin, axis=which_axis) + added


def body(forcing, start_field, modulus, corners):
    brick_shape = modulus.shape
    zone_span = 2 * PC
    lower = (
        lax.axis_index("gx") * brick_shape[0],
        lax.axis_index("gy") * brick_shape[1],
        lax.axis_index("gz") * brick_shape[2],
    )
    modulus_pad = face_halo(modulus[None])[0]
    field = start_field
    for sweep_count in range(FSWEEPS):
        field = relax_sweep(face_halo(field), modulus_pad, forcing)
    stacked = jnp.concatenate([field, forcing, modulus[None]], axis=0)
    widened = extended(stacked, (("gx", 1), ("gy", 2), ("gz", 3)), HALO)
    field_ext = widened[:3]
    forcing_ext = widened[3:6]
    modulus_ext = widened[6]
    lower_vec = jnp.stack([lower[0], lower[1], lower[2]]).astype(jnp.int32)
    starts = (corners - lower_vec[None, :] + HALO - 1).astype(jnp.int32)
    anchor = jnp.zeros((), jnp.int32)

    def one_zone(begin):
        field_rim = lax.dynamic_slice(
            field_ext,
            (anchor, begin[0], begin[1], begin[2]),
            (3, zone_span + 2, zone_span + 2, zone_span + 2),
        )
        modulus_rim = lax.dynamic_slice(
            modulus_ext,
            (begin[0], begin[1], begin[2]),
            (zone_span + 2, zone_span + 2, zone_span + 2),
        )
        forcing_zone = lax.dynamic_slice(
            forcing_ext,
            (anchor, begin[0] + 1, begin[1] + 1, begin[2] + 1),
            (3, zone_span, zone_span, zone_span),
        )
        return zone_update(field_rim, forcing_zone, modulus_rim)

    pieces = lax.map(one_zone, starts)

    def add_piece(number, total):
        begin = starts[number] + 1
        place = (begin[0], begin[1], begin[2])
        current = lax.dynamic_slice(total, place, (zone_span, zone_span, zone_span))
        return lax.dynamic_update_slice(total, current + pieces[number], place)

    summed = lax.fori_loop(0, starts.shape[0], add_piece, jnp.zeros(modulus_ext.shape, jnp.float32))
    received = extended(pack_margins(summed, 0, HALO), (("gx", 0),), HALO)
    summed = fold_margins(summed, received, 0, HALO)
    received = extended(pack_margins(summed, 1, HALO), (("gy", 1),), HALO)
    summed = fold_margins(summed, received, 1, HALO)
    received = extended(pack_margins(summed, 2, HALO), (("gz", 2),), HALO)
    summed = fold_margins(summed, received, 2, HALO)
    return (field, modulus + summed)


def solution(mesh):
    placed = (
        P(None, "gx", "gy", "gz"),
        P(None, "gx", "gy", "gz"),
        P("gx", "gy", "gz"),
        P(("gx", "gy", "gz"), None),
    )
    return jax.shard_map(
        body,
        mesh=mesh,
        in_specs=placed,
        out_specs=(P(None, "gx", "gy", "gz"), P("gx", "gy", "gz")),
        check_vma=False,
    )
```

profile of v0, /device:TPU:79, one launch (start us, length us, event | category | flops | bytes accessed | tf_op | source)
XLA Modules:
  0.0 1065.6 jit_solution(13003608803102773810)
XLA Ops:
  7.6 4.7 collective-permute-start.7
  27.8 4.6 collective-permute-start.5
  50.2 7.6 pad_maximum_fusion.1
  74.0 4.9 collective-permute-start.13
  95.9 7.6 pad_maximum_fusion.2
  121.3 4.9 collective-permute-start.19
  127.2 5.8 collective-permute-start.21
  145.6 7.6 pad_maximum_fusion.3
  171.0 5.1 collective-permute-start.25
  177.1 5.8 collective-permute-start.27
  195.4 7.6 pad_maximum_fusion.4
  218.9 5.1 collective-permute-start.30
  230.3 5.9 collective-permute-done.31
  236.6 5.8 collective-permute-start.32
  245.1 12.0 %copy.241 = f32[7,28,16,128]{2,1,3,0:T(8,128)} copy(f32[7,28,16,128]{3,2,1,0:T(8,128)S(1)} %pad_maximum_fusion.5) | data formatting | bytes 3211264 | tf_op jit(solution)/shard_map/concatenate | solution.py:28
  257.0 13.0 %copy.240 = f32[7,28,6,128]{2,1,3,0:T(8,128)} copy(f32[7,28,6,128]{3,1,2,0:T(8,128)} %collective-permute-done.32) | data formatting | bytes 1204224 | tf_op jit(solution)/shard_map/ppermute | solution.py:24
  270.0 13.1 %copy.242 = f32[7,28,6,128]{2,1,3,0:T(8,128)} copy(f32[7,28,6,128]{3,1,2,0:T(8,128)} %collective-permute-done.33) | data formatting | bytes 1204224 | tf_op jit(solution)/shard_map/ppermute | solution.py:27
  283.1 15.8 %pad_maximum_fusion = f32[7,28,28,128]{2,1,3,0:T(8,128)S(1)} fusion(f32[7,28,6,128]{2,1,3,0:T(8,128)} %copy.242, f32[7,28,16,128]{2,1,3,0:T(8,128)} %copy.241, f32[7,28,6,128]{2,1,3,0:T(8,128)} %copy.240), kind=kLoop, calls=%fused_computation.3 | loop fusion | flops 1404928 | bytes 5619712 | tf_op jit(solution)/shard_map/concatenate | solution.py:28
  298.9 5.2 copy-done
  325.9 11.6 %copy.244 = f32[7,28,28,128]{3,2,1,0:T(8,128)} copy(f32[7,28,28,128]{2,1,3,0:T(8,128)} %copy-done) | data formatting | bytes 5619712 | tf_op jit(solution)/shard_map/concatenate | solution.py:28
  359.3 6.5 reshape.1550
  377.0 6.4 reshape.1522
  383.3 8.5 slice_reduce_fusion.7
  391.9 5.0 copy.254
  396.9 6.4 reshape.1521
  403.2 7.3 slice_reduce_fusion.8
  414.6 6.4 reshape.1520
  421.0 7.3 slice_reduce_fusion.9
  432.3 6.8 reshape.1524
  439.1 4.7 reduce_sum.626
  443.8 4.7 reduce_sum.596
  457.2 5.0 copy.258
  462.2 6.4 reshape.1523
  468.6 8.7 slice_reduce_fusion.6
  481.4 6.4 reshape.1519
  487.8 7.5 slice_reduce_fusion.10
  499.4 6.4 reshape.1518
  505.9 5.5 slice_reduce_fusion.11
  511.4 10.7 %multiply_reduce_fusion.9 = (f32[10,10,10]{2,1,0:T(8,128)}, f32[10,10,10]{2,1,0:T(8,128)}, f32[10,10,10]{2,1,0:T(8,128)}, f32[10,10,10]{2,1,0:T(8,128)}, f32[10,...) fusion(f32[3,10,10,10]{0,3,2,1:T(8,128)S(1)} %copy-done.19, ...), kind=kLoop, calls=%fused_computation.106 | loop fusion | flops 211000 | bytes 308020 | tf_op jit(solution)/shard_map/while/body/eval_jaxpr/reduce_sum | solution.py:116
  534.6 6.6 reshape.1576
  541.4 135.7 %scatter_fusion = f32[1000000]{0:T(1024)} fusion(f32[1000000]{0:T(1024)} %reshape.1576, s32[25000]{0:T(1024)S(1)} %copy-done.27, f32[25000]{0:T(1024)S(1)} %concatenate.365), kind=kCustom, calls=%fused_computation | custom fusion | flops 25000 | bytes 400000
  677.1 6.1 reshape.1578
  683.2 5.7 copy.261
  695.2 11.7 %cholesky.225 = f32[128,128]{1,0:T(8,128)S(1)} custom-call(f32[128,128]{1,0:T(8,128)S(1)} %cholesky.583), custom_call_target="Cholesky" | custom-call | tf_op jit(solution)/shard_map/while/body/eval_jaxpr/jit(cholesky)/cholesky | solution.py:140
  709.3 9.8 custom-call.80
  723.7 11.9 %cholesky.244 = f32[128,128]{1,0:T(8,128)S(1)} custom-call(f32[128,128]{1,0:T(8,128)S(1)} %cholesky.587), custom_call_target="Cholesky" | custom-call | tf_op jit(solution)/shard_map/while/body/eval_jaxpr/jit(cholesky)/cholesky | solution.py:140
  737.6 9.8 custom-call.81
  751.0 11.7 %cholesky.468 = f32[128,128]{1,0:T(8,128)S(1)} custom-call(f32[128,128]{1,0:T(8,128)S(1)} %cholesky.592), custom_call_target="Cholesky" | custom-call | tf_op jit(solution)/shard_map/while/body/eval_jaxpr/jit(cholesky)/cholesky | solution.py:140
  764.0 9.8 custom-call.82
  778.0 11.7 %cholesky.487 = f32[128,128]{1,0:T(8,128)S(1)} custom-call(f32[128,128]{1,0:T(8,128)S(1)} %cholesky.597), custom_call_target="Cholesky" | custom-call | tf_op jit(solution)/shard_map/while/body/eval_jaxpr/jit(cholesky)/cholesky | solution.py:140
  791.0 9.8 custom-call.83
  804.4 11.7 %cholesky.506 = f32[128,128]{1,0:T(8,128)S(1)} custom-call(f32[128,128]{1,0:T(8,128)S(1)} %cholesky.602), custom_call_target="Cholesky" | custom-call | tf_op jit(solution)/shard_map/while/body/eval_jaxpr/jit(cholesky)/cholesky | solution.py:140
  817.4 10.2 custom-call.84
  831.1 11.7 %cholesky.526 = f32[128,128]{1,0:T(8,128)S(1)} custom-call(f32[128,128]{1,0:T(8,128)S(1)} %cholesky.607), custom_call_target="Cholesky" | custom-call | tf_op jit(solution)/shard_map/while/body/eval_jaxpr/jit(cholesky)/cholesky | solution.py:140
  844.2 9.8 custom-call.85
  857.0 11.9 %cholesky.546 = f32[128,128]{1,0:T(8,128)S(1)} custom-call(f32[128,128]{1,0:T(8,128)S(1)} %cholesky.612), custom_call_target="Cholesky" | custom-call | tf_op jit(solution)/shard_map/while/body/eval_jaxpr/jit(cholesky)/cholesky | solution.py:140
  870.1 9.8 custom-call.86
  882.4 9.5 cholesky.567
  902.9 19.7 %while.1 = (s32[]{:T(128)}, f32[1000,1000]{1,0:T(8,128)}, s32[7,2]{0,1:T(2,128)S(1)}, f32[7,128,128]{2,1,0:T(8,128)S(1)}, s32[]{:T(128)}) while((s32[]{:T(128)}, f32[1000,1000]{1,0:T(8,128)}, s32[7,2]{0,1:T(2,128)S(1)}, f32[7,128,128]{2,1,0:T(8,128)S(1)}, s32[]{:T(128)}) %tuple.195), condition=%wide.while_cond, body=%wide.while_body.sunk | while | flops 2 | bytes 131181 | solution.py:143
  922.7 78.8 %custom-call.87 = f32[8,128,128]{1,2,0:T(8,128)S(1)} custom-call(f32[8,128,128]{2,1,0:T(8,128)S(1)} %pad_maximum_fusion.6), custom_call_target="InvertDiagBlocksLowerTriangular" | custom-call | tf_op jit(solution)/shard_map/while/body/eval_jaxpr/triangular_solve | solution.py:143
  1024.1 6.9 dynamic_update_slice.7
  1031.0 4.6 collective-permute-start.36
  1044.4 5.8 collective-permute-start.38
  1052.6 5.9 collective-permute-done.39
  (461 shorter events, 345.5 us)
Async XLA Ops:
  1.3 13.5 %collective-permute-start = (f32[1,1,16,128]{3,2,1,0:T(8,128)S(1)}, f32[1,1,16,128]{3,2,1,0:T(8,128)S(1)}, u32[]{:S(2)}, u32[]{:S(2)}) collective-permute-start(f32[1,1,16,128]{3,2,1,0:T(8,128)S(1)} %get-tuple-element.191), channel_id=1, source_target_pairs={{0,32},{32,64},{64,96},{96,128},{128,160},{160,192},{192,224},{1,3... | collective-permute-start | bytes 24584 | tf_op jit(solution)/shard_map/ppermute | solution.py:24
  4.9 9.9 collective-permute-start.1
  7.6 24.8 %collective-permute-start.7 = (f32[3,1,16,128]{3,2,1,0:T(8,128)S(1)}, f32[3,1,16,128]{3,2,1,0:T(8,128)S(1)}, u32[]{:S(2)}, u32[]{:S(2)}) collective-permute-start(f32[3,1,16,128]{3,2,1,0:T(8,128)S(1)} %get-tuple-element.153), channel_id=1, source_target_pairs={{0,32},{32,64},{64,96},{96,128},{128,160},{160,192},{192,224},{1,3... | collective-permute-start | bytes 73736 | tf_op jit(solution)/shard_map/ppermute | solution.py:24
  12.3 21.1 %collective-permute-start.6 = (f32[3,1,16,128]{3,2,1,0:T(8,128)S(1)}, f32[3,1,16,128]{3,2,1,0:T(8,128)S(1)}, u32[]{:S(2)}, u32[]{:S(2)}) collective-permute-start(f32[3,1,16,128]{3,2,1,0:T(8,128)S(1)} %get-tuple-element.152), channel_id=1, source_target_pairs={{32,0},{64,32},{96,64},{128,96},{160,128},{192,160},{224,192},{33,... | collective-permute-start | bytes 73736 | tf_op jit(solution)/shard_map/ppermute | solution.py:27
  15.7 5.8 collective-permute-start.2
  18.9 6.5 collective-permute-start.3
  26.5 12.4 %collective-permute-start.4 = (f32[1,18,18,1]{3,2,1,0:T(8,128)S(1)}, f32[1,18,18,1]{3,2,1,0:T(8,128)S(1)}, u32[]{:S(2)}, u32[]{:S(2)}) collective-permute-start(f32[1,18,18,1]{3,2,1,0:T(8,128)S(1)} %get-tuple-element.169), channel_id=1, source_target_pairs={{0,1},{2,3},{4,5},{6,7},{8,9},{10,11},{12,13},{14,15},{16,17},{18,... | collective-permute-start | bytes 3896 | tf_op jit(solution)/shard_map/ppermute | solution.py:24
  27.8 11.1 %collective-permute-start.5 = (f32[1,18,18,1]{3,2,1,0:T(8,128)S(1)}, f32[1,18,18,1]{3,2,1,0:T(8,128)S(1)}, u32[]{:S(2)}, u32[]{:S(2)}) collective-permute-start(f32[1,18,18,1]{3,2,1,0:T(8,128)S(1)} %get-tuple-element.170), channel_id=1, source_target_pairs={{1,0},{3,2},{5,4},{7,6},{9,8},{11,10},{13,12},{15,14},{17,16},{19,... | collective-permute-start | bytes 3896 | tf_op jit(solution)/shard_map/ppermute | solution.py:27
  33.6 10.0 collective-permute-start.9
  35.5 11.4 %collective-permute-start.8 = (f32[3,18,1,128]{3,1,2,0:T(8,128)S(1)}, f32[3,18,1,128]{3,1,2,0:T(8,128)S(1)}, u32[]{:S(2)}, u32[]{:S(2)}) collective-permute-start(f32[3,18,1,128]{3,1,2,0:T(8,128)S(1)} %copy.275), channel_id=1, source_target_pairs={{2,0},{4,2},{6,4},{8,6},{10,8},{12,10},{14,12},{16,14},{18,16},{20... | collective-permute-start | bytes 82952 | tf_op jit(solution)/shard_map/ppermute | solution.py:27
  60.0 8.1 collective-permute-start.10
  61.8 8.0 copy-start.9
  61.8 6.7 collective-permute-start.11
  68.0 17.7 %copy-start.36 = (s32[1,3]{1,0:T(1,128)S(1)}, s32[1,3]{1,0:T(1,128)}, u32[]{:S(2)}) copy-start(s32[1,3]{1,0:T(1,128)} %param.7) | copy-start | bytes 40
  72.0 6.9 collective-permute-start.12
  74.0 5.8 collective-permute-start.13
  79.8 9.4 collective-permute-start.15
  83.6 9.0 collective-permute-start.14
  105.7 10.0 collective-permute-start.16
  109.8 6.3 collective-permute-start.17
  115.6 10.6 copy-start.35
  119.3 7.2 collective-permute-start.18
  121.3 5.8 collective-permute-start.19
  127.2 11.7 %collective-permute-start.21 = (f32[3,18,1,128]{3,1,2,0:T(8,128)S(1)}, f32[3,18,1,128]{3,1,2,0:T(8,128)S(1)}, u32[]{:S(2)}, u32[]{:S(2)}) collective-permute-start(f32[3,18,1,128]{3,1,2,0:T(8,128)S(1)} %copy.280), channel_id=1, source_target_pairs={{0,2},{2,4},{4,6},{6,8},{8,10},{10,12},{12,14},{14,16},{16,18},{18... | collective-permute-start | bytes 82952 | tf_op jit(solution)/shard_map/ppermute | solution.py:24
  132.9 9.4 collective-permute-start.20
  155.4 10.0 collective-permute-start.22
  159.5 6.3 collective-permute-start.23
  169.0 7.1 collective-permute-start.24
  171.0 6.1 collective-permute-start.25
  177.1 11.5 %collective-permute-start.27 = (f32[3,18,1,128]{3,1,2,0:T(8,128)S(1)}, f32[3,18,1,128]{3,1,2,0:T(8,128)S(1)}, u32[]{:S(2)}, u32[]{:S(2)}) collective-permute-start(f32[3,18,1,128]{3,1,2,0:T(8,128)S(1)} %copy.282), channel_id=1, source_target_pairs={{0,2},{2,4},{4,6},{6,8},{8,10},{10,12},{12,14},{14,16},{16,18},{18... | collective-permute-start | bytes 82952 | tf_op jit(solution)/shard_map/ppermute | solution.py:24
  182.9 9.1 collective-permute-start.26
  205.1 10.0 collective-permute-start.28
  209.3 6.3 collective-permute-start.29
  210.6 16.5 %copy-start.33 = (f32[20]{0:T(128)}, f32[20]{0:T(128)S(1)}, u32[]{:S(2)}) copy-start(f32[20]{0:T(128)S(1)} %multiply_sine_fusion) | copy-start | bytes 244
  218.8 17.6 %copy-start.13 = (f32[3,16,16,128]{3,2,1,0:T(8,128)}, f32[3,16,16,128]{3,2,1,0:T(8,128)S(1)}, u32[]{:S(2)}) copy-start(f32[3,16,16,128]{3,2,1,0:T(8,128)S(1)} %fusion.41) | copy-start | bytes 1179652
  218.9 11.4 %collective-permute-start.30 = (f32[7,6,16,128]{3,2,1,0:T(8,128)S(1)}, f32[7,6,16,128]{3,2,1,0:T(8,128)S(1)}, u32[]{:S(2)}, u32[]{:S(2)}) collective-permute-start(f32[7,6,16,128]{3,2,1,0:T(8,128)S(1)} %get-tuple-element.127), channel_id=1, source_target_pairs={{0,32},{32,64},{64,96},{96,128},{128,160},{160,192},{192,224},{1,3... | collective-permute-start | bytes 1032200 | tf_op jit(solution)/shard_map/ppermute | solution.py:24
  224.1 12.1 %collective-permute-start.31 = (f32[7,6,16,128]{3,2,1,0:T(8,128)S(1)}, f32[7,6,16,128]{3,2,1,0:T(8,128)S(1)}, u32[]{:S(2)}, u32[]{:S(2)}) collective-permute-start(f32[7,6,16,128]{3,2,1,0:T(8,128)S(1)} %get-tuple-element.128), channel_id=1, source_target_pairs={{32,0},{64,32},{96,64},{128,96},{160,128},{192,160},{224,192},{33,... | collective-permute-start | bytes 1032200 | tf_op jit(solution)/shard_map/ppermute | solution.py:27
  236.6 20.4 %collective-permute-start.32 = (f32[7,28,6,128]{3,1,2,0:T(8,128)S(1)}, f32[7,28,6,128]{3,1,2,0:T(8,128)}, u32[]{:S(2)}, u32[]{:S(2)}) collective-permute-start(f32[7,28,6,128]{3,1,2,0:T(8,128)S(1)} %copy.283), channel_id=1, source_target_pairs={{0,2},{2,4},{4,6},{6,8},{8,10},{10,12},{12,14},{14,16},{16,18},{18... | collective-permute-start | bytes 1806344 | tf_op jit(solution)/shard_map/ppermute | solution.py:24
  242.5 27.6 %collective-permute-start.33 = (f32[7,28,6,128]{3,1,2,0:T(8,128)S(1)}, f32[7,28,6,128]{3,1,2,0:T(8,128)}, u32[]{:S(2)}, u32[]{:S(2)}) collective-permute-start(f32[7,28,6,128]{3,1,2,0:T(8,128)S(1)} %copy.284), channel_id=1, source_target_pairs={{2,0},{4,2},{6,4},{8,6},{10,8},{12,10},{14,12},{16,14},{18,16},{20... | collective-permute-start | bytes 1806344 | tf_op jit(solution)/shard_map/ppermute | solution.py:27
  304.3 33.2 %collective-permute-start.34 = (f32[7,28,28,6]{2,1,3,0:T(8,128)S(1)}, f32[7,28,28,6]{2,1,3,0:T(8,128)S(1)}, u32[]{:S(2)}, u32[]{:S(2)}) collective-permute-start(f32[7,28,28,6]{2,1,3,0:T(8,128)S(1)} %get-tuple-element.114), channel_id=1, source_target_pairs={{0,1},{2,3},{4,5},{6,7},{8,9},{10,11},{12,13},{14,15},{16,17},{18,... | collective-permute-start | bytes 395144 | tf_op jit(solution)/shard_map/ppermute | solution.py:24
  305.6 34.7 %collective-permute-start.35 = (f32[7,28,28,6]{2,1,3,0:T(8,128)S(1)}, f32[7,28,28,6]{2,1,3,0:T(8,128)S(1)}, u32[]{:S(2)}, u32[]{:S(2)}) collective-permute-start(f32[7,28,28,6]{2,1,3,0:T(8,128)S(1)} %get-tuple-element.113), channel_id=1, source_target_pairs={{1,0},{3,2},{5,4},{7,6},{9,8},{11,10},{13,12},{15,14},{17,16},{19,... | collective-permute-start | bytes 395144 | tf_op jit(solution)/shard_map/ppermute | solution.py:27
  359.3 6.5 copy-start.25
  359.3 7.4 copy-start.24
  359.3 8.3 copy-start.23
  468.6 8.7 copy-start.22
  487.8 7.5 copy-start.21
  505.8 5.6 copy-start.17
  505.8 5.6 copy-start.18
  505.8 5.6 copy-start.19
  505.8 5.6 copy-start.20
  522.1 7.7 copy-start.28
  522.1 7.7 copy-start.29
  522.1 7.7 copy-start.30
  534.6 6.7 copy-start.27
  898.3 24.3 %copy-start.31 = (f32[128,24]{1,0:T(8,128)S(1)}, f32[128,24]{1,0:T(8,128)}, u32[]{:S(2)}) copy-start(f32[128,24]{1,0:T(8,128)} %pad_convert_fusion) | copy-start | bytes 36868
  922.7 100.9 %copy-start.32 = (f32[20,20]{1,0:T(8,128)S(1)}, f32[20,20]{1,0:T(8,128)}, u32[]{:S(2)}) copy-start(f32[20,20]{1,0:T(8,128)} %broadcast_multiply_fusion.6) | copy-start | bytes 4804
  922.7 100.9 %copy-start.34 = (f32[20]{0:T(128)S(1)}, f32[20]{0:T(128)}, u32[]{:S(2)}) copy-start(f32[20]{0:T(128)} %copy-done.33) | copy-start | bytes 244
  1023.0 41.5 %copy-start.12 = (f32[16,16,128]{2,1,0:T(8,128)S(1)}, f32[16,16,128]{2,1,0:T(8,128)}, u32[]{:S(2)}) copy-start(f32[16,16,128]{2,1,0:T(8,128)} %param.6) | copy-start | bytes 393220
  1031.0 9.1 collective-permute-start.36
  1035.6 8.7 collective-permute-start.37
  1044.4 8.2 collective-permute-start.38
  1050.2 8.3 collective-permute-start.39
  1058.7 4.9 collective-permute-start.40
  1060.0 4.5 collective-permute-start.41
  (16 other events, 57.1 us)
where the time goes:
time: 1080 us; the launch traced here: 1070 us
  other arithmetic  543 us (50%)
  local copies, waits for them, and re-layouts  296 us (27%)
  starting transfers between devices  130 us (12%)
  matrix products  45.2 us (4%)
  waiting for transfers between devices  28.4 us (3%)
  between operations  23.2 us (2%)
    another operation x31, other arithmetic, zone_update(): factor = jnp.linalg.cholesky(hessian)  171 us
    unnamed x5, other arithmetic  137 us
    another operation x7, other arithmetic, zone_update(): lax.linalg.triangular_solve(factor, middle_sol, left_side=True, lower=Tru...  82.8 us
    ppermute x21, starting transfers between devices, extended(): lax.ppermute(lax.slice_in_dim(block, block.shape[dim] - width, None, axis...  73.8 us
    ppermute x21, starting transfers between devices, extended(): lax.ppermute(lax.slice_in_dim(block, 0, width, axis=dim), axis, backward)  56.1 us
    concatenate x11, local copies, waits for them, and re-layouts, extended(): block = jnp.concatenate([low, block, high], axis=dim)  54.9 us
    concatenate x10, other arithmetic, extended(): block = jnp.concatenate([low, block, high], axis=dim)  47.4 us
    reduce_sum x6, other arithmetic, zone_update(): lax.index_in_dim(blocks, 1 - inner_pos, 2 + 2 * which_axis, keepdims=True)  44.8 us
  transfers between devices with their start and end apart: 42, of which 11 were waited for; matrix products, arithmetic and copies ran while one was open for 9% of the time, Pallas kernels for 0%

commit v1 on v0

v1 whole, which is shorter than its diff:
```python
import functools
import math

import jax
import jax.numpy as jnp
from jax import lax
from jax.experimental import pallas as pl
from jax.experimental.pallas import tpu as pltpu
from jax.sharding import PartitionSpec as P

PC = 10
SPAN = 2 * PC
FSWEEPS = 4
MASS_TERM = 0.5
DAMPING = 0.1
EPSILON = 1e-06
BX, BY, BZ = 16, 16, 128
DEEP = 10
WIN = 30
WY = 32
AX = 24
ROWS = 104
TILES = ROWS // 8
PLANES = 3 * DEEP + 3 * (DEEP - 1) + DEEP
AXES = ("gx", "gy", "gz")
F32 = jnp.float32
BF16 = jnp.bfloat16
HIGH = lax.Precision.HIGHEST
VMEM_LIMIT = 48 * 1024 * 1024


def iota(shape, dim):
    return lax.broadcasted_iota(jnp.int32, shape, dim)


def lane_roll(values, shift):
    if isinstance(shift, int):
        shift = shift % values.shape[-1]
        return values if shift == 0 else pltpu.roll(values, shift, values.ndim - 1)
    size = values.shape[-1]
    return pltpu.roll(values, lax.rem(shift + 8 * size, size), values.ndim - 1)


def row_roll(values, shift):
    if isinstance(shift, int):
        shift = shift % values.shape[-2]
        return values if shift == 0 else pltpu.roll(values, shift, values.ndim - 2)
    size = values.shape[-2]
    return pltpu.roll(values, lax.rem(shift + 8 * size, size), values.ndim - 2)


def three_parts(values):
    first = values.astype(BF16)
    rest = values - first.astype(F32)
    second = rest.astype(BF16)
    third = (rest - second.astype(F32)).astype(BF16)
    return first, second, third


def dot(a, b):
    return lax.dot_general(a, b, (((1,), (0,)), ((), ())), precision=HIGH, preferred_element_type=F32)


def dot_exact(values, selector):
    parts = [
        lax.dot_general(part, selector, (((1,), (0,)), ((), ())), preferred_element_type=F32)
        for part in three_parts(values)
    ]
    return parts[0] + parts[1] + parts[2]


def div10(value):
    return lax.shift_right_arithmetic(value * 205, 11)


def edge_kernel(sc, u, f, m, msg1, msg2, strip, strip1, strip2):
    gz = sc[0]
    low_first = gz == 0
    s1 = jnp.where(low_first, BX - DEEP, 0)
    s2 = BX - DEEP - s1
    f1 = jnp.where(low_first, BX - DEEP + 1, 0)
    f2 = BX - DEEP + 1 - f1
    for out, s, fs in ((msg1, s1, f1), (msg2, s2, f2)):
        for k in range(3):
            out[k * DEEP : (k + 1) * DEEP] = u[k, pl.ds(s, DEEP)]
            base = 3 * DEEP + k * (DEEP - 1)
            out[base : base + DEEP - 1] = f[k, pl.ds(fs, DEEP - 1)]
        out[PLANES - DEEP : PLANES] = m[pl.ds(s, DEEP)]
    lane = iota((BY, 128), 1)
    extra = jnp.where(low_first, DEEP, 0)

    def one(x, carry):
        total = jnp.zeros((BY, 128), F32)
        for c in range(7):
            source = u[c, x] if c < 3 else (f[c - 3, x] if c < 6 else m[x])
            moved = lane_roll(source, extra + DEEP * c)
            total = jnp.where((lane >= DEEP * c) & (lane < DEEP * (c + 1)), moved, total)
        strip[x] = total
        return carry

    lax.fori_loop(0, BX, one, 0)
    strip1[...] = strip[pl.ds(s1, DEEP)]
    strip2[...] = strip[pl.ds(s2, DEEP)]


def pack_kernel(sc, u, f, m, x1, x2, strip, strip1, strip2, own_u, own_f, msg1, msg2, side1, side2, eu, ef, em, es):
    gz = sc[0]
    low_first = gz == 0
    p1 = jnp.where(low_first, 0, BX + DEEP)
    p2 = BX + DEEP - p1
    q1 = jnp.where(low_first, 1, BX + DEEP)
    q2 = BX + DEEP + 1 - q1
    for k in range(3):
        eu[k, DEEP : DEEP + BX] = u[k]
        ef[k, DEEP : DEEP + BX] = f[k]
        ef[k, 0] = jnp.zeros((BY, 128), F32)
        ef[k, 2 * DEEP + BX - 1] = jnp.zeros((BY, 128), F32)
        for msg, p, q in ((x1, p1, q1), (x2, p2, q2)):
            eu[k, pl.ds(p, DEEP)] = msg[k * DEEP : (k + 1) * DEEP]
            base = 3 * DEEP + k * (DEEP - 1)
            ef[k, pl.ds(q, DEEP - 1)] = msg[base : base + DEEP - 1]
    em[DEEP : DEEP + BX] = m[...]
    es[DEEP : DEEP + BX] = strip[...]
    em[pl.ds(p1, DEEP)] = x1[PLANES - DEEP : PLANES]
    em[pl.ds(p2, DEEP)] = x2[PLANES - DEEP : PLANES]
    es[pl.ds(p2, DEEP)] = strip1[...]
    es[pl.ds(p1, DEEP)] = strip2[...]

    lane = iota((BY, 128), 1)
    group = lax.shift_right_arithmetic(lane, 5)
    inner = lane & 31
    zoff = jnp.where(low_first, BZ, -DEEP)

    def window(relz):
        w0 = relz - (DEEP - 5)
        z = inner + w0
        main_ok = (z >= 0) & (z < BZ)
        strip_ok = (z >= zoff) & (z < zoff + DEEP)

        def take(x):
            side = es[x]
            values = []
            for sources in ((eu, 0), (ef, 3)):
                ref, first = sources
                main = jnp.zeros((BY, 128), F32)
                far = jnp.zeros((BY, 128), F32)
                for k in range(4 if first == 0 else 3):
                    source, c = (ref[k, x], first + k) if k < 3 else (em[x], 6)
                    main = jnp.where(group == k, lane_roll(source, 32 * k - w0), main)
                    far = jnp.where(group == k, lane_roll(side, 32 * k + zoff - w0 - DEEP * c), far)
                values.append(jnp.where(main_ok, main, jnp.where(strip_ok, far, 0.0)))
            return values

        return take

    take_own = window(sc[3])
    x0 = sc[1] + 5

    def own(i, carry):
        field, force = take_own(x0 + i)
        own_u[i] = field
        own_f[i] = force
        return carry

    lax.fori_loop(0, WIN, own, 0)

    sub = iota((8, 128), 0)
    for msg, side, base, upward in ((msg1, side1, 4, low_first), (msg2, side2, 7, gz != 0)):
        take = window(sc[base + 2])
        start = sc[base] + 5

        def pair(i, carry, msg=msg, take=take, start=start, upward=upward):
            mixed = jnp.zeros((8, 128), F32)
            number = 0
            for step in range(2):
                for values in take(start + 2 * i + step):
                    top, bottom = values[0:8], values[8:16]
                    msg[i, 8 * number : 8 * number + 8] = jnp.where(upward, bottom, top)
                    edge = jnp.where(upward, row_roll(top, 2), bottom)
                    mixed = jnp.where((sub >= 2 * number) & (sub < 2 * number + 2), row_roll(edge, 2 * number), mixed)
                    number += 1
            msg[i, 32:40] = mixed
            return carry

        lax.fori_loop(0, WIN // 2, pair, 0)

        def plane(i, carry, side=side, upward=upward):
            x = i + DEEP - FSWEEPS

            def edge(values):
                return jnp.where(upward, row_roll(values[8:16], 4), values[0:8])

            every = [edge(eu[k, x]) for k in range(3)] + [edge(ef[k, x]) for k in range(3)] + [edge(em[x]), edge(es[x])]
            for j in range(4):
                side[i, 8 * j : 8 * j + 8] = jnp.where(sub < 4, every[2 * j], row_roll(every[2 * j + 1], 4))
            return carry

        lax.fori_loop(0, AX, plane, 0)


def invert(chains):
    sub = iota((8, 128), 0)
    lane = iota((8, 128), 1)

    def row_of(values, j):
        return jnp.broadcast_to(values[j : j + 1, :], (8, 128))

    def column_of(values, j):
        return jnp.broadcast_to(values[:, j : j + 1], (8, 128))

    for b in range(TILES):
        in_block = (lane >= 8 * b) & (lane < 8 * b + 8)
        for chain in chains:
            columns = [[column_of(tile, 8 * b + j) for j in range(8)] for tile in chain]
            pivot = chain[b]
            own = columns[b]
            for j in range(8):
                at = lane == 8 * b + j
                scale = 1.0 / row_of(own[j], j)
                line = jnp.where(at, 1.0, row_of(pivot, j)) * scale
                pivot = jnp.where(sub == j, line, jnp.where(at, 0.0, pivot) - own[j] * line)
                for n in range(j + 1, 8):
                    other = row_of(own[n], j) * scale
                    own[n] = jnp.where(sub == j, other, own[n] - own[j] * other)
            lines = [row_of(pivot, j) for j in range(8)]
            for i in range(TILES):
                if i != b:
                    tile = jnp.where(in_block, 0.0, chain[i])
                    for j in range(8):
                        tile = tile - columns[i][j] * lines[j]
                    chain[i] = tile
            chain[b] = pivot
    return chains


OFFSETS = (0, PC, -PC, 1, -1)
BANDS = (0, 1, 2, 9, 10, 11, 20)


def zone_kernel(
    sizes, sc, own_u, own_f, r1, r2, out,
    ua, ub, fo, m3, cx, cy, cz, iv, rows, band, up, down, far, grad, hess, bl, br, yt, zs, dl, gs,
):
    nx, ny, nz = sizes
    low_first = sc[0] == 0
    rely = sc[2]
    lane32 = iota((WY, 128), 1)
    group = lax.shift_right_arithmetic(lane32, 5)
    inner = lane32 & 31
    row32 = iota((WY, 128), 0)
    shift = -(rely + 11)

    def unpack(i, carry):
        for step in range(2):
            for which in range(2):
                number = 2 * step + which
                first = r1[i, 8 * number : 8 * number + 8]
                second = r2[i, 8 * number : 8 * number + 8]
                mix1 = r1[i, 32:40]
                mix2 = r2[i, 32:40]
                low, high = jnp.where(low_first, first, second), jnp.where(low_first, second, first)
                low_mix, high_mix = jnp.where(low_first, mix1, mix2), jnp.where(low_first, mix2, mix1)
                middle = own_u[2 * i + step] if which == 0 else own_f[2 * i + step]
                tall = jnp.concatenate(
                    [row_roll(low_mix, 6 - 2 * number), low, middle, high, row_roll(high_mix, -2 * number)], axis=0
                )
                tall = row_roll(tall, shift)[0:WY]
                if which == 0:
                    ua[2 * i + step] = tall
                    moved = jnp.where(group == 0, lane_roll(tall, 32), 0.0)
                    moved = jnp.where(group == 1, lane_roll(tall, 64), moved)
                    m3[2 * i + step] = jnp.where(group == 2, lane_roll(tall, 96), moved)
                else:
                    fo[2 * i + step] = tall
        return carry

    lax.fori_loop(0, WIN // 2, unpack, 0)

    inside_y = sc[11] - 5 + row32
    inside_z = sc[12] - 5 + inner
    inside = (inside_y >= 0) & (inside_y < ny) & (inside_z >= 0) & (inside_z < nz)

    def faces(i, carry):
        here = m3[i]
        cx[i] = 0.5 * (here + m3[jnp.minimum(i + 1, WIN - 1)])
        cy[i] = 0.5 * (here + row_roll(here, -1))
        cz[i] = 0.5 * (here + lane_roll(here, -1))
        return carry

    lax.fori_loop(0, WIN, faces, 0)

    def scale(i, carry):
        total = MASS_TERM + cx[i] + cx[i - 1] + cy[i] + row_roll(cy[i], 1) + cz[i] + lane_roll(cz[i], 1)
        gx = sc[10] - 5 + i
        good = inside & (gx >= 0) & (gx < nx)
        iv[i] = jnp.where(good, 1.0 / total, 0.0)
        return carry

    lax.fori_loop(1, WIN - 1, scale, 0)

    for sweep in range(FSWEEPS):
        src, dst = (ua, ub) if sweep % 2 == 0 else (ub, ua)

        def relax(i, carry, src=src, dst=dst):
            here = src[i]
            total = fo[i] + cx[i] * src[i + 1] + cx[i - 1] * src[i - 1]
            total = total + cy[i] * row_roll(here, -1) + row_roll(cy[i] * here, 1)
            total = total + cz[i] * lane_roll(here, -1) + lane_roll(cz[i] * here, 1)
            dst[i] = total * iv[i]
            return carry

        lax.fori_loop(sweep + 1, WIN - 1 - sweep, relax, 0)

    line = iota((128, 384), 0)
    column = iota((128, 384), 1)
    part = lax.shift_right_arithmetic(column, 7)
    spot = column & 127
    spot_y = div10(spot)
    spot_z = spot - PC * spot_y
    inner_z = (line & 31) - 5
    hit = (lax.shift_right_arithmetic(line, 5) == part) & (inner_z >= 0) & (inner_z < SPAN) & (spot < PC * PC)
    hit = hit & (lax.shift_right_arithmetic(inner_z, 1) == spot_z)
    selector = jnp.where(hit, 1.0, 0.0).astype(BF16)
    zone_y = row32 - 5
    lane_y = div10(lane32)
    pick_y = (zone_y >= 0) & (zone_y < SPAN) & (lax.shift_right_arithmetic(zone_y, 1) == lane_y) & (lane32 < PC * PC)
    pick_y = jnp.where(pick_y, 1.0, 0.0)
    even_y = (zone_y & 1) == 0
    even_z = ((inner - 5) & 1) == 0
    rows[...] = jnp.zeros(rows.shape, F32)

    def layer(a, carry):
        sums = None
        for odd in range(2):
            i = 5 + 2 * a + odd
            here, m_here = ua[i], m3[i]
            ch_x, ch_b = here - ua[i + 1], ua[i - 1] - here
            ch_y = here - row_roll(here, -1)
            ch_z = here - lane_roll(here, -1)
            flow_y, flow_z = cy[i] * ch_y, cz[i] * ch_z
            applied = MASS_TERM * here + cx[i] * ch_x - cx[i - 1] * ch_b
            applied = applied + flow_y - row_roll(flow_y, 1) + flow_z - lane_roll(flow_z, 1)
            resid = fo[i] - applied
            back_y, back_z = row_roll(ch_y, 1), lane_roll(ch_z, 1)
            laplace = ch_x - ch_b + ch_y - back_y + ch_z - back_z
            xp = -0.5 * m3[i + 1] * ch_x
            xm = 0.5 * m3[i - 1] * ch_b
            yp = -0.5 * row_roll(m_here, -1) * ch_y
            ym = 0.5 * row_roll(m_here, 1) * back_y
            zp = -0.5 * lane_roll(m_here, -1) * ch_z
            zm = 0.5 * lane_roll(m_here, 1) * back_z
            diag = -0.5 * m_here * laplace + jnp.where(even_y, yp, ym) + jnp.where(even_z, zp, zm)
            diag = diag + (xm if odd else xp)
            now = [
                diag, xp if odd else None, None if odd else xm,
                jnp.where(even_y, 0.0, yp), jnp.where(even_y, ym, 0.0),
                jnp.where(even_z, 0.0, zp), jnp.where(even_z, zm, 0.0), resid,
            ]
            if sums is None:
                sums = now
            else:
                sums = [p if q is None else (q if p is None else p + q) for p, q in zip(sums, now)]
        tall = dot_exact(jnp.concatenate(sums, axis=0), selector)
        for n in range(8):
            for k in range(3):
                piece = tall[n * WY : (n + 1) * WY, 128 * k : 128 * k + 128] * pick_y
                rows[n, k, pl.ds(a, 1), :] = jnp.sum(piece, axis=0, keepdims=True)
        return carry

    lax.fori_loop(0, PC, layer, 0)

    lane16 = iota((16, 128), 1)
    row16 = iota((16, 128), 0)
    at_y = div10(lane16)
    at_z = lane16 - PC * at_y

    def masked(n, keep):
        return [jnp.where(keep, rows[n, k], 0.0) for k in range(3)]

    full = row16 < PC
    v = {
        0: masked(0, full),
        PC: masked(3, full & (at_y < PC - 1)),
        -PC: masked(4, full & (at_y > 0)),
        1: masked(5, full & (at_z < PC - 1)),
        -1: masked(6, full & (at_z > 0)),
    }
    vxp = masked(1, row16 < PC - 1)
    vxm = masked(2, full & (row16 > 0))
    res = masked(7, full)

    def mix(p, q):
        return p[0] * q[0] + p[1] * q[1] + p[2] * q[2]

    bands = {}
    for o1 in OFFSETS:
        for o2 in OFFSETS:
            key = o1 - o2
            if key >= 0:
                term = lane_roll(mix(v[o1], v[o2]), o2)
                bands[key] = bands[key] + term if key in bands else term
    bands[0] = bands[0] + row_roll(mix(vxp, vxp), 1) + row_roll(mix(vxm, vxm), -1)
    trace = jnp.sum(jnp.sum(bands[0], axis=1, keepdims=True), axis=0, keepdims=True)
    ridge = DAMPING * trace / PC**3 + EPSILON
    bands[0] = jnp.where(lane16 < PC * PC, bands[0] + ridge, jnp.where(lane16 < ROWS, 1.0, 0.0))
    slots = {}
    for n, key in enumerate(BANDS):
        band[n] = bands[key]
        slots[key] = n
    for n, key in enumerate(BANDS[1:]):
        band[len(BANDS) + n] = lane_roll(bands[key], key)
        slots[-key] = len(BANDS) + n
    for n, key in enumerate(OFFSETS):
        above = row_roll(mix(vxm, v[-key]), -1)
        below = row_roll(mix(vxp, v[-key]), 1)
        up[n] = mix(vxp, v[key]) + lane_roll(above, -key)
        down[n] = mix(vxm, v[key]) + lane_roll(below, -key)
    cross = mix(vxm, vxp)
    far[0] = row_roll(cross, -1)
    far[1] = row_roll(cross, 1)
    gradient = row_roll(mix(vxp, res), 1) + row_roll(mix(vxm, res), -1)
    for key in OFFSETS:
        gradient = gradient + lane_roll(mix(v[key], res), key)
    grad[...] = gradient

    sub = iota((8, 128), 0)
    lane8 = iota((8, 128), 1)

    def spread(ref, n, x):
        return jnp.broadcast_to(ref[n, pl.ds(x, 1), :], (8, 128))

    def fill(dst, lines, lead):
        for r in range(TILES):
            apart = sub + 8 * r - lane8
            tile = jnp.zeros((8, 128), F32)
            for key, values in lines:
                if 8 * r + 7 - key >= 0 and 8 * r - key < 128:
                    tile = jnp.where(apart == key, values, tile)
            dst[lead + (slice(8 * r, 8 * r + 8), slice(None))] = tile
        dst[lead + (slice(ROWS, 128), slice(None))] = jnp.zeros((128 - ROWS, 128), F32)

    def dense(x, carry):
        fill(hess, [(key, spread(band, n, x)) for key, n in slots.items()], (x,))
        gs[x] = jnp.broadcast_to(grad[pl.ds(x, 1), :], (8, 128))
        return carry

    lax.fori_loop(0, PC, dense, 0)

    def couple(t, carry):
        right = PC - 1 - t
        fill(bl, [(key, spread(up, n, t)) for n, key in enumerate(OFFSETS)], (t, 0))
        fill(bl, [(key, spread(down, n, t + 1)) for n, key in enumerate(OFFSETS)], (t, 1))

        @pl.when(t < 4)
        def _():
            fill(br, [(key, spread(down, n, right)) for n, key in enumerate(OFFSETS)], (t, 0))
            fill(br, [(key, spread(up, n, right - 1)) for n, key in enumerate(OFFSETS)], (t, 1))

        return carry

    lax.fori_loop(0, 5, couple, 0)
    br[4] = jnp.zeros((2, 128, 128), F32)

    apart = [sub + 8 * r - lane8 for r in range(16)]

    def diagonal(n, x):
        values = spread(far, n, x)
        return jnp.concatenate([jnp.where(a == 0, values, 0.0) for a in apart], axis=0)

    def tiles_of(x):
        return [hess[x, 8 * r : 8 * r + 8, :] for r in range(TILES)]

    def whole(chain):
        return jnp.concatenate(chain + [jnp.zeros((128 - ROWS, 128), F32)], axis=0)

    def eliminate(t, carry):
        right = PC - 1 - t
        left_tiles, right_tiles = invert([tiles_of(t), tiles_of(right)])
        for s, tiles, x, step, ref in ((0, left_tiles, t, 1, bl), (1, right_tiles, right, -1, br)):
            q = whole(tiles)
            two = diagonal(s, x)
            w = jnp.concatenate([ref[t, 0], two], axis=1)
            wt = jnp.concatenate([ref[t, 1], two], axis=0)
            y = dot(q, w)
            yt[s, t] = dot(wt, q)
            schur = dot(wt, y)
            g = gs[x]
            zs[s, t] = dot(g, q)
            gy = dot(g, y)
            one, two_on = x + step, x + 2 * step
            hess[one] = hess[one] - schur[0:128, 0:128]
            hess[two_on] = hess[two_on] - schur[128:256, 128:256]
            ref[t + 1, 0] = ref[t + 1, 0] - schur[0:128, 128:256]
            ref[t + 1, 1] = ref[t + 1, 1] - schur[128:256, 0:128]
            gs[one] = gs[one] - gy[:, 0:128]
            gs[two_on] = gs[two_on] - gy[:, 128:256]
        return carry

    lax.fori_loop(0, 4, eliminate, 0)

    def middle(t, carry):
        x = 4 + t
        (tiles,) = invert([tiles_of(x)])
        q = whole(tiles)
        g = gs[x]
        dl[x] = dot(g, q)

        @pl.when(t == 0)
        def _():
            w = bl[4, 0] + br[4, 1]
            wt = bl[4, 1] + br[4, 0]
            y = dot(q, w)
            yt[0, 4, 0:128] = dot(wt, q)
            hess[5] = hess[5] - dot(wt, y)
            gs[5] = gs[5] - dot(g, y)

        return carry

    lax.fori_loop(0, 2, middle, 0)
    dl[4] = dl[4] - dot(dl[5], yt[0, 4, 0:128])
    for t in (3, 2, 1, 0):
        right = PC - 1 - t
        dl[t] = zs[0, t] - dot(jnp.concatenate([dl[t + 1], dl[t + 2]], axis=1), yt[0, t])
        dl[right] = zs[1, t] - dot(jnp.concatenate([dl[right - 1], dl[right - 2]], axis=1), yt[1, t])
    for x in range(PC):
        out[x : x + 1, :] = -dl[x, 0:1, :]
    spare = iota((16 - PC, 128), 1)
    corner = jnp.zeros((16 - PC, 128), F32)
    for n in range(3):
        corner = jnp.where(spare == n, sc[10 + n].astype(F32), corner)
    out[PC:16, :] = corner


def field_kernel(sizes, sc, u, f, m, x1, x2, strip, strip1, strip2, s1, s2, out, ua, ub, fo, mo, cx, cy, cz, iv):
    nx, ny, nz = sizes
    low_first = sc[0] == 0
    sub = iota((8, 128), 0)
    lane = iota((AX, 128), 1)
    lead = DEEP - FSWEEPS
    spot = jnp.where(low_first, 0, BZ - DEEP)
    strip_lanes = (lane >= spot) & (lane < spot + DEEP)

    def build(dest, values16):
        for q in range(8):
            j = q // 2
            a = s1[dest, 8 * j : 8 * j + 8]
            b = s2[dest, 8 * j : 8 * j + 8]
            low, high = jnp.where(low_first, a, b), jnp.where(low_first, b, a)
            if q % 2 == 0:
                high = row_roll(high, 4)
            else:
                low = row_roll(low, 4)
            t0, t1 = row_roll(values16[q][0:8], 4), row_roll(values16[q][8:16], 4)
            tall = jnp.concatenate(
                [jnp.where(sub < 4, low, t0), jnp.where(sub < 4, t0, t1), jnp.where(sub < 4, t1, high)], axis=0
            )
            if q < 7:
                ref = ua.at[q] if q < 3 else (fo.at[q - 3] if q < 6 else mo)
                ref[dest, :, 0:128] = tall
            else:
                for c in range(7):
                    ref = ua.at[c] if c < 3 else (fo.at[c - 3] if c < 6 else mo)
                    ref[dest, :, 128:256] = jnp.where(strip_lanes, lane_roll(tall, spot - DEEP * c), 0.0)

    def inner_plane(i, carry):
        build(i + FSWEEPS, [u[k, i] for k in range(3)] + [f[k, i] for k in range(3)] + [m[i], strip[i]])
        return carry

    lax.fori_loop(0, BX, inner_plane, 0)

    def outer_plane(i, carry):
        for a, b, sa, sb, start, dest in (
            (x1, x2, strip2, strip1, lead, i), (x2, x1, strip1, strip2, 0, i + FSWEEPS + BX),
        ):
            j = i + start
            force = j - (1 if start else 0)

            def pick(index):
                return jnp.where(low_first, a[index], b[index])

            build(
                dest,
                [pick(k * DEEP + j) for k in range(3)]
                + [pick(3 * DEEP + k * (DEEP - 1) + force) for k in range(3)]
                + [pick(PLANES - DEEP + j), jnp.where(low_first, sa[j], sb[j])],
            )
        return carry

    lax.fori_loop(0, FSWEEPS, outer_plane, 0)

    row = iota((AX, 256), 0)
    wide = iota((AX, 256), 1)
    gy = sc[14] - FSWEEPS + row
    second = (wide >= 128 + spot) & (wide < 128 + spot + DEEP)
    inside = (gy >= 0) & (gy < ny) & ((wide < 128) | second)

    def faces(i, carry):
        here = mo[i]
        cx[i] = 0.5 * (here + mo[jnp.minimum(i + 1, AX - 1)])
        cy[i] = 0.5 * (here + row_roll(here, -1))
        cz[i] = 0.5 * (here + lane_roll(here, -1))
        return carry

    lax.fori_loop(0, AX, faces, 0)

    def scale(i, carry):
        total = MASS_TERM + cx[i] + cx[i - 1] + cy[i] + row_roll(cy[i], 1) + cz[i] + lane_roll(cz[i], 1)
        gx = sc[13] - FSWEEPS + i
        good = inside & (gx >= 0) & (gx < nx)
        iv[i] = jnp.where(good, 1.0 / total, 0.0)
        return carry

    lax.fori_loop(1, AX - 1, scale, 0)
    for sweep in range(FSWEEPS):
        src, dst = (ua, ub) if sweep % 2 == 0 else (ub, ua)

        def relax(i, carry, src=src, dst=dst, last=sweep == FSWEEPS - 1):
            for k in range(3):
                here = src[k, i]
                total = fo[k, i] + cx[i] * src[k, i + 1] + cx[i - 1] * src[k, i - 1]
                total = total + cy[i] * row_roll(here, -1) + row_roll(cy[i] * here, 1)
                total = total + cz[i] * lane_roll(here, -1) + lane_roll(cz[i] * here, 1)
                total = total * iv[i]
                if last:
                    out[k, i - FSWEEPS] = row_roll(total[:, 0:128], -FSWEEPS)[0:BY]
                else:
                    dst[k, i] = total
            return carry

        lax.fori_loop(sweep + 1, AX - 1 - sweep, relax, 0)


def taper(offset):
    folded = jnp.minimum(offset, SPAN - 1 - offset)
    total = jnp.zeros(offset.shape, F32)
    for n in range(PC):
        total = jnp.where(folded == float(n), math.sin(math.pi * (n + 0.5) / SPAN), total)
    return total


def final_kernel(sc, m, parts, out, acc):
    number = parts.shape[0]
    row16 = iota((16, 128), 0).astype(F32)
    lane16i = iota((16, 128), 1)
    lane16 = lane16i.astype(F32)
    lane_y = div10(lane16i).astype(F32)
    rows128 = iota((128, 128), 0)
    rows_y = div10(rows128)
    rows_z = (rows128 - PC * rows_y).astype(F32)
    lanes128 = iota((128, 128), 1).astype(F32)
    acc[...] = jnp.zeros(acc.shape, F32)

    def add(n, carry):
        delta = parts[n]

        def place(axis, low):
            return delta[PC : PC + 1, axis : axis + 1] - low.astype(F32)

        cx, cy, cz = place(0, sc[13]), place(1, sc[14]), place(2, sc[15])
        off_x = row16 - cx
        apart = off_x - 2.0 * lane16
        choose = jnp.where((apart >= 0.0) & (apart < 2.0) & (lane16i < PC), 1.0, 0.0).astype(BF16)[:, 0:16]
        picked = [
            lax.dot_general(choose, p, (((1,), (0,)), ((), ())), preferred_element_type=F32) for p in three_parts(delta)
        ]
        lines = (picked[0] + picked[1] + picked[2]) * taper(off_x)
        off_y = row16 - cy
        apart = off_y - 2.0 * lane_y
        cover = jnp.where((apart >= 0.0) & (apart < 2.0) & (lane16i < PC * PC), taper(off_y), 0.0)
        off_z = lanes128 - cz
        apart = off_z - 2.0 * rows_z
        expand = jnp.where((apart >= 0.0) & (apart < 2.0) & (rows128 < PC * PC), 1.0, 0.0).astype(BF16)
        tall = jnp.concatenate([jnp.broadcast_to(lines[x : x + 1, :], (BY, 128)) * cover for x in range(BX)], axis=0)
        acc[...] += dot_exact(tall, expand) * taper(off_z[0:1, :])
        return carry

    lax.fori_loop(0, number, add, 0)
    for x in range(BX):
        out[x] = m[x] * (1.0 + acc[16 * x : 16 * x + 16, :])


def call(kernel, shapes, scratch, inputs, flops):
    specs = [pl.BlockSpec(memory_space=pltpu.SMEM)] + [pl.BlockSpec(memory_space=pltpu.VMEM)] * (len(inputs) - 1)
    single = not isinstance(shapes, list)
    outs = [jax.ShapeDtypeStruct(s, F32) for s in ([shapes] if single else shapes)]
    results = pl.pallas_call(
        kernel,
        out_shape=outs,
        in_specs=specs,
        out_specs=[pl.BlockSpec(memory_space=pltpu.VMEM)] * len(outs),
        scratch_shapes=[pltpu.VMEM(s, F32) for s in scratch],
        compiler_params=pltpu.CompilerParams(vmem_limit_bytes=VMEM_LIMIT),
        cost_estimate=pl.CostEstimate(flops=flops, bytes_accessed=1 << 20, transcendentals=0),
    )(*inputs)
    return results[0] if single else results


def body(forcing, start_field, modulus, corners):
    counts = tuple(lax.axis_size(axis) for axis in AXES)
    sizes = (counts[0] * BX, counts[1] * BY, counts[2] * BZ)
    place = tuple(lax.axis_index(axis) for axis in AXES)
    gz = place[2].astype(jnp.int32)
    lower = jnp.stack([place[0] * BX, place[1] * BY, place[2] * BZ]).astype(jnp.int32)

    def send(values, move):
        pairs = []
        for x in range(counts[0]):
            for y in range(counts[1]):
                for z in range(counts[2]):
                    to = move(x, y, z)
                    if all(0 <= t < c for t, c in zip(to, counts)):
                        pairs.append(((x * counts[1] + y) * counts[2] + z, (to[0] * counts[1] + to[1]) * counts[2] + to[2]))
        return lax.ppermute(values, AXES, pairs)

    def turn(z):
        return 1 if z == 0 else -1

    relative = corners[0] - lower
    near = jnp.broadcast_to(relative[None, :], (1, 3))
    want1 = send(near, lambda x, y, z: (x, y - turn(z), z))
    want2 = send(near, lambda x, y, z: (x, y + turn(z), z))
    scalar = jnp.concatenate([gz[None], relative, want1[0], want2[0], corners[0], lower]).astype(jnp.int32)
    first = gz[None]

    msg1, msg2, strip, strip1, strip2 = call(
        edge_kernel,
        [(PLANES, BY, 128), (PLANES, BY, 128), (BX, BY, 128), (DEEP, BY, 128), (DEEP, BY, 128)],
        [],
        [first, start_field, forcing, modulus],
        1 << 20,
    )
    x1 = send(msg1, lambda x, y, z: (x + turn(z), y, z))
    x2 = send(msg2, lambda x, y, z: (x - turn(z), y, z))
    far_strip = send(strip, lambda x, y, z: (x, y, 1 - z))
    far1 = send(strip1, lambda x, y, z: (x + turn(z), y, 1 - z))
    far2 = send(strip2, lambda x, y, z: (x - turn(z), y, 1 - z))
    own_u, own_f, y1, y2, a1, a2 = call(
        pack_kernel,
        [(WIN, BY, 128)] * 2 + [(WIN // 2, 40, 128)] * 2 + [(AX, 32, 128)] * 2,
        [(3, 36, BY, 128), (3, 36, BY, 128), (36, BY, 128), (36, BY, 128)],
        [scalar, start_field, forcing, modulus, x1, x2, far_strip, far1, far2],
        1 << 22,
    )
    r1 = send(y1, lambda x, y, z: (x, y + turn(z), z))
    r2 = send(y2, lambda x, y, z: (x, y - turn(z), z))
    b1 = send(a1, lambda x, y, z: (x, y + turn(z), z))
    b2 = send(a2, lambda x, y, z: (x, y - turn(z), z))
    window = (WIN, WY, 128)
    delta = call(
        functools.partial(zone_kernel, sizes),
        (16, 128),
        [window] * 8
        + [
            (8, 3, 16, 128), (13, 16, 128), (5, 16, 128), (5, 16, 128), (2, 16, 128), (16, 128),
            (PC, 128, 128), (5, 2, 128, 128), (5, 2, 128, 128), (2, 5, 256, 128), (2, 5, 8, 128), (PC, 8, 128), (PC, 8, 128),
        ],
        [scalar, own_u, own_f, r1, r2],
        1 << 33,
    )
    beside = [delta]
    beside.append(send(delta, lambda x, y, z: (x, y, 1 - z)))
    for step in (1, -1):
        beside.append(send(delta, lambda x, y, z, step=step: (x, y + step * turn(z), z)))
        beside.append(send(delta, lambda x, y, z, step=step: (x, y + step * turn(z), 1 - z)))
    plane = jnp.stack(beside)
    after = send(plane, lambda x, y, z: (x + turn(z), y, z))
    before = send(plane, lambda x, y, z: (x - turn(z), y, z))
    wide = (AX, AX, 256)
    displacement = call(
        functools.partial(field_kernel, sizes),
        (3, BX, BY, BZ),
        [(3,) + wide] * 3 + [wide] * 5,
        [scalar, start_field, forcing, modulus, x1, x2, far_strip, far1, far2, b1, b2],
        1 << 30,
    )
    new_modulus = call(
        final_kernel,
        (BX, BY, BZ),
        [(BX * BY, 128)],
        [scalar, modulus, jnp.concatenate([plane, after, before])],
        1 << 24,
    )
    return displacement, new_modulus


def solution(mesh):
    placed = (
        P(None, "gx", "gy", "gz"),
        P(None, "gx", "gy", "gz"),
        P("gx", "gy", "gz"),
        P(("gx", "gy", "gz"), None),
    )
    return jax.shard_map(
        body,
        mesh=mesh,
        in_specs=placed,
        out_specs=(P(None, "gx", "gy", "gz"), P("gx", "gy", "gz")),
        check_vma=False,
    )
```

time: 1080 us -> 172 us (0.16)
  the two profiles are of different devices: /device:TPU:79 before, /device:TPU:112 now
where the time goes in v1:
time: 172 us; the launch traced here: 171 us
  Pallas kernels  92.5 us (54%)
  starting transfers between devices  58.1 us (34%)
  waiting for transfers between devices  14.6 us (8%)
  local copies, waits for them, and re-layouts  4.89 us (3%)
    pallas_call x5, Pallas kernels, call(): pl.pallas_call(kernel, out_shape=outs, in_specs=specs, out_specs=[pl.Bloc...  92.5 us
    ppermute x18, starting transfers between devices, send(): return lax.ppermute(values, AXES, pairs)  58.1 us
    ppermute x18, waiting for transfers between devices, send(): return lax.ppermute(values, AXES, pairs)  14.6 us
    unnamed x22, local copies, waits for them, and re-layouts  4.14 us
  transfers between devices with their start and end apart: 18, of which 6 were waited for; matrix products, arithmetic and copies ran while one was open for 1% of the time, Pallas kernels for 39%

profile of v1, /device:TPU:112, one launch (start us, length us, event | category | flops | bytes accessed | tf_op | source)
XLA Modules:
  0.0 171.1 jit_solution(13411323797100786294)
XLA Ops:
  0.6 0.0 copy-start
  0.6 1.0 copy-done
  1.6 0.0 copy-start.2
  1.6 1.0 copy-done.2
  2.6 0.0 copy-start.4
  2.6 0.9 copy-done.4
  3.5 0.0 copy-start.1
  3.5 0.0 copy-start.3
  3.5 0.0 copy-start.5
  3.5 2.1 %shard_map.59 = (f32[67,16,128]{2,1,0:T(8,128)S(1)}, f32[67,16,128]{2,1,0:T(8,128)S(1)}, f32[16,16,128]{2,1,0:T(8,128)S(1)}, f32[10,16,128]{2,1,0:T(8,128)}, f32[10,16,128]{2,1,0:T(8,128)}) custom-call(s32[1]{0:T(128)} %bitcast.sc, f32[3,16,16,128]{3,2,1,0:T(8,128)S(1)} %copy-done, f32[3,16,16,128]{3,2,1,0:T(8,128)S(1)} %copy-done.2, ...), custom_call_target="tpu_custom_call" | custom-call | flops 1048576 | bytes 1048576 | tf_op jit(solution)/shard_map/pallas_call | solution.py:686
  5.6 5.0 %collective-permute-start.2 = (f32[67,16,128]{2,1,0:T(8,128)S(1)}, f32[67,16,128]{2,1,0:T(8,128)S(1)}, u32[]{:S(2)}, u32[]{:S(2)}) collective-permute-start(f32[67,16,128]{2,1,0:T(8,128)S(1)} %get-tuple-element.13), channel_id=1, source_target_pairs={{0,32},{2,34},{4,36},{6,38},{8,40},{10,42},{12,44},{14,46},{16,48}... | collective-permute-start | bytes 1646600 | tf_op jit(solution)/shard_map/ppermute | solution.py:713
  10.7 1.9 %collective-permute-start.3 = (f32[67,16,128]{2,1,0:T(8,128)S(1)}, f32[67,16,128]{2,1,0:T(8,128)S(1)}, u32[]{:S(2)}, u32[]{:S(2)}) collective-permute-start(f32[67,16,128]{2,1,0:T(8,128)S(1)} %get-tuple-element.14), channel_id=1, source_target_pairs={{1,33},{3,35},{5,37},{7,39},{9,41},{11,43},{13,45},{15,47},{17,49}... | collective-permute-start | bytes 1646600 | tf_op jit(solution)/shard_map/ppermute | solution.py:713
  12.6 0.0 copy-start.6
  12.6 0.6 copy-done.6
  13.3 0.1 add_subtract_fusion.1
  13.3 3.4 %collective-permute-start.1 = (s32[1,3]{1,0:T(1,128)S(1)}, s32[1,3]{1,0:T(1,128)S(1)}, u32[]{:S(2)}, u32[]{:S(2)}) collective-permute-start(s32[1,3]{1,0:T(1,128)S(1)} %add_subtract_fusion.1), channel_id=1, source_target_pairs={{0,2},{2,4},{3,1},{4,6},{5,3},{6,8},{7,5},{8,10},{9,7},{10,12},{11... | collective-permute-start | bytes 44 | tf_op jit(solution)/shard_map/ppermute | solution.py:713
  16.7 4.6 %collective-permute-start = (s32[1,3]{1,0:T(1,128)S(1)}, s32[1,3]{1,0:T(1,128)S(1)}, u32[]{:S(2)}, u32[]{:S(2)}) collective-permute-start(s32[1,3]{1,0:T(1,128)S(1)} %add_subtract_fusion.1), channel_id=1, source_target_pairs={{1,3},{2,0},{3,5},{4,2},{5,7},{6,4},{7,9},{8,6},{9,11},{10,8},{11,... | collective-permute-start | bytes 44 | tf_op jit(solution)/shard_map/ppermute | solution.py:713
  21.3 1.9 %collective-permute-start.5 = (f32[10,16,128]{2,1,0:T(8,128)}, f32[10,16,128]{2,1,0:T(8,128)S(1)}, u32[]{:S(2)}, u32[]{:S(2)}) collective-permute-start(f32[10,16,128]{2,1,0:T(8,128)} %get-tuple-element.16), channel_id=1, source_target_pairs={{0,33},{2,35},{4,37},{6,39},{8,41},{10,43},{12,45},{14,47},{16,49}... | collective-permute-start | bytes 245768 | tf_op jit(solution)/shard_map/ppermute | solution.py:713
  23.2 0.0 collective-permute-done.1
  23.2 1.9 %collective-permute-start.6 = (f32[10,16,128]{2,1,0:T(8,128)}, f32[10,16,128]{2,1,0:T(8,128)S(1)}, u32[]{:S(2)}, u32[]{:S(2)}) collective-permute-start(f32[10,16,128]{2,1,0:T(8,128)} %get-tuple-element.17), channel_id=1, source_target_pairs={{1,32},{3,34},{5,36},{7,38},{9,40},{11,42},{13,44},{15,46},{17,48}... | collective-permute-start | bytes 245768 | tf_op jit(solution)/shard_map/ppermute | solution.py:713
  25.2 0.0 collective-permute-done
  25.2 0.0 copy-start.7
  25.2 0.6 copy-done.7
  25.8 3.3 %collective-permute-start.4 = (f32[16,16,128]{2,1,0:T(8,128)S(1)}, f32[16,16,128]{2,1,0:T(8,128)S(1)}, u32[]{:S(2)}, u32[]{:S(2)}) collective-permute-start(f32[16,16,128]{2,1,0:T(8,128)S(1)} %get-tuple-element.15), channel_id=1, source_target_pairs={{0,1},{1,0},{2,3},{3,2},{4,5},{5,4},{6,7},{7,6},{8,9},{9,8},{10,11... | collective-permute-start | bytes 393224 | tf_op jit(solution)/shard_map/ppermute | solution.py:713
  29.1 0.1 add_subtract_fusion
  29.2 0.7 concatenate.9.sc
  29.9 0.0 collective-permute-done.5.strip1
  29.9 0.0 collective-permute-done.6.strip2
  29.9 0.2 collective-permute-done.4.strip
  30.1 0.0 collective-permute-done.2.x1
  30.1 0.0 collective-permute-done.3.x2
  30.1 0.0 copy-done.1
  30.1 0.0 copy-done.3
  30.1 0.0 copy-done.5
  30.1 8.1 %shard_map.60 = (f32[30,16,128]{2,1,0:T(8,128)S(1)}, f32[30,16,128]{2,1,0:T(8,128)S(1)}, f32[15,40,128]{2,1,0:T(8,128)S(1)}, f32[15,40,128]{2,1,0:T(8,128)S(1)},...) custom-call(s32[16]{0:T(128)S(1)} %concatenate.9.sc, f32[3,16,16,128]{3,2,1,0:T(8,128)S(1)} %copy-done.1, ...), custom_call_target="tpu_custom_call" | custom-call | flops 4194304 | bytes 1048576 | tf_op jit(solution)/shard_map/pallas_call | solution.py:686
  38.3 1.9 %collective-permute-start.9 = (f32[15,40,128]{2,1,0:T(8,128)S(1)}, f32[15,40,128]{2,1,0:T(8,128)S(1)}, u32[]{:S(2)}, u32[]{:S(2)}) collective-permute-start(f32[15,40,128]{2,1,0:T(8,128)S(1)} %get-tuple-element.22), channel_id=1, source_target_pairs={{0,2},{2,4},{3,1},{4,6},{5,3},{6,8},{7,5},{8,10},{9,7},{10,12},{11... | collective-permute-start | bytes 921608 | tf_op jit(solution)/shard_map/ppermute | solution.py:713
  40.2 6.0 %collective-permute-start.10 = (f32[15,40,128]{2,1,0:T(8,128)S(1)}, f32[15,40,128]{2,1,0:T(8,128)S(1)}, u32[]{:S(2)}, u32[]{:S(2)}) collective-permute-start(f32[15,40,128]{2,1,0:T(8,128)S(1)} %get-tuple-element.23), channel_id=1, source_target_pairs={{1,3},{2,0},{3,5},{4,2},{5,7},{6,4},{7,9},{8,6},{9,11},{10,8},{11,... | collective-permute-start | bytes 921608 | tf_op jit(solution)/shard_map/ppermute | solution.py:713
  46.2 1.9 %collective-permute-start.7 = (f32[24,32,128]{2,1,0:T(8,128)S(1)}, f32[24,32,128]{2,1,0:T(8,128)S(1)}, u32[]{:S(2)}, u32[]{:S(2)}) collective-permute-start(f32[24,32,128]{2,1,0:T(8,128)S(1)} %get-tuple-element.18), channel_id=1, source_target_pairs={{0,2},{2,4},{3,1},{4,6},{5,3},{6,8},{7,5},{8,10},{9,7},{10,12},{11... | collective-permute-start | bytes 1179656 | tf_op jit(solution)/shard_map/ppermute | solution.py:713
  48.1 6.0 %collective-permute-start.8 = (f32[24,32,128]{2,1,0:T(8,128)S(1)}, f32[24,32,128]{2,1,0:T(8,128)S(1)}, u32[]{:S(2)}, u32[]{:S(2)}) collective-permute-start(f32[24,32,128]{2,1,0:T(8,128)S(1)} %get-tuple-element.19), channel_id=1, source_target_pairs={{1,3},{2,0},{3,5},{4,2},{5,7},{6,4},{7,9},{8,6},{9,11},{10,8},{11,... | collective-permute-start | bytes 1179656 | tf_op jit(solution)/shard_map/ppermute | solution.py:713
  54.2 0.0 collective-permute-done.9.r1
  54.2 0.0 collective-permute-done.10.r2
  54.2 58.2 %shard_map.62 = f32[16,128]{1,0:T(8,128)S(1)} custom-call(s32[16]{0:T(128)S(1)} %concatenate.9.sc, f32[30,16,128]{2,1,0:T(8,128)S(1)} %get-tuple-element.20.own_u, f32[30,16,128]{2,1,0:T(8,128)S(1)} %get-tuple-element.21.own_f, f32[15,40,128]{2,1,0:T(8,128)S(1)} %collective-permute-done.9.r1, f32[15,40,128]{2,1,0:T(8,128)S(1)} %collective-permute-done.10.r2), custom_call_target="tpu_custom_call" | custom-call | flops 8589934592 | bytes 1048576 | tf_op jit(solution)/shard_map/pallas_call | solution.py:686
  112.4 2.4 %collective-permute-start.15 = (f32[16,128]{1,0:T(8,128)S(1)}, f32[16,128]{1,0:T(8,128)S(1)}, u32[]{:S(2)}, u32[]{:S(2)}) collective-permute-start(f32[16,128]{1,0:T(8,128)S(1)} %shard_map.62), channel_id=1, source_target_pairs={{1,2},{2,1},{3,4},{4,3},{5,6},{6,5},{7,8},{8,7},{9,10},{10,9},{11,... | collective-permute-start | bytes 24584 | tf_op jit(solution)/shard_map/ppermute | solution.py:713
  114.8 3.2 %collective-permute-start.14 = (f32[16,128]{1,0:T(8,128)S(1)}, f32[16,128]{1,0:T(8,128)S(1)}, u32[]{:S(2)}, u32[]{:S(2)}) collective-permute-start(f32[16,128]{1,0:T(8,128)S(1)} %shard_map.62), channel_id=1, source_target_pairs={{1,3},{2,0},{3,5},{4,2},{5,7},{6,4},{7,9},{8,6},{9,11},{10,8},{11,... | collective-permute-start | bytes 24584 | tf_op jit(solution)/shard_map/ppermute | solution.py:713
  118.0 0.1 collective-permute-start.11
  118.2 1.1 collective-permute-done.11
  119.3 2.6 %collective-permute-start.12 = (f32[16,128]{1,0:T(8,128)S(1)}, f32[16,128]{1,0:T(8,128)S(1)}, u32[]{:S(2)}, u32[]{:S(2)}) collective-permute-start(f32[16,128]{1,0:T(8,128)S(1)} %shard_map.62), channel_id=1, source_target_pairs={{0,2},{2,4},{3,1},{4,6},{5,3},{6,8},{7,5},{8,10},{9,7},{10,12},{11... | collective-permute-start | bytes 24584 | tf_op jit(solution)/shard_map/ppermute | solution.py:713
  121.9 5.0 %collective-permute-done.12 = f32[16,128]{1,0:T(8,128)S(1)} collective-permute-done((f32[16,128]{1,0:T(8,128)S(1)}, f32[16,128]{1,0:T(8,128)S(1)}, u32[]{:S(2)}, u32[]{:S(2)}) %collective-permute-start.12) | collective-permute-done | bytes 8224 | tf_op jit(solution)/shard_map/ppermute | solution.py:713
  127.0 1.9 %collective-permute-start.13 = (f32[16,128]{1,0:T(8,128)S(1)}, f32[16,128]{1,0:T(8,128)S(1)}, u32[]{:S(2)}, u32[]{:S(2)}) collective-permute-start(f32[16,128]{1,0:T(8,128)S(1)} %shard_map.62), channel_id=1, source_target_pairs={{0,3},{2,5},{3,0},{4,7},{5,2},{6,9},{7,4},{8,11},{9,6},{10,13},{11... | collective-permute-start | bytes 24584 | tf_op jit(solution)/shard_map/ppermute | solution.py:713
  128.9 3.0 %collective-permute-done.13 = f32[16,128]{1,0:T(8,128)S(1)} collective-permute-done((f32[16,128]{1,0:T(8,128)S(1)}, f32[16,128]{1,0:T(8,128)S(1)}, u32[]{:S(2)}, u32[]{:S(2)}) %collective-permute-start.13) | collective-permute-done | bytes 8224 | tf_op jit(solution)/shard_map/ppermute | solution.py:713
  131.9 0.0 collective-permute-done.14
  131.9 0.0 collective-permute-done.15
  131.9 7.9 %collective-permute-start.16 = (f32[6,16,128]{2,1,0:T(8,128)S(1)}, f32[6,16,128]{2,1,0:T(8,128)S(1)}, u32[]{:S(2)}, u32[]{:S(2)}) collective-permute-start(f32[6,16,128]{2,1,0:T(8,128)S(1)} %get-tuple-element.24), channel_id=1, source_target_pairs={{0,32},{2,34},{4,36},{6,38},{8,40},{10,42},{12,44},{14,46},{16,48}... | collective-permute-start | bytes 147464 | tf_op jit(solution)/shard_map/ppermute | solution.py:713
  139.9 1.9 %collective-permute-start.17 = (f32[6,16,128]{2,1,0:T(8,128)S(1)}, f32[6,16,128]{2,1,0:T(8,128)S(1)}, u32[]{:S(2)}, u32[]{:S(2)}) collective-permute-start(f32[6,16,128]{2,1,0:T(8,128)S(1)} %get-tuple-element.24), channel_id=1, source_target_pairs={{1,33},{3,35},{5,37},{7,39},{9,41},{11,43},{13,45},{15,47},{17,49}... | collective-permute-start | bytes 147464 | tf_op jit(solution)/shard_map/ppermute | solution.py:713
  141.8 0.2 collective-permute-done.16
  142.0 5.1 %collective-permute-done.17 = f32[6,16,128]{2,1,0:T(8,128)S(1)} collective-permute-done((f32[6,16,128]{2,1,0:T(8,128)S(1)}, f32[6,16,128]{2,1,0:T(8,128)S(1)}, u32[]{:S(2)}, u32[]{:S(2)}) %collective-permute-start.17) | collective-permute-done | bytes 49184 | tf_op jit(solution)/shard_map/ppermute | solution.py:713
  147.1 8.0 %shard_map.63 = f32[16,16,128]{2,1,0:T(8,128)} custom-call(s32[16]{0:T(128)S(1)} %concatenate.9.sc, f32[16,16,128]{2,1,0:T(8,128)S(1)} %copy-done.5, f32[18,16,128]{2,1,0:T(8,128)S(1)} %constant_dynamic-update-slice_fusion.6.parts), custom_call_target="tpu_custom_call" | custom-call | flops 16777216 | bytes 1048576 | tf_op jit(solution)/shard_map/pallas_call | solution.py:686
  155.1 0.0 collective-permute-done.7.s1
  155.1 0.0 collective-permute-done.8.s2
  155.1 16.0 %shard_map.61 = f32[3,16,16,128]{3,2,1,0:T(8,128)} custom-call(s32[16]{0:T(128)S(1)} %concatenate.9.sc, f32[3,16,16,128]{3,2,1,0:T(8,128)S(1)} %copy-done.1, f32[3,16,16,128]{3,2,1,0:T(8,128)S(1)} %copy-done.3, f32[16,16,128]{2,1,0:T(8,128)S(1)} %copy-done.5, f32[67,16,128]{2,1,0:T(8,128)S(1)} %collective-permute-done.2.x1, ...), custom_call_target="tpu_custom_call" | custom-call | flops 1073741824 | bytes 1048576 | tf_op jit(solution)/shard_map/pallas_call | solution.py:686
  (8 shorter events, 0.0 us)
Async XLA Ops:
  0.6 1.0 copy-start
  1.6 1.0 copy-start.2
  2.6 0.9 copy-start.4
  3.5 26.5 %copy-start.1 = (f32[3,16,16,128]{3,2,1,0:T(8,128)S(1)}, f32[3,16,16,128]{3,2,1,0:T(8,128)}, u32[]{:S(2)}) copy-start(f32[3,16,16,128]{3,2,1,0:T(8,128)} %u.5) | copy-start | bytes 1179652
  3.5 26.5 %copy-start.3 = (f32[3,16,16,128]{3,2,1,0:T(8,128)S(1)}, f32[3,16,16,128]{3,2,1,0:T(8,128)}, u32[]{:S(2)}) copy-start(f32[3,16,16,128]{3,2,1,0:T(8,128)} %f.5) | copy-start | bytes 1179652
  3.5 26.6 %copy-start.5 = (f32[16,16,128]{2,1,0:T(8,128)S(1)}, f32[16,16,128]{2,1,0:T(8,128)}, u32[]{:S(2)}) copy-start(f32[16,16,128]{2,1,0:T(8,128)} %m.7) | copy-start | bytes 393220
  5.6 24.4 %collective-permute-start.2 = (f32[67,16,128]{2,1,0:T(8,128)S(1)}, f32[67,16,128]{2,1,0:T(8,128)S(1)}, u32[]{:S(2)}, u32[]{:S(2)}) collective-permute-start(f32[67,16,128]{2,1,0:T(8,128)S(1)} %get-tuple-element.13), channel_id=1, source_target_pairs={{0,32},{2,34},{4,36},{6,38},{8,40},{10,42},{12,44},{14,46},{16,48}... | collective-permute-start | bytes 1646600 | tf_op jit(solution)/shard_map/ppermute | solution.py:713
  10.7 19.4 %collective-permute-start.3 = (f32[67,16,128]{2,1,0:T(8,128)S(1)}, f32[67,16,128]{2,1,0:T(8,128)S(1)}, u32[]{:S(2)}, u32[]{:S(2)}) collective-permute-start(f32[67,16,128]{2,1,0:T(8,128)S(1)} %get-tuple-element.14), channel_id=1, source_target_pairs={{1,33},{3,35},{5,37},{7,39},{9,41},{11,43},{13,45},{15,47},{17,49}... | collective-permute-start | bytes 1646600 | tf_op jit(solution)/shard_map/ppermute | solution.py:713
  12.6 0.7 copy-start.6
  13.3 9.9 %collective-permute-start.1 = (s32[1,3]{1,0:T(1,128)S(1)}, s32[1,3]{1,0:T(1,128)S(1)}, u32[]{:S(2)}, u32[]{:S(2)}) collective-permute-start(s32[1,3]{1,0:T(1,128)S(1)} %add_subtract_fusion.1), channel_id=1, source_target_pairs={{0,2},{2,4},{3,1},{4,6},{5,3},{6,8},{7,5},{8,10},{9,7},{10,12},{11... | collective-permute-start | bytes 44 | tf_op jit(solution)/shard_map/ppermute | solution.py:713
  16.7 8.4 %collective-permute-start = (s32[1,3]{1,0:T(1,128)S(1)}, s32[1,3]{1,0:T(1,128)S(1)}, u32[]{:S(2)}, u32[]{:S(2)}) collective-permute-start(s32[1,3]{1,0:T(1,128)S(1)} %add_subtract_fusion.1), channel_id=1, source_target_pairs={{1,3},{2,0},{3,5},{4,2},{5,7},{6,4},{7,9},{8,6},{9,11},{10,8},{11,... | collective-permute-start | bytes 44 | tf_op jit(solution)/shard_map/ppermute | solution.py:713
  21.3 8.6 %collective-permute-start.5 = (f32[10,16,128]{2,1,0:T(8,128)}, f32[10,16,128]{2,1,0:T(8,128)S(1)}, u32[]{:S(2)}, u32[]{:S(2)}) collective-permute-start(f32[10,16,128]{2,1,0:T(8,128)} %get-tuple-element.16), channel_id=1, source_target_pairs={{0,33},{2,35},{4,37},{6,39},{8,41},{10,43},{12,45},{14,47},{16,49}... | collective-permute-start | bytes 245768 | tf_op jit(solution)/shard_map/ppermute | solution.py:713
  23.2 6.7 %collective-permute-start.6 = (f32[10,16,128]{2,1,0:T(8,128)}, f32[10,16,128]{2,1,0:T(8,128)S(1)}, u32[]{:S(2)}, u32[]{:S(2)}) collective-permute-start(f32[10,16,128]{2,1,0:T(8,128)} %get-tuple-element.17), channel_id=1, source_target_pairs={{1,32},{3,34},{5,36},{7,38},{9,40},{11,42},{13,44},{15,46},{17,48}... | collective-permute-start | bytes 245768 | tf_op jit(solution)/shard_map/ppermute | solution.py:713
  25.2 0.6 copy-start.7
  25.8 4.3 %collective-permute-start.4 = (f32[16,16,128]{2,1,0:T(8,128)S(1)}, f32[16,16,128]{2,1,0:T(8,128)S(1)}, u32[]{:S(2)}, u32[]{:S(2)}) collective-permute-start(f32[16,16,128]{2,1,0:T(8,128)S(1)} %get-tuple-element.15), channel_id=1, source_target_pairs={{0,1},{1,0},{2,3},{3,2},{4,5},{5,4},{6,7},{7,6},{8,9},{9,8},{10,11... | collective-permute-start | bytes 393224 | tf_op jit(solution)/shard_map/ppermute | solution.py:713
  38.3 15.9 %collective-permute-start.9 = (f32[15,40,128]{2,1,0:T(8,128)S(1)}, f32[15,40,128]{2,1,0:T(8,128)S(1)}, u32[]{:S(2)}, u32[]{:S(2)}) collective-permute-start(f32[15,40,128]{2,1,0:T(8,128)S(1)} %get-tuple-element.22), channel_id=1, source_target_pairs={{0,2},{2,4},{3,1},{4,6},{5,3},{6,8},{7,5},{8,10},{9,7},{10,12},{11... | collective-permute-start | bytes 921608 | tf_op jit(solution)/shard_map/ppermute | solution.py:713
  40.2 14.0 %collective-permute-start.10 = (f32[15,40,128]{2,1,0:T(8,128)S(1)}, f32[15,40,128]{2,1,0:T(8,128)S(1)}, u32[]{:S(2)}, u32[]{:S(2)}) collective-permute-start(f32[15,40,128]{2,1,0:T(8,128)S(1)} %get-tuple-element.23), channel_id=1, source_target_pairs={{1,3},{2,0},{3,5},{4,2},{5,7},{6,4},{7,9},{8,6},{9,11},{10,8},{11,... | collective-permute-start | bytes 921608 | tf_op jit(solution)/shard_map/ppermute | solution.py:713
  46.2 108.9 %collective-permute-start.7 = (f32[24,32,128]{2,1,0:T(8,128)S(1)}, f32[24,32,128]{2,1,0:T(8,128)S(1)}, u32[]{:S(2)}, u32[]{:S(2)}) collective-permute-start(f32[24,32,128]{2,1,0:T(8,128)S(1)} %get-tuple-element.18), channel_id=1, source_target_pairs={{0,2},{2,4},{3,1},{4,6},{5,3},{6,8},{7,5},{8,10},{9,7},{10,12},{11... | collective-permute-start | bytes 1179656 | tf_op jit(solution)/shard_map/ppermute | solution.py:713
  48.1 107.0 %collective-permute-start.8 = (f32[24,32,128]{2,1,0:T(8,128)S(1)}, f32[24,32,128]{2,1,0:T(8,128)S(1)}, u32[]{:S(2)}, u32[]{:S(2)}) collective-permute-start(f32[24,32,128]{2,1,0:T(8,128)S(1)} %get-tuple-element.19), channel_id=1, source_target_pairs={{1,3},{2,0},{3,5},{4,2},{5,7},{6,4},{7,9},{8,6},{9,11},{10,8},{11,... | collective-permute-start | bytes 1179656 | tf_op jit(solution)/shard_map/ppermute | solution.py:713
  112.4 19.5 %collective-permute-start.15 = (f32[16,128]{1,0:T(8,128)S(1)}, f32[16,128]{1,0:T(8,128)S(1)}, u32[]{:S(2)}, u32[]{:S(2)}) collective-permute-start(f32[16,128]{1,0:T(8,128)S(1)} %shard_map.62), channel_id=1, source_target_pairs={{1,2},{2,1},{3,4},{4,3},{5,6},{6,5},{7,8},{8,7},{9,10},{10,9},{11,... | collective-permute-start | bytes 24584 | tf_op jit(solution)/shard_map/ppermute | solution.py:713
  114.8 17.1 %collective-permute-start.14 = (f32[16,128]{1,0:T(8,128)S(1)}, f32[16,128]{1,0:T(8,128)S(1)}, u32[]{:S(2)}, u32[]{:S(2)}) collective-permute-start(f32[16,128]{1,0:T(8,128)S(1)} %shard_map.62), channel_id=1, source_target_pairs={{1,3},{2,0},{3,5},{4,2},{5,7},{6,4},{7,9},{8,6},{9,11},{10,8},{11,... | collective-permute-start | bytes 24584 | tf_op jit(solution)/shard_map/ppermute | solution.py:713
  118.0 1.3 collective-permute-start.11
  119.3 7.6 %collective-permute-start.12 = (f32[16,128]{1,0:T(8,128)S(1)}, f32[16,128]{1,0:T(8,128)S(1)}, u32[]{:S(2)}, u32[]{:S(2)}) collective-permute-start(f32[16,128]{1,0:T(8,128)S(1)} %shard_map.62), channel_id=1, source_target_pairs={{0,2},{2,4},{3,1},{4,6},{5,3},{6,8},{7,5},{8,10},{9,7},{10,12},{11... | collective-permute-start | bytes 24584 | tf_op jit(solution)/shard_map/ppermute | solution.py:713
  127.0 5.0 %collective-permute-start.13 = (f32[16,128]{1,0:T(8,128)S(1)}, f32[16,128]{1,0:T(8,128)S(1)}, u32[]{:S(2)}, u32[]{:S(2)}) collective-permute-start(f32[16,128]{1,0:T(8,128)S(1)} %shard_map.62), channel_id=1, source_target_pairs={{0,3},{2,5},{3,0},{4,7},{5,2},{6,9},{7,4},{8,11},{9,6},{10,13},{11... | collective-permute-start | bytes 24584 | tf_op jit(solution)/shard_map/ppermute | solution.py:713
  131.9 10.1 %collective-permute-start.16 = (f32[6,16,128]{2,1,0:T(8,128)S(1)}, f32[6,16,128]{2,1,0:T(8,128)S(1)}, u32[]{:S(2)}, u32[]{:S(2)}) collective-permute-start(f32[6,16,128]{2,1,0:T(8,128)S(1)} %get-tuple-element.24), channel_id=1, source_target_pairs={{0,32},{2,34},{4,36},{6,38},{8,40},{10,42},{12,44},{14,46},{16,48}... | collective-permute-start | bytes 147464 | tf_op jit(solution)/shard_map/ppermute | solution.py:713
  139.9 7.2 %collective-permute-start.17 = (f32[6,16,128]{2,1,0:T(8,128)S(1)}, f32[6,16,128]{2,1,0:T(8,128)S(1)}, u32[]{:S(2)}, u32[]{:S(2)}) collective-permute-start(f32[6,16,128]{2,1,0:T(8,128)S(1)} %get-tuple-element.24), channel_id=1, source_target_pairs={{1,33},{3,35},{5,37},{7,39},{9,41},{11,43},{13,45},{15,47},{17,49}... | collective-permute-start | bytes 147464 | tf_op jit(solution)/shard_map/ppermute | solution.py:713

commit v2 on v1

--- a/solution.py
+++ b/solution.py
@@ -49,6 +49,23 @@
     return pltpu.roll(values, lax.rem(shift + 8 * size, size), values.ndim - 2)
 
 
+def loop(low, high, step, unroll):
+    whole = (high - low) // unroll
+    if whole == 1:
+        for i in range(low, low + unroll):
+            step(i)
+    elif whole > 1:
+
+        def chunk(t, carry):
+            for n in range(unroll):
+                step(low + t * unroll + n)
+            return carry
+
+        lax.fori_loop(0, whole, chunk, 0)
+    for i in range(low + whole * unroll, high):
+        step(i)
+
+
 def three_parts(values):
     first = values.astype(BF16)
     rest = values - first.astype(F32)
@@ -73,32 +90,37 @@
     return lax.shift_right_arithmetic(value * 205, 11)
 
 
-def edge_kernel(sc, u, f, m, msg1, msg2, strip, strip1, strip2):
+def edge_kernel(sc, u, f, m, msg1, msg2, strip, strip1, strip2, vu, vf, vm, sems):
     gz = sc[0]
     low_first = gz == 0
     s1 = jnp.where(low_first, BX - DEEP, 0)
     s2 = BX - DEEP - s1
     f1 = jnp.where(low_first, BX - DEEP + 1, 0)
     f2 = BX - DEEP + 1 - f1
-    for out, s, fs in ((msg1, s1, f1), (msg2, s2, f2)):
-        for k in range(3):
-            out[k * DEEP : (k + 1) * DEEP] = u[k, pl.ds(s, DEEP)]
-            base = 3 * DEEP + k * (DEEP - 1)
-            out[base : base + DEEP - 1] = f[k, pl.ds(fs, DEEP - 1)]
-        out[PLANES - DEEP : PLANES] = m[pl.ds(s, DEEP)]
+    loads = [pltpu.make_async_copy(u, vu, sems.at[0]), pltpu.make_async_copy(f, vf, sems.at[1])]
+    loads.append(pltpu.make_async_copy(m, vm, sems.at[2]))
+    for load in loads:
+        load.start()
+    for load in loads:
+        load.wait()
     lane = iota((BY, 128), 1)
     extra = jnp.where(low_first, DEEP, 0)
 
-    def one(x, carry):
+    def one(x):
         total = jnp.zeros((BY, 128), F32)
         for c in range(7):
-            source = u[c, x] if c < 3 else (f[c - 3, x] if c < 6 else m[x])
+            source = vu[c, x] if c < 3 else (vf[c - 3, x] if c < 6 else vm[x])
             moved = lane_roll(source, extra + DEEP * c)
             total = jnp.where((lane >= DEEP * c) & (lane < DEEP * (c + 1)), moved, total)
         strip[x] = total
-        return carry
-
-    lax.fori_loop(0, BX, one, 0)
+
+    loop(0, BX, one, 8)
+    for out, s, fs in ((msg1, s1, f1), (msg2, s2, f2)):
+        for k in range(3):
+            out[k * DEEP : (k + 1) * DEEP] = vu[k, pl.ds(s, DEEP)]
+            base = 3 * DEEP + k * (DEEP - 1)
+            out[base : base + DEEP - 1] = vf[k, pl.ds(fs, DEEP - 1)]
+        out[PLANES - DEEP : PLANES] = vm[pl.ds(s, DEEP)]
     strip1[...] = strip[pl.ds(s1, DEEP)]
     strip2[...] = strip[pl.ds(s2, DEEP)]
 
@@ -156,20 +178,19 @@
     take_own = window(sc[3])
     x0 = sc[1] + 5
 
-    def own(i, carry):
+    def own(i):
         field, force = take_own(x0 + i)
         own_u[i] = field
         own_f[i] = force
-        return carry
-
-    lax.fori_loop(0, WIN, own, 0)
+
+    loop(0, WIN, own, 6)
 
     sub = iota((8, 128), 0)
     for msg, side, base, upward in ((msg1, side1, 4, low_first), (msg2, side2, 7, gz != 0)):
         take = window(sc[base + 2])
         start = sc[base] + 5
 
-        def pair(i, carry, msg=msg, take=take, start=start, upward=upward):
+        def pair(i, msg=msg, take=take, start=start, upward=upward):
             mixed = jnp.zeros((8, 128), F32)
             number = 0
             for step in range(2):
@@ -180,11 +201,10 @@
                     mixed = jnp.where((sub >= 2 * number) & (sub < 2 * number + 2), row_roll(edge, 2 * number), mixed)
                     number += 1
             msg[i, 32:40] = mixed
-            return carry
-
-        lax.fori_loop(0, WIN // 2, pair, 0)
-
-        def plane(i, carry, side=side, upward=upward):
+
+        loop(0, WIN // 2, pair, 3)
+
+        def plane(i, side=side, upward=upward):
             x = i + DEEP - FSWEEPS
 
             def edge(values):
@@ -193,9 +213,8 @@
             every = [edge(eu[k, x]) for k in range(3)] + [edge(ef[k, x]) for k in range(3)] + [edge(em[x]), edge(es[x])]
             for j in range(4):
                 side[i, 8 * j : 8 * j + 8] = jnp.where(sub < 4, every[2 * j], row_roll(every[2 * j + 1], 4))
-            return carry
-
-        lax.fori_loop(0, AX, plane, 0)
+
+        loop(0, AX, plane, 6)
 
 
 def invert(chains):
@@ -208,28 +227,47 @@
     def column_of(values, j):
         return jnp.broadcast_to(values[:, j : j + 1], (8, 128))
 
+    empty = jnp.zeros((8, 128), F32)
     for b in range(TILES):
         in_block = (lane >= 8 * b) & (lane < 8 * b + 8)
         for chain in chains:
-            columns = [[column_of(tile, 8 * b + j) for j in range(8)] for tile in chain]
             pivot = chain[b]
-            own = columns[b]
-            for j in range(8):
-                at = lane == 8 * b + j
-                scale = 1.0 / row_of(own[j], j)
-                line = jnp.where(at, 1.0, row_of(pivot, j)) * scale
-                pivot = jnp.where(sub == j, line, jnp.where(at, 0.0, pivot) - own[j] * line)
-                for n in range(j + 1, 8):
-                    other = row_of(own[n], j) * scale
-                    own[n] = jnp.where(sub == j, other, own[n] - own[j] * other)
-            lines = [row_of(pivot, j) for j in range(8)]
+            own = [column_of(pivot, 8 * b + j) for j in range(8)]
+            for j in range(0, 8, 2):
+                here0, here1 = sub == j, sub == j + 1
+                at0, at1 = lane == 8 * b + j, lane == 8 * b + j + 1
+                p00, p01 = row_of(own[j], j), row_of(own[j + 1], j)
+                p10, p11 = row_of(own[j], j + 1), row_of(own[j + 1], j + 1)
+                scale = pl.reciprocal(p00 * p11 - p01 * p10, approx=True)
+                side0 = jnp.where(here0, -1.0, jnp.where(here1, 0.0, own[j]))
+                side1 = jnp.where(here0, 0.0, jnp.where(here1, -1.0, own[j + 1]))
+                both = here0 | here1
+
+                def step(values, line0, line1):
+                    first = p11 * line0 - p01 * line1
+                    second = p00 * line1 - p10 * line0
+                    return jnp.where(both, 0.0, values) - (side0 * first + side1 * second) * scale
+
+                for n in range(j + 2, 8):
+                    own[n] = step(own[n], row_of(own[n], j), row_of(own[n], j + 1))
+                line0 = jnp.where(at0, 1.0, jnp.where(at1, 0.0, row_of(pivot, j)))
+                line1 = jnp.where(at0, 0.0, jnp.where(at1, 1.0, row_of(pivot, j + 1)))
+                pivot = step(jnp.where(at0 | at1, 0.0, pivot), line0, line1)
+            if b + 1 < TILES:
+                after = jnp.where(in_block, 0.0, chain[b + 1])
+                terms = [column_of(chain[b + 1], 8 * b + j) * row_of(pivot, j) for j in range(8)]
+                while len(terms) > 1:
+                    terms = [p + q for p, q in zip(terms[0::2], terms[1::2])]
+                after = after - terms[0]
+            spread = jnp.concatenate([pivot if r == b else empty for r in range(16)], axis=0)
+            change = dot(jnp.concatenate(chain, axis=0), spread)
             for i in range(TILES):
-                if i != b:
-                    tile = jnp.where(in_block, 0.0, chain[i])
-                    for j in range(8):
-                        tile = tile - columns[i][j] * lines[j]
-                    chain[i] = tile
-            chain[b] = pivot
+                if i == b:
+                    chain[i] = pivot
+                elif i == b + 1:
+                    chain[i] = after
+                else:
+                    chain[i] = jnp.where(in_block, 0.0, chain[i]) - change[8 * i : 8 * i + 8]
     return chains
 
 
@@ -250,8 +288,14 @@
     row32 = iota((WY, 128), 0)
     shift = -(rely + 11)
 
-    def unpack(i, carry):
+    inside_y = sc[11] - 5 + row32
+    inside_z = sc[12] - 5 + inner
+    inside = (inside_y >= 0) & (inside_y < ny) & (inside_z >= 0) & (inside_z < nz)
+
+    def unpack(i):
         for step in range(2):
+            gx = sc[10] - 5 + 2 * i + step
+            good = inside & (gx >= 0) & (gx < nx)
             for which in range(2):
                 number = 2 * step + which
                 first = r1[i, 8 * number : 8 * number + 8]
@@ -266,50 +310,43 @@
                 )
                 tall = row_roll(tall, shift)[0:WY]
                 if which == 0:
+                    tall = jnp.where(good, tall, 0.0)
                     ua[2 * i + step] = tall
                     moved = jnp.where(group == 0, lane_roll(tall, 32), 0.0)
                     moved = jnp.where(group == 1, lane_roll(tall, 64), moved)
                     m3[2 * i + step] = jnp.where(group == 2, lane_roll(tall, 96), moved)
                 else:
                     fo[2 * i + step] = tall
-        return carry
-
-    lax.fori_loop(0, WIN // 2, unpack, 0)
-
-    inside_y = sc[11] - 5 + row32
-    inside_z = sc[12] - 5 + inner
-    inside = (inside_y >= 0) & (inside_y < ny) & (inside_z >= 0) & (inside_z < nz)
-
-    def faces(i, carry):
+
+    loop(0, WIN // 2, unpack, 3)
+
+    def faces(i):
         here = m3[i]
         cx[i] = 0.5 * (here + m3[jnp.minimum(i + 1, WIN - 1)])
         cy[i] = 0.5 * (here + row_roll(here, -1))
         cz[i] = 0.5 * (here + lane_roll(here, -1))
-        return carry
-
-    lax.fori_loop(0, WIN, faces, 0)
-
-    def scale(i, carry):
+
+    loop(0, WIN, faces, 10)
+
+    def scale(i):
         total = MASS_TERM + cx[i] + cx[i - 1] + cy[i] + row_roll(cy[i], 1) + cz[i] + lane_roll(cz[i], 1)
         gx = sc[10] - 5 + i
         good = inside & (gx >= 0) & (gx < nx)
         iv[i] = jnp.where(good, 1.0 / total, 0.0)
-        return carry
-
-    lax.fori_loop(1, WIN - 1, scale, 0)
+
+    loop(1, WIN - 1, scale, 7)
 
     for sweep in range(FSWEEPS):
         src, dst = (ua, ub) if sweep % 2 == 0 else (ub, ua)
 
-        def relax(i, carry, src=src, dst=dst):
+        def relax(i, src=src, dst=dst):
             here = src[i]
             total = fo[i] + cx[i] * src[i + 1] + cx[i - 1] * src[i - 1]
             total = total + cy[i] * row_roll(here, -1) + row_roll(cy[i] * here, 1)
             total = total + cz[i] * lane_roll(here, -1) + lane_roll(cz[i] * here, 1)
             dst[i] = total * iv[i]
-            return carry
-
-        lax.fori_loop(sweep + 1, WIN - 1 - sweep, relax, 0)
+
+        loop(sweep + 1, WIN - 1 - sweep, relax, WIN)
 
     line = iota((128, 384), 0)
     column = iota((128, 384), 1)
@@ -329,7 +366,7 @@
     even_z = ((inner - 5) & 1) == 0
     rows[...] = jnp.zeros(rows.shape, F32)
 
-    def layer(a, carry):
+    def layer(a):
         sums = None
         for odd in range(2):
             i = 5 + 2 * a + odd
@@ -365,9 +402,8 @@
             for k in range(3):
                 piece = tall[n * WY : (n + 1) * WY, 128 * k : 128 * k + 128] * pick_y
                 rows[n, k, pl.ds(a, 1), :] = jnp.sum(piece, axis=0, keepdims=True)
-        return carry
-
-    lax.fori_loop(0, PC, layer, 0)
+
+    loop(0, PC, layer, 2)
 
     lane16 = iota((16, 128), 1)
     row16 = iota((16, 128), 0)
@@ -461,11 +497,8 @@
     lax.fori_loop(0, 5, couple, 0)
     br[4] = jnp.zeros((2, 128, 128), F32)
 
-    apart = [sub + 8 * r - lane8 for r in range(16)]
-
-    def diagonal(n, x):
-        values = spread(far, n, x)
-        return jnp.concatenate([jnp.where(a == 0, values, 0.0) for a in apart], axis=0)
+    on_diagonal = iota((128, 128), 0) == iota((128, 128), 1)
+    ones = jnp.ones((128, 128), BF16)
 
     def tiles_of(x):
         return [hess[x, 8 * r : 8 * r + 8, :] for r in range(TILES)]
@@ -478,22 +511,23 @@
         left_tiles, right_tiles = invert([tiles_of(t), tiles_of(right)])
         for s, tiles, x, step, ref in ((0, left_tiles, t, 1, bl), (1, right_tiles, right, -1, br)):
             q = whole(tiles)
-            two = diagonal(s, x)
-            w = jnp.concatenate([ref[t, 0], two], axis=1)
-            wt = jnp.concatenate([ref[t, 1], two], axis=0)
-            y = dot(q, w)
-            yt[s, t] = dot(wt, q)
-            schur = dot(wt, y)
+            row = jnp.broadcast_to(far[s, pl.ds(x, 1), :], (128, 128))
+            column = dot_exact(jnp.where(on_diagonal, row, 0.0), ones)
+            w, wt = ref[t, 0], ref[t, 1]
+            y1, y2 = dot(q, w), q * row
+            yt[s, t, 0:128] = dot(wt, q)
+            yt[s, t, 128:256] = column * q
+            s1 = dot(wt, jnp.concatenate([y1, y2], axis=1))
             g = gs[x]
-            zs[s, t] = dot(g, q)
-            gy = dot(g, y)
+            z = dot(g, q)
+            zs[s, t] = z
             one, two_on = x + step, x + 2 * step
-            hess[one] = hess[one] - schur[0:128, 0:128]
-            hess[two_on] = hess[two_on] - schur[128:256, 128:256]
-            ref[t + 1, 0] = ref[t + 1, 0] - schur[0:128, 128:256]
-            ref[t + 1, 1] = ref[t + 1, 1] - schur[128:256, 0:128]
-            gs[one] = gs[one] - gy[:, 0:128]
-            gs[two_on] = gs[two_on] - gy[:, 128:256]
+            hess[one] = hess[one] - s1[:, 0:128]
+            hess[two_on] = hess[two_on] - column * y2
+            ref[t + 1, 0] = ref[t + 1, 0] - s1[:, 128:256]
+            ref[t + 1, 1] = ref[t + 1, 1] - column * y1
+            gs[one] = gs[one] - dot(z, w)
+            gs[two_on] = gs[two_on] - z * row[0:8]
         return carry
 
     lax.fori_loop(0, 4, eliminate, 0)
@@ -540,7 +574,12 @@
     spot = jnp.where(low_first, 0, BZ - DEEP)
     strip_lanes = (lane >= spot) & (lane < spot + DEEP)
 
+    row24 = iota((AX, 128), 0)
+    inside24 = (sc[14] - FSWEEPS + row24 >= 0) & (sc[14] - FSWEEPS + row24 < ny)
+
     def build(dest, values16):
+        gx = sc[13] - FSWEEPS + dest
+        good = inside24 & (gx >= 0) & (gx < nx)
         for q in range(8):
             j = q // 2
             a = s1[dest, 8 * j : 8 * j + 8]
@@ -554,6 +593,7 @@
             tall = jnp.concatenate(
                 [jnp.where(sub < 4, low, t0), jnp.where(sub < 4, t0, t1), jnp.where(sub < 4, t1, high)], axis=0
             )
+            tall = jnp.where(good, tall, 0.0)
             if q < 7:
                 ref = ua.at[q] if q < 3 else (fo.at[q - 3] if q < 6 else mo)
                 ref[dest, :, 0:128] = tall
@@ -562,13 +602,12 @@
                     ref = ua.at[c] if c < 3 else (fo.at[c - 3] if c < 6 else mo)
                     ref[dest, :, 128:256] = jnp.where(strip_lanes, lane_roll(tall, spot - DEEP * c), 0.0)
 
-    def inner_plane(i, carry):
+    def inner_plane(i):
         build(i + FSWEEPS, [u[k, i] for k in range(3)] + [f[k, i] for k in range(3)] + [m[i], strip[i]])
-        return carry
-
-    lax.fori_loop(0, BX, inner_plane, 0)
-
-    def outer_plane(i, carry):
+
+    loop(0, BX, inner_plane, 2)
+
+    def outer_plane(i):
         for a, b, sa, sb, start, dest in (
             (x1, x2, strip2, strip1, lead, i), (x2, x1, strip1, strip2, 0, i + FSWEEPS + BX),
         ):
@@ -584,9 +623,8 @@
                 + [pick(3 * DEEP + k * (DEEP - 1) + force) for k in range(3)]
                 + [pick(PLANES - DEEP + j), jnp.where(low_first, sa[j], sb[j])],
             )
-        return carry
-
-    lax.fori_loop(0, FSWEEPS, outer_plane, 0)
+
+    loop(0, FSWEEPS, outer_plane, 1)
 
     row = iota((AX, 256), 0)
     wide = iota((AX, 256), 1)
@@ -594,27 +632,25 @@
     second = (wide >= 128 + spot) & (wide < 128 + spot + DEEP)
     inside = (gy >= 0) & (gy < ny) & ((wide < 128) | second)
 
-    def faces(i, carry):
+    def faces(i):
         here = mo[i]
         cx[i] = 0.5 * (here + mo[jnp.minimum(i + 1, AX - 1)])
         cy[i] = 0.5 * (here + row_roll(here, -1))
         cz[i] = 0.5 * (here + lane_roll(here, -1))
-        return carry
-
-    lax.fori_loop(0, AX, faces, 0)
-
-    def scale(i, carry):
+
+    loop(0, AX, faces, 4)
+
+    def scale(i):
         total = MASS_TERM + cx[i] + cx[i - 1] + cy[i] + row_roll(cy[i], 1) + cz[i] + lane_roll(cz[i], 1)
         gx = sc[13] - FSWEEPS + i
         good = inside & (gx >= 0) & (gx < nx)
         iv[i] = jnp.where(good, 1.0 / total, 0.0)
-        return carry
-
-    lax.fori_loop(1, AX - 1, scale, 0)
+
+    loop(1, AX - 1, scale, 2)
     for sweep in range(FSWEEPS):
         src, dst = (ua, ub) if sweep % 2 == 0 else (ub, ua)
 
-        def relax(i, carry, src=src, dst=dst, last=sweep == FSWEEPS - 1):
+        def relax(i, src=src, dst=dst, last=sweep == FSWEEPS - 1):
             for k in range(3):
                 here = src[k, i]
                 total = fo[k, i] + cx[i] * src[k, i + 1] + cx[i - 1] * src[k, i - 1]
@@ -625,9 +661,8 @@
                     out[k, i - FSWEEPS] = row_roll(total[:, 0:128], -FSWEEPS)[0:BY]
                 else:
                     dst[k, i] = total
-            return carry
-
-        lax.fori_loop(sweep + 1, AX - 1 - sweep, relax, 0)
+
+        loop(sweep + 1, AX - 1 - sweep, relax, 2)
 
 
 def taper(offset):
@@ -650,7 +685,7 @@
     lanes128 = iota((128, 128), 1).astype(F32)
     acc[...] = jnp.zeros(acc.shape, F32)
 
-    def add(n, carry):
+    def add(n):
         delta = parts[n]
 
         def place(axis, low):
@@ -672,15 +707,14 @@
         expand = jnp.where((apart >= 0.0) & (apart < 2.0) & (rows128 < PC * PC), 1.0, 0.0).astype(BF16)
         tall = jnp.concatenate([jnp.broadcast_to(lines[x : x + 1, :], (BY, 128)) * cover for x in range(BX)], axis=0)
         acc[...] += dot_exact(tall, expand) * taper(off_z[0:1, :])
-        return carry
-
-    lax.fori_loop(0, number, add, 0)
+
+    loop(0, number, add, 3)
     for x in range(BX):
         out[x] = m[x] * (1.0 + acc[16 * x : 16 * x + 16, :])
 
 
-def call(kernel, shapes, scratch, inputs, flops):
-    specs = [pl.BlockSpec(memory_space=pltpu.SMEM)] + [pl.BlockSpec(memory_space=pltpu.VMEM)] * (len(inputs) - 1)
+def call(kernel, shapes, scratch, inputs, flops, space=pltpu.VMEM):
+    specs = [pl.BlockSpec(memory_space=pltpu.SMEM)] + [pl.BlockSpec(memory_space=space)] * (len(inputs) - 1)
     single = not isinstance(shapes, list)
     outs = [jax.ShapeDtypeStruct(s, F32) for s in ([shapes] if single else shapes)]
     results = pl.pallas_call(
@@ -688,7 +722,7 @@
         out_shape=outs,
         in_specs=specs,
         out_specs=[pl.BlockSpec(memory_space=pltpu.VMEM)] * len(outs),
-        scratch_shapes=[pltpu.VMEM(s, F32) for s in scratch],
+        scratch_shapes=[pltpu.VMEM(s, F32) if isinstance(s, tuple) else s for s in scratch],
         compiler_params=pltpu.CompilerParams(vmem_limit_bytes=VMEM_LIMIT),
         cost_estimate=pl.CostEstimate(flops=flops, bytes_accessed=1 << 20, transcendentals=0),
     )(*inputs)
@@ -707,9 +741,8 @@
         for x in range(counts[0]):
             for y in range(counts[1]):
                 for z in range(counts[2]):
-                    to = move(x, y, z)
-                    if all(0 <= t < c for t, c in zip(to, counts)):
-                        pairs.append(((x * counts[1] + y) * counts[2] + z, (to[0] * counts[1] + to[1]) * counts[2] + to[2]))
+                    to = [t % c for t, c in zip(move(x, y, z), counts)]
+                    pairs.append(((x * counts[1] + y) * counts[2] + z, (to[0] * counts[1] + to[1]) * counts[2] + to[2]))
         return lax.ppermute(values, AXES, pairs)
 
     def turn(z):
@@ -725,9 +758,10 @@
     msg1, msg2, strip, strip1, strip2 = call(
         edge_kernel,
         [(PLANES, BY, 128), (PLANES, BY, 128), (BX, BY, 128), (DEEP, BY, 128), (DEEP, BY, 128)],
-        [],
+        [(3, BX, BY, BZ), (3, BX, BY, BZ), (BX, BY, BZ), pltpu.SemaphoreType.DMA((3,))],
         [first, start_field, forcing, modulus],
         1 << 20,
+        pl.ANY,
     )
     x1 = send(msg1, lambda x, y, z: (x + turn(z), y, z))
     x2 = send(msg2, lambda x, y, z: (x - turn(z), y, z))
@@ -757,14 +791,9 @@
         [scalar, own_u, own_f, r1, r2],
         1 << 33,
     )
-    beside = [delta]
-    beside.append(send(delta, lambda x, y, z: (x, y, 1 - z)))
-    for step in (1, -1):
-        beside.append(send(delta, lambda x, y, z, step=step: (x, y + step * turn(z), z)))
-        beside.append(send(delta, lambda x, y, z, step=step: (x, y + step * turn(z), 1 - z)))
-    plane = jnp.stack(beside)
-    after = send(plane, lambda x, y, z: (x + turn(z), y, z))
-    before = send(plane, lambda x, y, z: (x - turn(z), y, z))
+    plane = jnp.stack([delta, send(delta, lambda x, y, z: (x, y, 1 - z))])
+    right = send(plane, lambda x, y, z: (x, y + turn(z), z))
+    left = send(plane, lambda x, y, z: (x, y - turn(z), z))
     wide = (AX, AX, 256)
     displacement = call(
         functools.partial(field_kernel, sizes),
@@ -773,6 +802,10 @@
         [scalar, start_field, forcing, modulus, x1, x2, far_strip, far1, far2, b1, b2],
         1 << 30,
     )
+    right, left, displacement = lax.optimization_barrier((right, left, displacement))
+    plane = jnp.concatenate([plane, right, left])
+    after = send(plane, lambda x, y, z: (x + turn(z), y, z))
+    before = send(plane, lambda x, y, z: (x - turn(z), y, z))
     new_modulus = call(
         final_kernel,
         (BX, BY, BZ),

time: 172 us -> 110 us (0.64)
  the two profiles are of different devices: /device:TPU:112 before, /device:TPU:0 now
where the time goes in v2:
time: 110 us; the launch traced here: 108 us
  Pallas kernels  57.6 us (52%)
  starting transfers between devices  32 us (29%)
  waiting for transfers between devices  12.3 us (11%)
  local copies, waits for them, and re-layouts  4.81 us (4%)
    pallas_call x5, Pallas kernels, call(): pl.pallas_call(kernel, out_shape=outs, in_specs=specs, out_specs=[pl.Bloc...  57.6 us
    ppermute x16, starting transfers between devices, send(): return lax.ppermute(values, AXES, pairs)  32 us
    ppermute x16, waiting for transfers between devices, send(): return lax.ppermute(values, AXES, pairs)  12.3 us
    unnamed x21, local copies, waits for them, and re-layouts  4.1 us
  transfers between devices with their start and end apart: 16, of which 5 were waited for; matrix products, arithmetic and copies ran while one was open for 1% of the time, Pallas kernels for 43%

profile of v2, /device:TPU:0, one launch (start us, length us, event | category | flops | bytes accessed | tf_op | source)
XLA Modules:
  0.0 107.7 jit_solution(15451230033802459704)
XLA Ops:
  0.6 0.0 copy-start
  0.6 1.0 copy-done
  1.6 0.0 copy-start.2
  1.6 1.0 copy-done.2
  2.6 0.0 copy-start.4
  2.6 0.9 copy-done.4
  3.5 0.0 copy-start.1
  3.5 0.0 copy-start.3
  3.5 0.0 copy-start.5
  3.5 1.7 %shard_map.59 = (f32[67,16,128]{2,1,0:T(8,128)S(1)}, f32[67,16,128]{2,1,0:T(8,128)S(1)}, f32[16,16,128]{2,1,0:T(8,128)S(1)}, f32[10,16,128]{2,1,0:T(8,128)}, f32[10,16,128]{2,1,0:T(8,128)}) custom-call(s32[1]{0:T(128)} %bitcast.sc, f32[3,16,16,128]{3,2,1,0:T(8,128)S(1)} %copy-done, f32[3,16,16,128]{3,2,1,0:T(8,128)S(1)} %copy-done.2, ...), custom_call_target="tpu_custom_call" | custom-call | flops 1048576 | bytes 1048576 | tf_op jit(solution)/shard_map/pallas_call | solution.py:720
  5.2 0.3 collective-permute-start.2
  5.5 4.0 %collective-permute-start.3 = (f32[67,16,128]{2,1,0:T(8,128)S(1)}, f32[67,16,128]{2,1,0:T(8,128)S(1)}, u32[]{:S(2)}, u32[]{:S(2)}) collective-permute-start(f32[67,16,128]{2,1,0:T(8,128)S(1)} %get-tuple-element.17), channel_id=1, source_target_pairs={{0,224},{1,33},{2,226},{3,35},{4,228},{5,37},{6,230},{7,39},{8,232... | collective-permute-start | bytes 1646600 | tf_op jit(solution)/shard_map/ppermute | solution.py:746
  9.5 0.0 copy-start.6
  9.5 0.7 copy-done.6
  10.2 0.1 add_subtract_fusion.1
  10.2 1.5 %collective-permute-start.1 = (s32[1,3]{1,0:T(1,128)S(1)}, s32[1,3]{1,0:T(1,128)S(1)}, u32[]{:S(2)}, u32[]{:S(2)}) collective-permute-start(s32[1,3]{1,0:T(1,128)S(1)} %add_subtract_fusion.1), channel_id=1, source_target_pairs={{0,2},{1,31},{2,4},{3,1},{4,6},{5,3},{6,8},{7,5},{8,10},{9,7},{10,... | collective-permute-start | bytes 44 | tf_op jit(solution)/shard_map/ppermute | solution.py:746
  11.7 3.9 %collective-permute-start = (s32[1,3]{1,0:T(1,128)S(1)}, s32[1,3]{1,0:T(1,128)S(1)}, u32[]{:S(2)}, u32[]{:S(2)}) collective-permute-start(s32[1,3]{1,0:T(1,128)S(1)} %add_subtract_fusion.1), channel_id=1, source_target_pairs={{0,30},{1,3},{2,0},{3,5},{4,2},{5,7},{6,4},{7,9},{8,6},{9,11},{10,... | collective-permute-start | bytes 44 | tf_op jit(solution)/shard_map/ppermute | solution.py:746
  15.6 0.0 collective-permute-start.5
  15.6 1.5 %collective-permute-done.1 = s32[1,3]{1,0:T(1,128)S(1)} collective-permute-done((s32[1,3]{1,0:T(1,128)S(1)}, s32[1,3]{1,0:T(1,128)S(1)}, u32[]{:S(2)}, u32[]{:S(2)}) %collective-permute-start.1) | collective-permute-done | bytes 44 | tf_op jit(solution)/shard_map/ppermute | solution.py:746
  17.1 1.2 %collective-permute-start.6 = (f32[10,16,128]{2,1,0:T(8,128)}, f32[10,16,128]{2,1,0:T(8,128)S(1)}, u32[]{:S(2)}, u32[]{:S(2)}) collective-permute-start(f32[10,16,128]{2,1,0:T(8,128)} %get-tuple-element.20), channel_id=1, source_target_pairs={{0,225},{1,32},{2,227},{3,34},{4,229},{5,36},{6,231},{7,38},{8,233... | collective-permute-start | bytes 245768 | tf_op jit(solution)/shard_map/ppermute | solution.py:746
  18.3 0.0 collective-permute-done
  18.3 0.0 copy-start.7
  18.3 0.5 copy-done.7
  18.8 2.1 %collective-permute-start.4 = (f32[16,16,128]{2,1,0:T(8,128)S(1)}, f32[16,16,128]{2,1,0:T(8,128)S(1)}, u32[]{:S(2)}, u32[]{:S(2)}) collective-permute-start(f32[16,16,128]{2,1,0:T(8,128)S(1)} %get-tuple-element.18), channel_id=1, source_target_pairs={{0,1},{1,0},{2,3},{3,2},{4,5},{5,4},{6,7},{7,6},{8,9},{9,8},{10,11... | collective-permute-start | bytes 393224 | tf_op jit(solution)/shard_map/ppermute | solution.py:746
  20.9 0.1 add_subtract_fusion
  21.0 0.7 concatenate.13.sc
  21.7 0.0 collective-permute-done.5.strip1
  21.7 2.8 %collective-permute-done.6.strip2 = f32[10,16,128]{2,1,0:T(8,128)S(1)} collective-permute-done((f32[10,16,128]{2,1,0:T(8,128)}, f32[10,16,128]{2,1,0:T(8,128)S(1)}, u32[]{:S(2)}, u32[]{:S(2)}) %collective-permute-start.6) | collective-permute-done | bytes 81952 | tf_op jit(solution)/shard_map/ppermute | solution.py:746
  24.5 0.0 collective-permute-done.4.strip
  24.5 0.0 collective-permute-done.2.x1
  24.5 0.0 collective-permute-done.3.x2
  24.5 0.0 copy-done.1
  24.5 0.0 copy-done.3
  24.5 0.0 copy-done.5
  24.5 4.6 %shard_map.60 = (f32[30,16,128]{2,1,0:T(8,128)S(1)}, f32[30,16,128]{2,1,0:T(8,128)S(1)}, f32[15,40,128]{2,1,0:T(8,128)S(1)}, f32[15,40,128]{2,1,0:T(8,128)S(1)},...) custom-call(s32[16]{0:T(128)S(1)} %concatenate.13.sc, f32[3,16,16,128]{3,2,1,0:T(8,128)S(1)} %copy-done.1, ...), custom_call_target="tpu_custom_call" | custom-call | flops 4194304 | bytes 1048576 | tf_op jit(solution)/shard_map/pallas_call | solution.py:720
  29.2 1.6 %collective-permute-start.7 = (f32[15,40,128]{2,1,0:T(8,128)S(1)}, f32[15,40,128]{2,1,0:T(8,128)S(1)}, u32[]{:S(2)}, u32[]{:S(2)}) collective-permute-start(f32[15,40,128]{2,1,0:T(8,128)S(1)} %get-tuple-element.23), channel_id=1, source_target_pairs={{0,2},{1,31},{2,4},{3,1},{4,6},{5,3},{6,8},{7,5},{8,10},{9,7},{10,... | collective-permute-start | bytes 921608 | tf_op jit(solution)/shard_map/ppermute | solution.py:746
  30.7 3.9 %collective-permute-start.8 = (f32[15,40,128]{2,1,0:T(8,128)S(1)}, f32[15,40,128]{2,1,0:T(8,128)S(1)}, u32[]{:S(2)}, u32[]{:S(2)}) collective-permute-start(f32[15,40,128]{2,1,0:T(8,128)S(1)} %get-tuple-element.24), channel_id=1, source_target_pairs={{0,30},{1,3},{2,0},{3,5},{4,2},{5,7},{6,4},{7,9},{8,6},{9,11},{10,... | collective-permute-start | bytes 921608 | tf_op jit(solution)/shard_map/ppermute | solution.py:746
  34.6 0.0 collective-permute-start.12
  34.6 5.3 %collective-permute-start.13 = (f32[24,32,128]{2,1,0:T(8,128)S(1)}, f32[24,32,128]{2,1,0:T(8,128)S(1)}, u32[]{:S(2)}, u32[]{:S(2)}) collective-permute-start(f32[24,32,128]{2,1,0:T(8,128)S(1)} %get-tuple-element.26), channel_id=1, source_target_pairs={{0,30},{1,3},{2,0},{3,5},{4,2},{5,7},{6,4},{7,9},{8,6},{9,11},{10,... | collective-permute-start | bytes 1179656 | tf_op jit(solution)/shard_map/ppermute | solution.py:746
  39.9 0.0 collective-permute-done.7.r1
  40.0 1.8 %collective-permute-done.8.r2 = f32[15,40,128]{2,1,0:T(8,128)S(1)} collective-permute-done((f32[15,40,128]{2,1,0:T(8,128)S(1)}, f32[15,40,128]{2,1,0:T(8,128)S(1)}, u32[]{:S(2)}, u32[]{:S(2)}) %collective-permute-start.8) | collective-permute-done | bytes 307232 | tf_op jit(solution)/shard_map/ppermute | solution.py:746
  41.8 35.6 %shard_map.61 = f32[16,128]{1,0:T(8,128)S(1)} custom-call(s32[16]{0:T(128)S(1)} %concatenate.13.sc, f32[30,16,128]{2,1,0:T(8,128)S(1)} %get-tuple-element.21.own_u, f32[30,16,128]{2,1,0:T(8,128)S(1)} %get-tuple-element.22.own_f, f32[15,40,128]{2,1,0:T(8,128)S(1)} %collective-permute-done.7.r1, f32[15,40,128]{2,1,0:T(8,128)S(1)} %collective-permute-done.8.r2), custom_call_target="tpu_custom_call" | custom-call | flops 8589934592 | bytes 1048576 | tf_op jit(solution)/shard_map/pallas_call | solution.py:720
  77.4 2.3 %collective-permute-start.9 = (f32[16,128]{1,0:T(8,128)S(1)}, f32[16,128]{1,0:T(8,128)S(1)}, u32[]{:S(2)}, u32[]{:S(2)}) collective-permute-start(f32[16,128]{1,0:T(8,128)S(1)} %shard_map.61), channel_id=1, source_target_pairs={{0,1},{1,0},{2,3},{3,2},{4,5},{5,4},{6,7},{7,6},{8,9},{9,8},{10,11... | collective-permute-start | bytes 24584 | tf_op jit(solution)/shard_map/ppermute | solution.py:746
  79.7 0.8 collective-permute-done.9
  80.5 3.9 %collective-permute-start.11 = (f32[2,16,128]{2,1,0:T(8,128)S(1)}, f32[2,16,128]{2,1,0:T(8,128)S(1)}, u32[]{:S(2)}, u32[]{:S(2)}) collective-permute-start(f32[2,16,128]{2,1,0:T(8,128)S(1)} %pad_maximum_fusion.1), channel_id=1, source_target_pairs={{0,30},{1,3},{2,0},{3,5},{4,2},{5,7},{6,4},{7,9},{8,6},{9,11},{10,... | collective-permute-start | bytes 49160 | tf_op jit(solution)/shard_map/ppermute | solution.py:746
  84.5 0.0 collective-permute-start.10
  84.5 0.0 collective-permute-done.12.s1
  84.5 0.0 collective-permute-done.13.s2
  84.5 10.2 %shard_map.62 = f32[3,16,16,128]{3,2,1,0:T(8,128)} custom-call(s32[16]{0:T(128)S(1)} %concatenate.13.sc, f32[3,16,16,128]{3,2,1,0:T(8,128)S(1)} %copy-done.1, f32[3,16,16,128]{3,2,1,0:T(8,128)S(1)} %copy-done.3, f32[16,16,128]{2,1,0:T(8,128)S(1)} %copy-done.5, f32[67,16,128]{2,1,0:T(8,128)S(1)} %collective-permute-done.2.x1, ...), custom_call_target="tpu_custom_call" | custom-call | flops 1073741824 | bytes 1048576 | tf_op jit(solution)/shard_map/pallas_call | solution.py:720
  94.7 0.0 collective-permute-done.11
  94.7 0.0 collective-permute-done.10
  94.7 2.1 %collective-permute-start.15 = (f32[6,16,128]{2,1,0:T(8,128)S(1)}, f32[6,16,128]{2,1,0:T(8,128)S(1)}, u32[]{:S(2)}, u32[]{:S(2)}) collective-permute-start(f32[6,16,128]{2,1,0:T(8,128)S(1)} %pad_maximum_fusion), channel_id=1, source_target_pairs={{0,224},{1,33},{2,226},{3,35},{4,228},{5,37},{6,230},{7,39},{8,232... | collective-permute-start | bytes 147464 | tf_op jit(solution)/shard_map/ppermute | solution.py:746
  96.9 0.0 collective-permute-start.14
  96.9 5.3 %collective-permute-done.14 = f32[6,16,128]{2,1,0:T(8,128)S(1)} collective-permute-done((f32[6,16,128]{2,1,0:T(8,128)S(1)}, f32[6,16,128]{2,1,0:T(8,128)S(1)}, u32[]{:S(2)}, u32[]{:S(2)}) %collective-permute-start.14) | collective-permute-done | bytes 49184 | tf_op jit(solution)/shard_map/ppermute | solution.py:746
  102.2 0.0 collective-permute-done.15
  102.2 5.5 %shard_map.63 = f32[16,16,128]{2,1,0:T(8,128)} custom-call(s32[16]{0:T(128)S(1)} %concatenate.13.sc, f32[16,16,128]{2,1,0:T(8,128)S(1)} %copy-done.5, f32[18,16,128]{2,1,0:T(8,128)S(1)} %constant_dynamic-update-slice_fusion.parts), custom_call_target="tpu_custom_call" | custom-call | flops 16777216 | bytes 1048576 | tf_op jit(solution)/shard_map/pallas_call | solution.py:720
  (8 shorter events, 0.0 us)
Async XLA Ops:
  0.6 1.0 copy-start
  1.6 1.0 copy-start.2
  2.6 0.9 copy-start.4
  3.5 21.0 %copy-start.1 = (f32[3,16,16,128]{3,2,1,0:T(8,128)S(1)}, f32[3,16,16,128]{3,2,1,0:T(8,128)}, u32[]{:S(2)}) copy-start(f32[3,16,16,128]{3,2,1,0:T(8,128)} %u.5) | copy-start | bytes 1179652
  3.5 21.0 %copy-start.3 = (f32[3,16,16,128]{3,2,1,0:T(8,128)S(1)}, f32[3,16,16,128]{3,2,1,0:T(8,128)}, u32[]{:S(2)}) copy-start(f32[3,16,16,128]{3,2,1,0:T(8,128)} %f.5) | copy-start | bytes 1179652
  3.5 21.0 %copy-start.5 = (f32[16,16,128]{2,1,0:T(8,128)S(1)}, f32[16,16,128]{2,1,0:T(8,128)}, u32[]{:S(2)}) copy-start(f32[16,16,128]{2,1,0:T(8,128)} %m.7) | copy-start | bytes 393220
  5.2 19.3 %collective-permute-start.2 = (f32[67,16,128]{2,1,0:T(8,128)S(1)}, f32[67,16,128]{2,1,0:T(8,128)S(1)}, u32[]{:S(2)}, u32[]{:S(2)}) collective-permute-start(f32[67,16,128]{2,1,0:T(8,128)S(1)} %get-tuple-element.16), channel_id=1, source_target_pairs={{0,32},{1,225},{2,34},{3,227},{4,36},{5,229},{6,38},{7,231},{8,40}... | collective-permute-start | bytes 1646600 | tf_op jit(solution)/shard_map/ppermute | solution.py:746
  5.5 19.0 %collective-permute-start.3 = (f32[67,16,128]{2,1,0:T(8,128)S(1)}, f32[67,16,128]{2,1,0:T(8,128)S(1)}, u32[]{:S(2)}, u32[]{:S(2)}) collective-permute-start(f32[67,16,128]{2,1,0:T(8,128)S(1)} %get-tuple-element.17), channel_id=1, source_target_pairs={{0,224},{1,33},{2,226},{3,35},{4,228},{5,37},{6,230},{7,39},{8,232... | collective-permute-start | bytes 1646600 | tf_op jit(solution)/shard_map/ppermute | solution.py:746
  9.5 0.7 copy-start.6
  10.2 6.9 %collective-permute-start.1 = (s32[1,3]{1,0:T(1,128)S(1)}, s32[1,3]{1,0:T(1,128)S(1)}, u32[]{:S(2)}, u32[]{:S(2)}) collective-permute-start(s32[1,3]{1,0:T(1,128)S(1)} %add_subtract_fusion.1), channel_id=1, source_target_pairs={{0,2},{1,31},{2,4},{3,1},{4,6},{5,3},{6,8},{7,5},{8,10},{9,7},{10,... | collective-permute-start | bytes 44 | tf_op jit(solution)/shard_map/ppermute | solution.py:746
  11.7 6.5 %collective-permute-start = (s32[1,3]{1,0:T(1,128)S(1)}, s32[1,3]{1,0:T(1,128)S(1)}, u32[]{:S(2)}, u32[]{:S(2)}) collective-permute-start(s32[1,3]{1,0:T(1,128)S(1)} %add_subtract_fusion.1), channel_id=1, source_target_pairs={{0,30},{1,3},{2,0},{3,5},{4,2},{5,7},{6,4},{7,9},{8,6},{9,11},{10,... | collective-permute-start | bytes 44 | tf_op jit(solution)/shard_map/ppermute | solution.py:746
  15.6 6.1 %collective-permute-start.5 = (f32[10,16,128]{2,1,0:T(8,128)}, f32[10,16,128]{2,1,0:T(8,128)S(1)}, u32[]{:S(2)}, u32[]{:S(2)}) collective-permute-start(f32[10,16,128]{2,1,0:T(8,128)} %get-tuple-element.19), channel_id=1, source_target_pairs={{0,33},{1,224},{2,35},{3,226},{4,37},{5,228},{6,39},{7,230},{8,41}... | collective-permute-start | bytes 245768 | tf_op jit(solution)/shard_map/ppermute | solution.py:746
  17.1 7.4 %collective-permute-start.6 = (f32[10,16,128]{2,1,0:T(8,128)}, f32[10,16,128]{2,1,0:T(8,128)S(1)}, u32[]{:S(2)}, u32[]{:S(2)}) collective-permute-start(f32[10,16,128]{2,1,0:T(8,128)} %get-tuple-element.20), channel_id=1, source_target_pairs={{0,225},{1,32},{2,227},{3,34},{4,229},{5,36},{6,231},{7,38},{8,233... | collective-permute-start | bytes 245768 | tf_op jit(solution)/shard_map/ppermute | solution.py:746
  18.3 0.5 copy-start.7
  18.8 5.7 %collective-permute-start.4 = (f32[16,16,128]{2,1,0:T(8,128)S(1)}, f32[16,16,128]{2,1,0:T(8,128)S(1)}, u32[]{:S(2)}, u32[]{:S(2)}) collective-permute-start(f32[16,16,128]{2,1,0:T(8,128)S(1)} %get-tuple-element.18), channel_id=1, source_target_pairs={{0,1},{1,0},{2,3},{3,2},{4,5},{5,4},{6,7},{7,6},{8,9},{9,8},{10,11... | collective-permute-start | bytes 393224 | tf_op jit(solution)/shard_map/ppermute | solution.py:746
  29.2 10.8 %collective-permute-start.7 = (f32[15,40,128]{2,1,0:T(8,128)S(1)}, f32[15,40,128]{2,1,0:T(8,128)S(1)}, u32[]{:S(2)}, u32[]{:S(2)}) collective-permute-start(f32[15,40,128]{2,1,0:T(8,128)S(1)} %get-tuple-element.23), channel_id=1, source_target_pairs={{0,2},{1,31},{2,4},{3,1},{4,6},{5,3},{6,8},{7,5},{8,10},{9,7},{10,... | collective-permute-start | bytes 921608 | tf_op jit(solution)/shard_map/ppermute | solution.py:746
  30.7 11.1 %collective-permute-start.8 = (f32[15,40,128]{2,1,0:T(8,128)S(1)}, f32[15,40,128]{2,1,0:T(8,128)S(1)}, u32[]{:S(2)}, u32[]{:S(2)}) collective-permute-start(f32[15,40,128]{2,1,0:T(8,128)S(1)} %get-tuple-element.24), channel_id=1, source_target_pairs={{0,30},{1,3},{2,0},{3,5},{4,2},{5,7},{6,4},{7,9},{8,6},{9,11},{10,... | collective-permute-start | bytes 921608 | tf_op jit(solution)/shard_map/ppermute | solution.py:746
  34.6 49.9 %collective-permute-start.12 = (f32[24,32,128]{2,1,0:T(8,128)S(1)}, f32[24,32,128]{2,1,0:T(8,128)S(1)}, u32[]{:S(2)}, u32[]{:S(2)}) collective-permute-start(f32[24,32,128]{2,1,0:T(8,128)S(1)} %get-tuple-element.25), channel_id=1, source_target_pairs={{0,2},{1,31},{2,4},{3,1},{4,6},{5,3},{6,8},{7,5},{8,10},{9,7},{10,... | collective-permute-start | bytes 1179656 | tf_op jit(solution)/shard_map/ppermute | solution.py:746
  34.6 49.9 %collective-permute-start.13 = (f32[24,32,128]{2,1,0:T(8,128)S(1)}, f32[24,32,128]{2,1,0:T(8,128)S(1)}, u32[]{:S(2)}, u32[]{:S(2)}) collective-permute-start(f32[24,32,128]{2,1,0:T(8,128)S(1)} %get-tuple-element.26), channel_id=1, source_target_pairs={{0,30},{1,3},{2,0},{3,5},{4,2},{5,7},{6,4},{7,9},{8,6},{9,11},{10,... | collective-permute-start | bytes 1179656 | tf_op jit(solution)/shard_map/ppermute | solution.py:746
  77.4 3.1 %collective-permute-start.9 = (f32[16,128]{1,0:T(8,128)S(1)}, f32[16,128]{1,0:T(8,128)S(1)}, u32[]{:S(2)}, u32[]{:S(2)}) collective-permute-start(f32[16,128]{1,0:T(8,128)S(1)} %shard_map.61), channel_id=1, source_target_pairs={{0,1},{1,0},{2,3},{3,2},{4,5},{5,4},{6,7},{7,6},{8,9},{9,8},{10,11... | collective-permute-start | bytes 24584 | tf_op jit(solution)/shard_map/ppermute | solution.py:746
  80.5 14.2 %collective-permute-start.11 = (f32[2,16,128]{2,1,0:T(8,128)S(1)}, f32[2,16,128]{2,1,0:T(8,128)S(1)}, u32[]{:S(2)}, u32[]{:S(2)}) collective-permute-start(f32[2,16,128]{2,1,0:T(8,128)S(1)} %pad_maximum_fusion.1), channel_id=1, source_target_pairs={{0,30},{1,3},{2,0},{3,5},{4,2},{5,7},{6,4},{7,9},{8,6},{9,11},{10,... | collective-permute-start | bytes 49160 | tf_op jit(solution)/shard_map/ppermute | solution.py:746
  84.5 10.2 %collective-permute-start.10 = (f32[2,16,128]{2,1,0:T(8,128)S(1)}, f32[2,16,128]{2,1,0:T(8,128)S(1)}, u32[]{:S(2)}, u32[]{:S(2)}) collective-permute-start(f32[2,16,128]{2,1,0:T(8,128)S(1)} %pad_maximum_fusion.1), channel_id=1, source_target_pairs={{0,2},{1,31},{2,4},{3,1},{4,6},{5,3},{6,8},{7,5},{8,10},{9,7},{10,... | collective-permute-start | bytes 49160 | tf_op jit(solution)/shard_map/ppermute | solution.py:746
  94.7 7.4 %collective-permute-start.15 = (f32[6,16,128]{2,1,0:T(8,128)S(1)}, f32[6,16,128]{2,1,0:T(8,128)S(1)}, u32[]{:S(2)}, u32[]{:S(2)}) collective-permute-start(f32[6,16,128]{2,1,0:T(8,128)S(1)} %pad_maximum_fusion), channel_id=1, source_target_pairs={{0,224},{1,33},{2,226},{3,35},{4,228},{5,37},{6,230},{7,39},{8,232... | collective-permute-start | bytes 147464 | tf_op jit(solution)/shard_map/ppermute | solution.py:746
  96.9 5.3 %collective-permute-start.14 = (f32[6,16,128]{2,1,0:T(8,128)S(1)}, f32[6,16,128]{2,1,0:T(8,128)S(1)}, u32[]{:S(2)}, u32[]{:S(2)}) collective-permute-start(f32[6,16,128]{2,1,0:T(8,128)S(1)} %pad_maximum_fusion), channel_id=1, source_target_pairs={{0,32},{1,225},{2,34},{3,227},{4,36},{5,229},{6,38},{7,231},{8,40}... | collective-permute-start | bytes 147464 | tf_op jit(solution)/shard_map/ppermute | solution.py:746

commit v3 on v2

--- a/solution.py
+++ b/solution.py
@@ -15,6 +15,7 @@
 DAMPING = 0.1
 EPSILON = 1e-06
 BX, BY, BZ = 16, 16, 128
+HALO = 6
 DEEP = 10
 WIN = 30
 WY = 32
@@ -228,46 +229,53 @@
         return jnp.broadcast_to(values[:, j : j + 1], (8, 128))
 
     empty = jnp.zeros((8, 128), F32)
-    for b in range(TILES):
-        in_block = (lane >= 8 * b) & (lane < 8 * b + 8)
-        for chain in chains:
-            pivot = chain[b]
-            own = [column_of(pivot, 8 * b + j) for j in range(8)]
-            for j in range(0, 8, 2):
-                here0, here1 = sub == j, sub == j + 1
-                at0, at1 = lane == 8 * b + j, lane == 8 * b + j + 1
-                p00, p01 = row_of(own[j], j), row_of(own[j + 1], j)
-                p10, p11 = row_of(own[j], j + 1), row_of(own[j + 1], j + 1)
-                scale = pl.reciprocal(p00 * p11 - p01 * p10, approx=True)
-                side0 = jnp.where(here0, -1.0, jnp.where(here1, 0.0, own[j]))
-                side1 = jnp.where(here0, 0.0, jnp.where(here1, -1.0, own[j + 1]))
-                both = here0 | here1
-
-                def step(values, line0, line1):
-                    first = p11 * line0 - p01 * line1
-                    second = p00 * line1 - p10 * line0
-                    return jnp.where(both, 0.0, values) - (side0 * first + side1 * second) * scale
-
-                for n in range(j + 2, 8):
-                    own[n] = step(own[n], row_of(own[n], j), row_of(own[n], j + 1))
-                line0 = jnp.where(at0, 1.0, jnp.where(at1, 0.0, row_of(pivot, j)))
-                line1 = jnp.where(at0, 0.0, jnp.where(at1, 1.0, row_of(pivot, j + 1)))
-                pivot = step(jnp.where(at0 | at1, 0.0, pivot), line0, line1)
-            if b + 1 < TILES:
-                after = jnp.where(in_block, 0.0, chain[b + 1])
-                terms = [column_of(chain[b + 1], 8 * b + j) * row_of(pivot, j) for j in range(8)]
-                while len(terms) > 1:
-                    terms = [p + q for p, q in zip(terms[0::2], terms[1::2])]
-                after = after - terms[0]
-            spread = jnp.concatenate([pivot if r == b else empty for r in range(16)], axis=0)
-            change = dot(jnp.concatenate(chain, axis=0), spread)
+
+    def eliminate(b, tile):
+        own = [column_of(tile, 8 * b + j) for j in range(8)]
+        for j in range(0, 8, 2):
+            here0, here1 = sub == j, sub == j + 1
+            at0, at1 = lane == 8 * b + j, lane == 8 * b + j + 1
+            p00, p01 = row_of(own[j], j), row_of(own[j + 1], j)
+            p10, p11 = row_of(own[j], j + 1), row_of(own[j + 1], j + 1)
+            scale = pl.reciprocal(p00 * p11 - p01 * p10, approx=True)
+            side0 = jnp.where(here0, -1.0, jnp.where(here1, 0.0, own[j]))
+            side1 = jnp.where(here0, 0.0, jnp.where(here1, -1.0, own[j + 1]))
+            both = here0 | here1
+
+            def step(values, line0, line1):
+                first = p11 * line0 - p01 * line1
+                second = p00 * line1 - p10 * line0
+                return jnp.where(both, 0.0, values) - (side0 * first + side1 * second) * scale
+
+            for n in range(j + 2, 8):
+                own[n] = step(own[n], row_of(own[n], j), row_of(own[n], j + 1))
+            line0 = jnp.where(at0, 1.0, jnp.where(at1, 0.0, row_of(tile, j)))
+            line1 = jnp.where(at0, 0.0, jnp.where(at1, 1.0, row_of(tile, j + 1)))
+            tile = step(jnp.where(at0 | at1, 0.0, tile), line0, line1)
+        return tile
+
+    def reduced(b, tile, pivot):
+        terms = [column_of(tile, 8 * b + j) * row_of(pivot, j) for j in range(8)]
+        while len(terms) > 1:
+            terms = [p + q for p, q in zip(terms[0::2], terms[1::2])]
+        return jnp.where((lane >= 8 * b) & (lane < 8 * b + 8), 0.0, tile) - terms[0]
+
+    for first in range(0, TILES, 2):
+        blocks = [b for b in (first, first + 1) if b < TILES]
+        in_blocks = (lane >= 8 * first) & (lane < 8 * first + 8 * len(blocks))
+        before = [list(chain) for chain in chains]
+        for b in blocks:
+            for chain in chains:
+                chain[b] = eliminate(b, chain[b])
+                for i in range(first, min(first + 4, TILES)):
+                    if i != b:
+                        chain[i] = reduced(b, chain[i], chain[b])
+        for chain, old in zip(chains, before):
+            spread = jnp.concatenate([chain[r] if r in blocks else empty for r in range(16)], axis=0)
+            change = dot(jnp.concatenate(old, axis=0), spread)
             for i in range(TILES):
-                if i == b:
-                    chain[i] = pivot
-                elif i == b + 1:
-                    chain[i] = after
-                else:
-                    chain[i] = jnp.where(in_block, 0.0, chain[i]) - change[8 * i : 8 * i + 8]
+                if not first <= i < first + 4:
+                    chain[i] = jnp.where(in_blocks, 0.0, old[i]) - change[8 * i : 8 * i + 8]
     return chains
 
 
@@ -326,7 +334,7 @@
         cy[i] = 0.5 * (here + row_roll(here, -1))
         cz[i] = 0.5 * (here + lane_roll(here, -1))
 
-    loop(0, WIN, faces, 10)
+    loop(0, WIN, faces, 15)
 
     def scale(i):
         total = MASS_TERM + cx[i] + cx[i - 1] + cy[i] + row_roll(cy[i], 1) + cz[i] + lane_roll(cz[i], 1)
@@ -334,7 +342,7 @@
         good = inside & (gx >= 0) & (gx < nx)
         iv[i] = jnp.where(good, 1.0 / total, 0.0)
 
-    loop(1, WIN - 1, scale, 7)
+    loop(1, WIN - 1, scale, 14)
 
     for sweep in range(FSWEEPS):
         src, dst = (ua, ub) if sweep % 2 == 0 else (ub, ua)
@@ -346,7 +354,7 @@
             total = total + cz[i] * lane_roll(here, -1) + lane_roll(cz[i] * here, 1)
             dst[i] = total * iv[i]
 
-        loop(sweep + 1, WIN - 1 - sweep, relax, WIN)
+        loop(sweep + 1, WIN - 1 - sweep, relax, WIN - 2 - 2 * sweep)
 
     line = iota((128, 384), 0)
     column = iota((128, 384), 1)
@@ -403,7 +411,7 @@
                 piece = tall[n * WY : (n + 1) * WY, 128 * k : 128 * k + 128] * pick_y
                 rows[n, k, pl.ds(a, 1), :] = jnp.sum(piece, axis=0, keepdims=True)
 
-    loop(0, PC, layer, 2)
+    loop(0, PC, layer, 5)
 
     lane16 = iota((16, 128), 1)
     row16 = iota((16, 128), 0)
@@ -565,21 +573,33 @@
     out[PC:16, :] = corner
 
 
-def field_kernel(sizes, sc, u, f, m, x1, x2, strip, strip1, strip2, s1, s2, out, ua, ub, fo, mo, cx, cy, cz, iv):
+def field_kernel(
+    sizes, sc, u, f, m, x1, x2, strip, strip1, strip2, s1, s2, out,
+    ua, ub, fo, mo, cx, cy, zu, zd, ze, iv, ba, bb, bf, bm, bx, by, bz, bi,
+):
     nx, ny, nz = sizes
     low_first = sc[0] == 0
     sub = iota((8, 128), 0)
     lane = iota((AX, 128), 1)
+    group = lax.shift_right_arithmetic(lane, 5)
+    inner = lane & 31
     lead = DEEP - FSWEEPS
-    spot = jnp.where(low_first, 0, BZ - DEEP)
-    strip_lanes = (lane >= spot) & (lane < spot + DEEP)
-
+    w0 = jnp.where(low_first, BZ - 8, -8)
+    zoff = jnp.where(low_first, BZ, -DEEP)
+    z = inner + w0
+    main_ok = (z >= 0) & (z < BZ)
+    far_ok = (z >= zoff) & (z < zoff + DEEP)
+    edge_lane = jnp.where(low_first, BZ - 1, 0)
+    edge_from = jnp.where(low_first, 8, 7)
+    at_edge = lane == edge_lane
     row24 = iota((AX, 128), 0)
-    inside24 = (sc[14] - FSWEEPS + row24 >= 0) & (sc[14] - FSWEEPS + row24 < ny)
+    gy = sc[14] - FSWEEPS + row24
+    inside = (gy >= 0) & (gy < ny)
 
     def build(dest, values16):
         gx = sc[13] - FSWEEPS + dest
-        good = inside24 & (gx >= 0) & (gx < nx)
+        good = inside & (gx >= 0) & (gx < nx)
+        every = []
         for q in range(8):
             j = q // 2
             a = s1[dest, 8 * j : 8 * j + 8]
@@ -593,19 +613,28 @@
             tall = jnp.concatenate(
                 [jnp.where(sub < 4, low, t0), jnp.where(sub < 4, t0, t1), jnp.where(sub < 4, t1, high)], axis=0
             )
-            tall = jnp.where(good, tall, 0.0)
-            if q < 7:
-                ref = ua.at[q] if q < 3 else (fo.at[q - 3] if q < 6 else mo)
-                ref[dest, :, 0:128] = tall
-            else:
-                for c in range(7):
-                    ref = ua.at[c] if c < 3 else (fo.at[c - 3] if c < 6 else mo)
-                    ref[dest, :, 128:256] = jnp.where(strip_lanes, lane_roll(tall, spot - DEEP * c), 0.0)
+            every.append(jnp.where(good, tall, 0.0))
+        for k in range(3):
+            ua[k, dest] = every[k]
+            fo[k, dest] = every[3 + k]
+        mo[dest] = every[6]
+        side = []
+        for channels in ((0, 1, 2), (3, 4, 5)):
+            main, far = jnp.zeros((AX, 128), F32), jnp.zeros((AX, 128), F32)
+            for k, c in enumerate(channels):
+                main = jnp.where(group == k, lane_roll(every[c], 32 * k - w0), main)
+                far = jnp.where(group == k, lane_roll(every[7], 32 * k + zoff - w0 - DEEP * c), far)
+            side.append(jnp.where(main_ok, main, jnp.where(far_ok, far, 0.0)))
+        ba[dest], bf[dest] = side
+        main = jnp.where(main_ok, lane_roll(every[6], -w0), jnp.where(far_ok, lane_roll(every[7], zoff - w0 - DEEP * 6), 0.0))
+        first = jnp.where(group == 0, main, 0.0)
+        first = jnp.where(group == 1, lane_roll(main, 32), first)
+        bm[dest] = jnp.where(group == 2, lane_roll(main, 64), first)
 
     def inner_plane(i):
         build(i + FSWEEPS, [u[k, i] for k in range(3)] + [f[k, i] for k in range(3)] + [m[i], strip[i]])
 
-    loop(0, BX, inner_plane, 2)
+    loop(0, BX, inner_plane, 4)
 
     def outer_plane(i):
         for a, b, sa, sb, start, dest in (
@@ -624,45 +653,59 @@
                 + [pick(PLANES - DEEP + j), jnp.where(low_first, sa[j], sb[j])],
             )
 
-    loop(0, FSWEEPS, outer_plane, 1)
-
-    row = iota((AX, 256), 0)
-    wide = iota((AX, 256), 1)
-    gy = sc[14] - FSWEEPS + row
-    second = (wide >= 128 + spot) & (wide < 128 + spot + DEEP)
-    inside = (gy >= 0) & (gy < ny) & ((wide < 128) | second)
+    loop(0, FSWEEPS, outer_plane, 2)
+
+    def edge(values, k):
+        return jnp.where(at_edge, lane_roll(values, edge_lane - edge_from - 32 * k), 0.0)
 
     def faces(i):
-        here = mo[i]
+        here, there = mo[i], bm[i]
         cx[i] = 0.5 * (here + mo[jnp.minimum(i + 1, AX - 1)])
+        bx[i] = 0.5 * (there + bm[jnp.minimum(i + 1, AX - 1)])
         cy[i] = 0.5 * (here + row_roll(here, -1))
-        cz[i] = 0.5 * (here + lane_roll(here, -1))
-
-    loop(0, AX, faces, 4)
+        by[i] = 0.5 * (there + row_roll(there, -1))
+        bz[i] = 0.5 * (there + lane_roll(there, -1))
+        zu[i] = jnp.where(lane == BZ - 1, 0.0, 0.5 * (here + lane_roll(here, -1)))
+        zd[i] = jnp.where(lane == 0, 0.0, 0.5 * (here + lane_roll(here, 1)))
+        ze[i] = jnp.where(at_edge, 0.5 * (here + edge(there, 0)), 0.0)
+
+    loop(0, AX, faces, 12)
+    side_inside = (sc[15] + z >= 0) & (sc[15] + z < nz)
+    far_edge = BZ - 1 - edge_lane
 
     def scale(i):
-        total = MASS_TERM + cx[i] + cx[i - 1] + cy[i] + row_roll(cy[i], 1) + cz[i] + lane_roll(cz[i], 1)
+        open_face = jnp.where(lane == far_edge, 0.5 * mo[i], 0.0)
+        total = MASS_TERM + cx[i] + cx[i - 1] + cy[i] + row_roll(cy[i], 1) + zu[i] + zd[i] + ze[i] + open_face
         gx = sc[13] - FSWEEPS + i
         good = inside & (gx >= 0) & (gx < nx)
         iv[i] = jnp.where(good, 1.0 / total, 0.0)
-
-    loop(1, AX - 1, scale, 2)
+        total = MASS_TERM + bx[i] + bx[i - 1] + by[i] + row_roll(by[i], 1) + bz[i] + lane_roll(bz[i], 1)
+        bi[i] = jnp.where(good & side_inside, 1.0 / total, 0.0)
+
+    loop(1, AX - 1, scale, 11)
     for sweep in range(FSWEEPS):
         src, dst = (ua, ub) if sweep % 2 == 0 else (ub, ua)
-
-        def relax(i, src=src, dst=dst, last=sweep == FSWEEPS - 1):
+        bsrc, bdst = (ba, bb) if sweep % 2 == 0 else (bb, ba)
+
+        def relax(i, src=src, dst=dst, bsrc=bsrc, bdst=bdst, last=sweep == FSWEEPS - 1):
+            there = bsrc[i]
             for k in range(3):
                 here = src[k, i]
                 total = fo[k, i] + cx[i] * src[k, i + 1] + cx[i - 1] * src[k, i - 1]
                 total = total + cy[i] * row_roll(here, -1) + row_roll(cy[i] * here, 1)
-                total = total + cz[i] * lane_roll(here, -1) + lane_roll(cz[i] * here, 1)
+                total = total + zu[i] * lane_roll(here, -1) + zd[i] * lane_roll(here, 1) + ze[i] * edge(there, k)
                 total = total * iv[i]
                 if last:
-                    out[k, i - FSWEEPS] = row_roll(total[:, 0:128], -FSWEEPS)[0:BY]
+                    out[k, i - FSWEEPS] = row_roll(total, -FSWEEPS)[0:BY]
                 else:
                     dst[k, i] = total
-
-        loop(sweep + 1, AX - 1 - sweep, relax, 2)
+            if not last:
+                total = bf[i] + bx[i] * bsrc[i + 1] + bx[i - 1] * bsrc[i - 1]
+                total = total + by[i] * row_roll(there, -1) + row_roll(by[i] * there, 1)
+                total = total + bz[i] * lane_roll(there, -1) + lane_roll(bz[i] * there, 1)
+                bdst[i] = total * bi[i]
+
+        loop(sweep + 1, AX - 1 - sweep, relax, AX - 2 - 2 * sweep)
 
 
 def taper(offset):
@@ -673,42 +716,53 @@
     return total
 
 
-def final_kernel(sc, m, parts, out, acc):
-    number = parts.shape[0]
-    row16 = iota((16, 128), 0).astype(F32)
+def contribution(sc, delta, start, planes):
+    rows = 16 if planes > 8 else 8
+    laneix = iota((rows, 128), 1)
     lane16i = iota((16, 128), 1)
-    lane16 = lane16i.astype(F32)
     lane_y = div10(lane16i).astype(F32)
     rows128 = iota((128, 128), 0)
-    rows_y = div10(rows128)
-    rows_z = (rows128 - PC * rows_y).astype(F32)
-    lanes128 = iota((128, 128), 1).astype(F32)
+    rows_z = (rows128 - PC * div10(rows128)).astype(F32)
+
+    def place(axis):
+        return delta[PC : PC + 1, axis : axis + 1] - sc[13 + axis].astype(F32)
+
+    off_x = (iota((rows, 128), 0) + start).astype(F32) - place(0)
+    apart = off_x - 2.0 * laneix.astype(F32)
+    choose = jnp.where((apart >= 0.0) & (apart < 2.0) & (laneix < PC), 1.0, 0.0).astype(BF16)[:, 0:16]
+    picked = [lax.dot_general(choose, p, (((1,), (0,)), ((), ())), preferred_element_type=F32) for p in three_parts(delta)]
+    lines = (picked[0] + picked[1] + picked[2]) * taper(off_x)
+    off_y = iota((16, 128), 0).astype(F32) - place(1)
+    apart = off_y - 2.0 * lane_y
+    cover = jnp.where((apart >= 0.0) & (apart < 2.0) & (lane16i < PC * PC), taper(off_y), 0.0)
+    off_z = iota((128, 128), 1).astype(F32) - place(2)
+    apart = off_z - 2.0 * rows_z
+    expand = jnp.where((apart >= 0.0) & (apart < 2.0) & (rows128 < PC * PC), 1.0, 0.0).astype(BF16)
+    tall = jnp.concatenate([jnp.broadcast_to(lines[x : x + 1, :], (BY, 128)) * cover for x in range(planes)], axis=0)
+    return dot_exact(tall, expand) * taper(off_z[0:1, :])
+
+
+def near_kernel(sc, parts, acc):
     acc[...] = jnp.zeros(acc.shape, F32)
 
     def add(n):
-        delta = parts[n]
-
-        def place(axis, low):
-            return delta[PC : PC + 1, axis : axis + 1] - low.astype(F32)
-
-        cx, cy, cz = place(0, sc[13]), place(1, sc[14]), place(2, sc[15])
-        off_x = row16 - cx
-        apart = off_x - 2.0 * lane16
-        choose = jnp.where((apart >= 0.0) & (apart < 2.0) & (lane16i < PC), 1.0, 0.0).astype(BF16)[:, 0:16]
-        picked = [
-            lax.dot_general(choose, p, (((1,), (0,)), ((), ())), preferred_element_type=F32) for p in three_parts(delta)
-        ]
-        lines = (picked[0] + picked[1] + picked[2]) * taper(off_x)
-        off_y = row16 - cy
-        apart = off_y - 2.0 * lane_y
-        cover = jnp.where((apart >= 0.0) & (apart < 2.0) & (lane16i < PC * PC), taper(off_y), 0.0)
-        off_z = lanes128 - cz
-        apart = off_z - 2.0 * rows_z
-        expand = jnp.where((apart >= 0.0) & (apart < 2.0) & (rows128 < PC * PC), 1.0, 0.0).astype(BF16)
-        tall = jnp.concatenate([jnp.broadcast_to(lines[x : x + 1, :], (BY, 128)) * cover for x in range(BX)], axis=0)
-        acc[...] += dot_exact(tall, expand) * taper(off_z[0:1, :])
-
-    loop(0, number, add, 3)
+        acc[...] += contribution(sc, parts[n], 0, BX)
+
+    loop(0, parts.shape[0], add, 3)
+
+
+def final_kernel(sc, m, near, parts1, parts2, out, acc):
+    acc[...] = near[...]
+    reach = HALO - 1
+    start1 = jnp.where(sc[0] == 0, 0, BX - reach)
+    start2 = BX - reach - start1
+
+    def add(n):
+        for parts, start in ((parts1, start1), (parts2, start2)):
+            where = pl.ds(pl.multiple_of(start * BY, BY), reach * BY)
+            acc[where, :] += contribution(sc, parts[n], start, reach)
+
+    loop(0, parts1.shape[0], add, 3)
     for x in range(BX):
         out[x] = m[x] * (1.0 + acc[16 * x : 16 * x + 16, :])
 
@@ -761,7 +815,7 @@
         [(3, BX, BY, BZ), (3, BX, BY, BZ), (BX, BY, BZ), pltpu.SemaphoreType.DMA((3,))],
         [first, start_field, forcing, modulus],
         1 << 20,
-        pl.ANY,
+        pltpu.HBM,
     )
     x1 = send(msg1, lambda x, y, z: (x + turn(z), y, z))
     x2 = send(msg2, lambda x, y, z: (x - turn(z), y, z))
@@ -794,11 +848,11 @@
     plane = jnp.stack([delta, send(delta, lambda x, y, z: (x, y, 1 - z))])
     right = send(plane, lambda x, y, z: (x, y + turn(z), z))
     left = send(plane, lambda x, y, z: (x, y - turn(z), z))
-    wide = (AX, AX, 256)
+    wide = (AX, AX, 128)
     displacement = call(
         functools.partial(field_kernel, sizes),
         (3, BX, BY, BZ),
-        [(3,) + wide] * 3 + [wide] * 5,
+        [(3,) + wide] * 3 + [wide] * 15,
         [scalar, start_field, forcing, modulus, x1, x2, far_strip, far1, far2, b1, b2],
         1 << 30,
     )
@@ -806,12 +860,10 @@
     plane = jnp.concatenate([plane, right, left])
     after = send(plane, lambda x, y, z: (x + turn(z), y, z))
     before = send(plane, lambda x, y, z: (x - turn(z), y, z))
+    near = call(near_kernel, (BX * BY, 128), [], [scalar, plane], 1 << 29)
+    near, after, before = lax.optimization_barrier((near, after, before))
     new_modulus = call(
-        final_kernel,
-        (BX, BY, BZ),
-        [(BX * BY, 128)],
-        [scalar, modulus, jnp.concatenate([plane, after, before])],
-        1 << 24,
+        final_kernel, (BX, BY, BZ), [(BX * BY, 128)], [scalar, modulus, near, after, before], 1 << 24
     )
     return displacement, new_modulus
 

time: 110 us -> 103 us (0.936)
  the two profiles are of different devices: /device:TPU:0 before, /device:TPU:1 now
where the time goes in v3:
time: 103 us
  Pallas kernels  52.6 us (51%)
  starting transfers between devices  33 us (32%)
  waiting for transfers between devices  11.7 us (11%)
  local copies, waits for them, and re-layouts  4.79 us (5%)
    pallas_call x6, Pallas kernels, call(): pl.pallas_call(kernel, out_shape=outs, in_specs=specs, out_specs=[pl.Bloc...  52.6 us
    ppermute x16, starting transfers between devices, send(): return lax.ppermute(values, AXES, pairs)  33 us
    ppermute x16, waiting for transfers between devices, send(): return lax.ppermute(values, AXES, pairs)  11.7 us
    unnamed x16, local copies, waits for them, and re-layouts  4.09 us
  transfers between devices with their start and end apart: 16, of which 5 were waited for; matrix products, arithmetic and copies ran while one was open for 1% of the time, Pallas kernels for 42%

profile of v3, /device:TPU:1, one launch (start us, length us, event | category | flops | bytes accessed | tf_op | source)
XLA Modules:
  0.0 103.0 jit_solution(2507095738225915482)
XLA Ops:
  0.6 0.0 copy-start
  0.6 1.0 copy-done
  1.6 0.0 copy-start.2
  1.6 1.0 copy-done.2
  2.6 0.0 copy-start.4
  2.6 0.9 copy-done.4
  3.5 0.0 copy-start.1
  3.5 0.0 copy-start.3
  3.5 0.0 copy-start.5
  3.5 1.7 %shard_map.59 = (f32[67,16,128]{2,1,0:T(8,128)S(1)}, f32[67,16,128]{2,1,0:T(8,128)S(1)}, f32[16,16,128]{2,1,0:T(8,128)S(1)}, f32[10,16,128]{2,1,0:T(8,128)}, f32[10,16,128]{2,1,0:T(8,128)}) custom-call(s32[1]{0:T(128)} %bitcast.sc, f32[3,16,16,128]{3,2,1,0:T(8,128)S(1)} %copy-done, f32[3,16,16,128]{3,2,1,0:T(8,128)S(1)} %copy-done.2, ...), custom_call_target="tpu_custom_call" | custom-call | flops 1048576 | bytes 1048576 | tf_op jit(solution)/shard_map/pallas_call | solution.py:774
  5.2 6.5 %collective-permute-start.2 = (f32[67,16,128]{2,1,0:T(8,128)S(1)}, f32[67,16,128]{2,1,0:T(8,128)S(1)}, u32[]{:S(2)}, u32[]{:S(2)}) collective-permute-start(f32[67,16,128]{2,1,0:T(8,128)S(1)} %get-tuple-element.19), channel_id=1, source_target_pairs={{0,32},{1,225},{2,34},{3,227},{4,36},{5,229},{6,38},{7,231},{8,40}... | collective-permute-start | bytes 1646600 | tf_op jit(solution)/shard_map/ppermute | solution.py:800
  11.7 0.0 collective-permute-start.3
  11.7 0.0 copy-start.6
  11.7 0.7 copy-done.6
  12.4 0.1 add_subtract_fusion.1
  12.4 4.9 %collective-permute-start.1 = (s32[1,3]{1,0:T(1,128)S(1)}, s32[1,3]{1,0:T(1,128)S(1)}, u32[]{:S(2)}, u32[]{:S(2)}) collective-permute-start(s32[1,3]{1,0:T(1,128)S(1)} %add_subtract_fusion.1), channel_id=1, source_target_pairs={{0,2},{1,31},{2,4},{3,1},{4,6},{5,3},{6,8},{7,5},{8,10},{9,7},{10,... | collective-permute-start | bytes 44 | tf_op jit(solution)/shard_map/ppermute | solution.py:800
  17.4 0.0 collective-permute-start
  17.4 3.0 %collective-permute-start.5 = (f32[10,16,128]{2,1,0:T(8,128)}, f32[10,16,128]{2,1,0:T(8,128)S(1)}, u32[]{:S(2)}, u32[]{:S(2)}) collective-permute-start(f32[10,16,128]{2,1,0:T(8,128)} %get-tuple-element.22), channel_id=1, source_target_pairs={{0,33},{1,224},{2,35},{3,226},{4,37},{5,228},{6,39},{7,230},{8,41}... | collective-permute-start | bytes 245768 | tf_op jit(solution)/shard_map/ppermute | solution.py:800
  20.4 0.0 collective-permute-done.1
  20.4 0.0 collective-permute-start.6
  20.4 2.7 %collective-permute-done = s32[1,3]{1,0:T(1,128)S(1)} collective-permute-done((s32[1,3]{1,0:T(1,128)S(1)}, s32[1,3]{1,0:T(1,128)S(1)}, u32[]{:S(2)}, u32[]{:S(2)}) %collective-permute-start) | collective-permute-done | bytes 44 | tf_op jit(solution)/shard_map/ppermute | solution.py:800
  23.1 0.0 copy-start.7
  23.1 0.5 copy-done.7
  23.6 0.0 collective-permute-start.4
  23.6 0.1 add_subtract_fusion
  23.7 0.7 concatenate.9.sc
  24.4 0.7 collective-permute-done.5.strip1
  25.2 0.0 collective-permute-done.6.strip2
  25.2 0.0 collective-permute-done.4.strip
  25.2 0.0 collective-permute-done.2.x1
  25.2 1.0 collective-permute-done.3.x2
  26.2 0.0 copy-done.1
  26.2 0.0 copy-done.3
  26.2 0.0 copy-done.5
  26.2 4.6 %shard_map.60 = (f32[30,16,128]{2,1,0:T(8,128)S(1)}, f32[30,16,128]{2,1,0:T(8,128)S(1)}, f32[15,40,128]{2,1,0:T(8,128)S(1)}, f32[15,40,128]{2,1,0:T(8,128)S(1)},...) custom-call(s32[16]{0:T(128)S(1)} %concatenate.9.sc, f32[3,16,16,128]{3,2,1,0:T(8,128)S(1)} %copy-done.1, ...), custom_call_target="tpu_custom_call" | custom-call | flops 4194304 | bytes 1048576 | tf_op jit(solution)/shard_map/pallas_call | solution.py:774
  30.8 5.0 %collective-permute-start.7 = (f32[15,40,128]{2,1,0:T(8,128)S(1)}, f32[15,40,128]{2,1,0:T(8,128)S(1)}, u32[]{:S(2)}, u32[]{:S(2)}) collective-permute-start(f32[15,40,128]{2,1,0:T(8,128)S(1)} %get-tuple-element.26), channel_id=1, source_target_pairs={{0,2},{1,31},{2,4},{3,1},{4,6},{5,3},{6,8},{7,5},{8,10},{9,7},{10,... | collective-permute-start | bytes 921608 | tf_op jit(solution)/shard_map/ppermute | solution.py:800
  35.8 0.0 collective-permute-start.8
  35.8 4.8 %collective-permute-start.12 = (f32[24,32,128]{2,1,0:T(8,128)S(1)}, f32[24,32,128]{2,1,0:T(8,128)S(1)}, u32[]{:S(2)}, u32[]{:S(2)}) collective-permute-start(f32[24,32,128]{2,1,0:T(8,128)S(1)} %get-tuple-element.28), channel_id=1, source_target_pairs={{0,2},{1,31},{2,4},{3,1},{4,6},{5,3},{6,8},{7,5},{8,10},{9,7},{10,... | collective-permute-start | bytes 1179656 | tf_op jit(solution)/shard_map/ppermute | solution.py:800
  40.6 0.0 collective-permute-start.13
  40.6 0.0 collective-permute-done.7.r1
  40.7 6.1 %collective-permute-done.8.r2 = f32[15,40,128]{2,1,0:T(8,128)S(1)} collective-permute-done((f32[15,40,128]{2,1,0:T(8,128)S(1)}, f32[15,40,128]{2,1,0:T(8,128)S(1)}, u32[]{:S(2)}, u32[]{:S(2)}) %collective-permute-start.8) | collective-permute-done | bytes 307232 | tf_op jit(solution)/shard_map/ppermute | solution.py:800
  46.7 33.8 %shard_map.61 = f32[16,128]{1,0:T(8,128)S(1)} custom-call(s32[16]{0:T(128)S(1)} %concatenate.9.sc, f32[30,16,128]{2,1,0:T(8,128)S(1)} %get-tuple-element.24.own_u, f32[30,16,128]{2,1,0:T(8,128)S(1)} %get-tuple-element.25.own_f, f32[15,40,128]{2,1,0:T(8,128)S(1)} %collective-permute-done.7.r1, f32[15,40,128]{2,1,0:T(8,128)S(1)} %collective-permute-done.8.r2), custom_call_target="tpu_custom_call" | custom-call | flops 8589934592 | bytes 1048576 | tf_op jit(solution)/shard_map/pallas_call | solution.py:774
  80.5 0.1 collective-permute-start.9
  80.6 1.2 %collective-permute-done.9 = f32[16,128]{1,0:T(8,128)S(1)} collective-permute-done((f32[16,128]{1,0:T(8,128)S(1)}, f32[16,128]{1,0:T(8,128)S(1)}, u32[]{:S(2)}, u32[]{:S(2)}) %collective-permute-start.9) | collective-permute-done | bytes 8224 | tf_op jit(solution)/shard_map/ppermute | solution.py:800
  81.8 0.0 collective-permute-start.11
  81.8 4.8 %collective-permute-start.10 = (f32[2,16,128]{2,1,0:T(8,128)S(1)}, f32[2,16,128]{2,1,0:T(8,128)S(1)}, u32[]{:S(2)}, u32[]{:S(2)}) collective-permute-start(f32[2,16,128]{2,1,0:T(8,128)S(1)} %pad_maximum_fusion.1), channel_id=1, source_target_pairs={{0,2},{1,31},{2,4},{3,1},{4,6},{5,3},{6,8},{7,5},{8,10},{9,7},{10,... | collective-permute-start | bytes 49160 | tf_op jit(solution)/shard_map/ppermute | solution.py:800
  86.6 0.0 collective-permute-done.12.s1
  86.6 0.0 collective-permute-done.13.s2
  86.6 7.7 %shard_map.62 = f32[3,16,16,128]{3,2,1,0:T(8,128)} custom-call(s32[16]{0:T(128)S(1)} %concatenate.9.sc, f32[3,16,16,128]{3,2,1,0:T(8,128)S(1)} %copy-done.1, f32[3,16,16,128]{3,2,1,0:T(8,128)S(1)} %copy-done.3, f32[16,16,128]{2,1,0:T(8,128)S(1)} %copy-done.5, f32[67,16,128]{2,1,0:T(8,128)S(1)} %collective-permute-done.2.x1, ...), custom_call_target="tpu_custom_call" | custom-call | flops 1073741824 | bytes 1048576 | tf_op jit(solution)/shard_map/pallas_call | solution.py:774
  94.3 0.0 collective-permute-done.11
  94.3 0.0 collective-permute-done.10
  94.3 0.1 collective-permute-start.15
  94.4 3.8 %collective-permute-start.14 = (f32[6,16,128]{2,1,0:T(8,128)S(1)}, f32[6,16,128]{2,1,0:T(8,128)S(1)}, u32[]{:S(2)}, u32[]{:S(2)}) collective-permute-start(f32[6,16,128]{2,1,0:T(8,128)S(1)} %pad_maximum_fusion.parts), channel_id=1, source_target_pairs={{0,32},{1,225},{2,34},{3,227},{4,36},{5,229},{6,38},{7,231},{8,40}... | collective-permute-start | bytes 147464 | tf_op jit(solution)/shard_map/ppermute | solution.py:800
  98.1 2.0 %shard_map.63.near = f32[256,128]{1,0:T(8,128)S(1)} custom-call(s32[16]{0:T(128)S(1)} %concatenate.9.sc, f32[6,16,128]{2,1,0:T(8,128)S(1)} %pad_maximum_fusion.parts), custom_call_target="tpu_custom_call" | custom-call | flops 536870912 | bytes 1048576 | tf_op jit(solution)/shard_map/pallas_call | solution.py:774
  100.1 0.0 collective-permute-done.15.parts2
  100.1 0.0 collective-permute-done.14.parts1
  100.1 2.8 %shard_map.64 = f32[16,16,128]{2,1,0:T(8,128)} custom-call(s32[16]{0:T(128)S(1)} %concatenate.9.sc, f32[16,16,128]{2,1,0:T(8,128)S(1)} %copy-done.5, f32[256,128]{1,0:T(8,128)S(1)} %shard_map.63.near, f32[6,16,128]{2,1,0:T(8,128)S(1)} %collective-permute-done.14.parts1, f32[6,16,128]{2,1,0:T(8,128)S(1)} %collective-permute-done.15.parts2), custom_call_target="tpu_custom_call" | custom-call | flops 16777216 | bytes 1048576 | tf_op jit(solution)/shard_map/pallas_call | solution.py:774
  (2 shorter events, 0.0 us)
Async XLA Ops:
  0.6 1.0 copy-start
  1.6 1.0 copy-start.2
  2.6 0.9 copy-start.4
  3.5 22.6 %copy-start.1 = (f32[3,16,16,128]{3,2,1,0:T(8,128)S(1)}, f32[3,16,16,128]{3,2,1,0:T(8,128)}, u32[]{:S(2)}) copy-start(f32[3,16,16,128]{3,2,1,0:T(8,128)} %u.5) | copy-start | bytes 1179652
  3.5 22.6 %copy-start.3 = (f32[3,16,16,128]{3,2,1,0:T(8,128)S(1)}, f32[3,16,16,128]{3,2,1,0:T(8,128)}, u32[]{:S(2)}) copy-start(f32[3,16,16,128]{3,2,1,0:T(8,128)} %f.5) | copy-start | bytes 1179652
  3.5 22.6 %copy-start.5 = (f32[16,16,128]{2,1,0:T(8,128)S(1)}, f32[16,16,128]{2,1,0:T(8,128)}, u32[]{:S(2)}) copy-start(f32[16,16,128]{2,1,0:T(8,128)} %m.7) | copy-start | bytes 393220
  5.2 19.9 %collective-permute-start.2 = (f32[67,16,128]{2,1,0:T(8,128)S(1)}, f32[67,16,128]{2,1,0:T(8,128)S(1)}, u32[]{:S(2)}, u32[]{:S(2)}) collective-permute-start(f32[67,16,128]{2,1,0:T(8,128)S(1)} %get-tuple-element.19), channel_id=1, source_target_pairs={{0,32},{1,225},{2,34},{3,227},{4,36},{5,229},{6,38},{7,231},{8,40}... | collective-permute-start | bytes 1646600 | tf_op jit(solution)/shard_map/ppermute | solution.py:800
  11.7 14.4 %collective-permute-start.3 = (f32[67,16,128]{2,1,0:T(8,128)S(1)}, f32[67,16,128]{2,1,0:T(8,128)S(1)}, u32[]{:S(2)}, u32[]{:S(2)}) collective-permute-start(f32[67,16,128]{2,1,0:T(8,128)S(1)} %get-tuple-element.20), channel_id=1, source_target_pairs={{0,224},{1,33},{2,226},{3,35},{4,228},{5,37},{6,230},{7,39},{8,232... | collective-permute-start | bytes 1646600 | tf_op jit(solution)/shard_map/ppermute | solution.py:800
  11.7 0.7 copy-start.6
  12.4 7.9 %collective-permute-start.1 = (s32[1,3]{1,0:T(1,128)S(1)}, s32[1,3]{1,0:T(1,128)S(1)}, u32[]{:S(2)}, u32[]{:S(2)}) collective-permute-start(s32[1,3]{1,0:T(1,128)S(1)} %add_subtract_fusion.1), channel_id=1, source_target_pairs={{0,2},{1,31},{2,4},{3,1},{4,6},{5,3},{6,8},{7,5},{8,10},{9,7},{10,... | collective-permute-start | bytes 44 | tf_op jit(solution)/shard_map/ppermute | solution.py:800
  17.4 5.7 %collective-permute-start = (s32[1,3]{1,0:T(1,128)S(1)}, s32[1,3]{1,0:T(1,128)S(1)}, u32[]{:S(2)}, u32[]{:S(2)}) collective-permute-start(s32[1,3]{1,0:T(1,128)S(1)} %add_subtract_fusion.1), channel_id=1, source_target_pairs={{0,30},{1,3},{2,0},{3,5},{4,2},{5,7},{6,4},{7,9},{8,6},{9,11},{10,... | collective-permute-start | bytes 44 | tf_op jit(solution)/shard_map/ppermute | solution.py:800
  17.4 7.8 %collective-permute-start.5 = (f32[10,16,128]{2,1,0:T(8,128)}, f32[10,16,128]{2,1,0:T(8,128)S(1)}, u32[]{:S(2)}, u32[]{:S(2)}) collective-permute-start(f32[10,16,128]{2,1,0:T(8,128)} %get-tuple-element.22), channel_id=1, source_target_pairs={{0,33},{1,224},{2,35},{3,226},{4,37},{5,228},{6,39},{7,230},{8,41}... | collective-permute-start | bytes 245768 | tf_op jit(solution)/shard_map/ppermute | solution.py:800
  20.4 4.8 %collective-permute-start.6 = (f32[10,16,128]{2,1,0:T(8,128)}, f32[10,16,128]{2,1,0:T(8,128)S(1)}, u32[]{:S(2)}, u32[]{:S(2)}) collective-permute-start(f32[10,16,128]{2,1,0:T(8,128)} %get-tuple-element.23), channel_id=1, source_target_pairs={{0,225},{1,32},{2,227},{3,34},{4,229},{5,36},{6,231},{7,38},{8,233... | collective-permute-start | bytes 245768 | tf_op jit(solution)/shard_map/ppermute | solution.py:800
  23.1 0.5 copy-start.7
  23.6 1.5 %collective-permute-start.4 = (f32[16,16,128]{2,1,0:T(8,128)S(1)}, f32[16,16,128]{2,1,0:T(8,128)S(1)}, u32[]{:S(2)}, u32[]{:S(2)}) collective-permute-start(f32[16,16,128]{2,1,0:T(8,128)S(1)} %get-tuple-element.21), channel_id=1, source_target_pairs={{0,1},{1,0},{2,3},{3,2},{4,5},{5,4},{6,7},{7,6},{8,9},{9,8},{10,11... | collective-permute-start | bytes 393224 | tf_op jit(solution)/shard_map/ppermute | solution.py:800
  30.8 9.8 %collective-permute-start.7 = (f32[15,40,128]{2,1,0:T(8,128)S(1)}, f32[15,40,128]{2,1,0:T(8,128)S(1)}, u32[]{:S(2)}, u32[]{:S(2)}) collective-permute-start(f32[15,40,128]{2,1,0:T(8,128)S(1)} %get-tuple-element.26), channel_id=1, source_target_pairs={{0,2},{1,31},{2,4},{3,1},{4,6},{5,3},{6,8},{7,5},{8,10},{9,7},{10,... | collective-permute-start | bytes 921608 | tf_op jit(solution)/shard_map/ppermute | solution.py:800
  35.8 10.9 %collective-permute-start.8 = (f32[15,40,128]{2,1,0:T(8,128)S(1)}, f32[15,40,128]{2,1,0:T(8,128)S(1)}, u32[]{:S(2)}, u32[]{:S(2)}) collective-permute-start(f32[15,40,128]{2,1,0:T(8,128)S(1)} %get-tuple-element.27), channel_id=1, source_target_pairs={{0,30},{1,3},{2,0},{3,5},{4,2},{5,7},{6,4},{7,9},{8,6},{9,11},{10,... | collective-permute-start | bytes 921608 | tf_op jit(solution)/shard_map/ppermute | solution.py:800
  35.8 50.7 %collective-permute-start.12 = (f32[24,32,128]{2,1,0:T(8,128)S(1)}, f32[24,32,128]{2,1,0:T(8,128)S(1)}, u32[]{:S(2)}, u32[]{:S(2)}) collective-permute-start(f32[24,32,128]{2,1,0:T(8,128)S(1)} %get-tuple-element.28), channel_id=1, source_target_pairs={{0,2},{1,31},{2,4},{3,1},{4,6},{5,3},{6,8},{7,5},{8,10},{9,7},{10,... | collective-permute-start | bytes 1179656 | tf_op jit(solution)/shard_map/ppermute | solution.py:800
  40.6 46.0 %collective-permute-start.13 = (f32[24,32,128]{2,1,0:T(8,128)S(1)}, f32[24,32,128]{2,1,0:T(8,128)S(1)}, u32[]{:S(2)}, u32[]{:S(2)}) collective-permute-start(f32[24,32,128]{2,1,0:T(8,128)S(1)} %get-tuple-element.29), channel_id=1, source_target_pairs={{0,30},{1,3},{2,0},{3,5},{4,2},{5,7},{6,4},{7,9},{8,6},{9,11},{10,... | collective-permute-start | bytes 1179656 | tf_op jit(solution)/shard_map/ppermute | solution.py:800
  80.5 1.3 %collective-permute-start.9 = (f32[16,128]{1,0:T(8,128)S(1)}, f32[16,128]{1,0:T(8,128)S(1)}, u32[]{:S(2)}, u32[]{:S(2)}) collective-permute-start(f32[16,128]{1,0:T(8,128)S(1)} %shard_map.61), channel_id=1, source_target_pairs={{0,1},{1,0},{2,3},{3,2},{4,5},{5,4},{6,7},{7,6},{8,9},{9,8},{10,11... | collective-permute-start | bytes 24584 | tf_op jit(solution)/shard_map/ppermute | solution.py:800
  81.8 12.5 %collective-permute-start.11 = (f32[2,16,128]{2,1,0:T(8,128)S(1)}, f32[2,16,128]{2,1,0:T(8,128)S(1)}, u32[]{:S(2)}, u32[]{:S(2)}) collective-permute-start(f32[2,16,128]{2,1,0:T(8,128)S(1)} %pad_maximum_fusion.1), channel_id=1, source_target_pairs={{0,30},{1,3},{2,0},{3,5},{4,2},{5,7},{6,4},{7,9},{8,6},{9,11},{10,... | collective-permute-start | bytes 49160 | tf_op jit(solution)/shard_map/ppermute | solution.py:800
  81.8 12.5 %collective-permute-start.10 = (f32[2,16,128]{2,1,0:T(8,128)S(1)}, f32[2,16,128]{2,1,0:T(8,128)S(1)}, u32[]{:S(2)}, u32[]{:S(2)}) collective-permute-start(f32[2,16,128]{2,1,0:T(8,128)S(1)} %pad_maximum_fusion.1), channel_id=1, source_target_pairs={{0,2},{1,31},{2,4},{3,1},{4,6},{5,3},{6,8},{7,5},{8,10},{9,7},{10,... | collective-permute-start | bytes 49160 | tf_op jit(solution)/shard_map/ppermute | solution.py:800
  94.3 5.8 %collective-permute-start.15 = (f32[6,16,128]{2,1,0:T(8,128)S(1)}, f32[6,16,128]{2,1,0:T(8,128)S(1)}, u32[]{:S(2)}, u32[]{:S(2)}) collective-permute-start(f32[6,16,128]{2,1,0:T(8,128)S(1)} %pad_maximum_fusion.parts), channel_id=1, source_target_pairs={{0,224},{1,33},{2,226},{3,35},{4,228},{5,37},{6,230},{7,39},{8,232... | collective-permute-start | bytes 147464 | tf_op jit(solution)/shard_map/ppermute | solution.py:800
  94.4 5.8 %collective-permute-start.14 = (f32[6,16,128]{2,1,0:T(8,128)S(1)}, f32[6,16,128]{2,1,0:T(8,128)S(1)}, u32[]{:S(2)}, u32[]{:S(2)}) collective-permute-start(f32[6,16,128]{2,1,0:T(8,128)S(1)} %pad_maximum_fusion.parts), channel_id=1, source_target_pairs={{0,32},{1,225},{2,34},{3,227},{4,36},{5,229},{6,38},{7,231},{8,40}... | collective-permute-start | bytes 147464 | tf_op jit(solution)/shard_map/ppermute | solution.py:800

commit v4 on v3

--- a/solution.py
+++ b/solution.py
@@ -28,6 +28,7 @@
 BF16 = jnp.bfloat16
 HIGH = lax.Precision.HIGHEST
 VMEM_LIMIT = 48 * 1024 * 1024
+LARGE_LIMIT = 61 * 1024 * 1024
 
 
 def iota(shape, dim):
@@ -126,7 +127,7 @@
     strip2[...] = strip[pl.ds(s2, DEEP)]
 
 
-def pack_kernel(sc, u, f, m, x1, x2, strip, strip1, strip2, own_u, own_f, msg1, msg2, side1, side2, eu, ef, em, es):
+def pack_kernel(sc, u, f, m, x1, x2, strip, strip1, strip2, own_u, own_f, msg1, msg2, eu, ef, em, es):
     gz = sc[0]
     low_first = gz == 0
     p1 = jnp.where(low_first, 0, BX + DEEP)
@@ -187,7 +188,7 @@
     loop(0, WIN, own, 6)
 
     sub = iota((8, 128), 0)
-    for msg, side, base, upward in ((msg1, side1, 4, low_first), (msg2, side2, 7, gz != 0)):
+    for msg, base, upward in ((msg1, 4, low_first), (msg2, 7, gz != 0)):
         take = window(sc[base + 2])
         start = sc[base] + 5
 
@@ -205,17 +206,40 @@
 
         loop(0, WIN // 2, pair, 3)
 
-        def plane(i, side=side, upward=upward):
-            x = i + DEEP - FSWEEPS
-
-            def edge(values):
-                return jnp.where(upward, row_roll(values[8:16], 4), values[0:8])
-
-            every = [edge(eu[k, x]) for k in range(3)] + [edge(ef[k, x]) for k in range(3)] + [edge(em[x]), edge(es[x])]
+
+def side_kernel(sc, u, f, m, x1, x2, strip, strip1, strip2, side1, side2):
+    low_first = sc[0] == 0
+    sub = iota((8, 128), 0)
+
+    def put(dest, values16):
+        for side, upward in ((side1, low_first), (side2, sc[0] != 0)):
+            every = [jnp.where(upward, row_roll(v[8:16], 4), v[0:8]) for v in values16]
             for j in range(4):
-                side[i, 8 * j : 8 * j + 8] = jnp.where(sub < 4, every[2 * j], row_roll(every[2 * j + 1], 4))
-
-        loop(0, AX, plane, 6)
+                side[dest, 8 * j : 8 * j + 8] = jnp.where(sub < 4, every[2 * j], row_roll(every[2 * j + 1], 4))
+
+    def inner_plane(i):
+        put(i + FSWEEPS, [u[k, i] for k in range(3)] + [f[k, i] for k in range(3)] + [m[i], strip[i]])
+
+    loop(0, BX, inner_plane, 8)
+
+    def outer_plane(i):
+        for a, b, sa, sb, start, dest in (
+            (x1, x2, strip2, strip1, DEEP - FSWEEPS, i), (x2, x1, strip1, strip2, 0, i + FSWEEPS + BX),
+        ):
+            j = i + start
+            force = j - (1 if start else 0)
+
+            def pick(index):
+                return jnp.where(low_first, a[index], b[index])
+
+            put(
+                dest,
+                [pick(k * DEEP + j) for k in range(3)]
+                + [pick(3 * DEEP + k * (DEEP - 1) + force) for k in range(3)]
+                + [pick(PLANES - DEEP + j), jnp.where(low_first, sa[j], sb[j])],
+            )
+
+    loop(0, FSWEEPS, outer_plane, 4)
 
 
 def invert(chains):
@@ -767,7 +791,7 @@
         out[x] = m[x] * (1.0 + acc[16 * x : 16 * x + 16, :])
 
 
-def call(kernel, shapes, scratch, inputs, flops, space=pltpu.VMEM):
+def call(kernel, shapes, scratch, inputs, flops, space=pltpu.VMEM, limit=VMEM_LIMIT):
     specs = [pl.BlockSpec(memory_space=pltpu.SMEM)] + [pl.BlockSpec(memory_space=space)] * (len(inputs) - 1)
     single = not isinstance(shapes, list)
     outs = [jax.ShapeDtypeStruct(s, F32) for s in ([shapes] if single else shapes)]
@@ -777,7 +801,7 @@
         in_specs=specs,
         out_specs=[pl.BlockSpec(memory_space=pltpu.VMEM)] * len(outs),
         scratch_shapes=[pltpu.VMEM(s, F32) if isinstance(s, tuple) else s for s in scratch],
-        compiler_params=pltpu.CompilerParams(vmem_limit_bytes=VMEM_LIMIT),
+        compiler_params=pltpu.CompilerParams(vmem_limit_bytes=limit),
         cost_estimate=pl.CostEstimate(flops=flops, bytes_accessed=1 << 20, transcendentals=0),
     )(*inputs)
     return results[0] if single else results
@@ -816,23 +840,35 @@
         [first, start_field, forcing, modulus],
         1 << 20,
         pltpu.HBM,
+        LARGE_LIMIT,
     )
     x1 = send(msg1, lambda x, y, z: (x + turn(z), y, z))
     x2 = send(msg2, lambda x, y, z: (x - turn(z), y, z))
     far_strip = send(strip, lambda x, y, z: (x, y, 1 - z))
     far1 = send(strip1, lambda x, y, z: (x + turn(z), y, 1 - z))
     far2 = send(strip2, lambda x, y, z: (x - turn(z), y, 1 - z))
-    own_u, own_f, y1, y2, a1, a2 = call(
+    spread = [scalar, start_field, forcing, modulus, x1, x2, far_strip, far1, far2]
+    a1, a2 = call(side_kernel, [(AX, 32, 128)] * 2, [], spread, 1 << 20)
+    b1 = send(a1, lambda x, y, z: (x, y + turn(z), z))
+    b2 = send(a2, lambda x, y, z: (x, y - turn(z), z))
+    own_u, own_f, y1, y2 = call(
         pack_kernel,
-        [(WIN, BY, 128)] * 2 + [(WIN // 2, 40, 128)] * 2 + [(AX, 32, 128)] * 2,
+        [(WIN, BY, 128)] * 2 + [(WIN // 2, 40, 128)] * 2,
         [(3, 36, BY, 128), (3, 36, BY, 128), (36, BY, 128), (36, BY, 128)],
-        [scalar, start_field, forcing, modulus, x1, x2, far_strip, far1, far2],
-        1 << 22,
+        spread,
+        1 << 31,
     )
     r1 = send(y1, lambda x, y, z: (x, y + turn(z), z))
     r2 = send(y2, lambda x, y, z: (x, y - turn(z), z))
-    b1 = send(a1, lambda x, y, z: (x, y + turn(z), z))
-    b2 = send(a2, lambda x, y, z: (x, y - turn(z), z))
+    wide = (AX, AX, 128)
+    displacement = call(
+        functools.partial(field_kernel, sizes),
+        (3, BX, BY, BZ),
+        [(3,) + wide] * 3 + [wide] * 15,
+        spread + [b1, b2],
+        1 << 32,
+    )
+    own_u, own_f, r1, r2, displacement = lax.optimization_barrier((own_u, own_f, r1, r2, displacement))
     window = (WIN, WY, 128)
     delta = call(
         functools.partial(zone_kernel, sizes),
@@ -848,15 +884,6 @@
     plane = jnp.stack([delta, send(delta, lambda x, y, z: (x, y, 1 - z))])
     right = send(plane, lambda x, y, z: (x, y + turn(z), z))
     left = send(plane, lambda x, y, z: (x, y - turn(z), z))
-    wide = (AX, AX, 128)
-    displacement = call(
-        functools.partial(field_kernel, sizes),
-        (3, BX, BY, BZ),
-        [(3,) + wide] * 3 + [wide] * 15,
-        [scalar, start_field, forcing, modulus, x1, x2, far_strip, far1, far2, b1, b2],
-        1 << 30,
-    )
-    right, left, displacement = lax.optimization_barrier((right, left, displacement))
     plane = jnp.concatenate([plane, right, left])
     after = send(plane, lambda x, y, z: (x + turn(z), y, z))
     before = send(plane, lambda x, y, z: (x - turn(z), y, z))

time: 103 us -> 103 us (level)
  the two profiles are of different devices: /device:TPU:1 before, /device:TPU:0 now
where the time goes in v4:
time: 103 us
  Pallas kernels  54.3 us (53%)
  starting transfers between devices  30.3 us (29%)
  waiting for transfers between devices  17 us (17%)
    pallas_call x7, Pallas kernels, call(): pl.pallas_call(kernel, out_shape=outs, in_specs=specs, out_specs=[pl.Bloc...  54.3 us
    ppermute x16, starting transfers between devices, send(): return lax.ppermute(values, AXES, pairs)  30.3 us
    ppermute x16, waiting for transfers between devices, send(): return lax.ppermute(values, AXES, pairs)  17 us
  transfers between devices with their start and end apart: 16, of which 6 were waited for; matrix products, arithmetic and copies ran while one was open for 0% of the time, Pallas kernels for 14%

profile of v4, /device:TPU:0, one launch (start us, length us, event | category | flops | bytes accessed | tf_op | source)
XLA Modules:
  0.0 103.2 jit_solution(13409595202177903284)
XLA Ops:
  0.6 0.0 copy-start
  0.6 0.0 copy-start.1
  0.7 0.0 copy-start.2
  0.7 2.7 %shard_map.59 = (f32[67,16,128]{2,1,0:T(8,128)}, f32[67,16,128]{2,1,0:T(8,128)}, f32[16,16,128]{2,1,0:T(8,128)}, f32[10,16,128]{2,1,0:T(8,128)}, f32[10,16,128]{2,1,0:T(8,128)}) custom-call(s32[1]{0:T(128)} %bitcast.sc, f32[3,16,16,128]{3,2,1,0:T(8,128)} %u.7, f32[3,16,16,128]{3,2,1,0:T(8,128)} %f.7, f32[16,16,128]{2,1,0:T(8,128)} %m.9), custom_call_target="tpu_custom_call" | custom-call | flops 1048576 | bytes 1048576 | tf_op jit(solution)/shard_map/pallas_call | solution.py:798
  3.4 0.3 collective-permute-start.2
  3.7 4.0 %collective-permute-start.3 = (f32[67,16,128]{2,1,0:T(8,128)}, f32[67,16,128]{2,1,0:T(8,128)S(1)}, u32[]{:S(2)}, u32[]{:S(2)}) collective-permute-start(f32[67,16,128]{2,1,0:T(8,128)} %get-tuple-element.22), channel_id=1, source_target_pairs={{0,224},{1,33},{2,226},{3,35},{4,228},{5,37},{6,230},{7,39},{8,232... | collective-permute-start | bytes 1646600 | tf_op jit(solution)/shard_map/ppermute | solution.py:824
  7.7 0.0 copy-start.3
  7.7 0.7 copy-done.3
  8.3 0.1 add_subtract_fusion.1
  8.4 1.5 %collective-permute-start.1 = (s32[1,3]{1,0:T(1,128)S(1)}, s32[1,3]{1,0:T(1,128)S(1)}, u32[]{:S(2)}, u32[]{:S(2)}) collective-permute-start(s32[1,3]{1,0:T(1,128)S(1)} %add_subtract_fusion.1), channel_id=1, source_target_pairs={{0,2},{1,31},{2,4},{3,1},{4,6},{5,3},{6,8},{7,5},{8,10},{9,7},{10,... | collective-permute-start | bytes 44 | tf_op jit(solution)/shard_map/ppermute | solution.py:824
  9.9 3.9 %collective-permute-start = (s32[1,3]{1,0:T(1,128)S(1)}, s32[1,3]{1,0:T(1,128)S(1)}, u32[]{:S(2)}, u32[]{:S(2)}) collective-permute-start(s32[1,3]{1,0:T(1,128)S(1)} %add_subtract_fusion.1), channel_id=1, source_target_pairs={{0,30},{1,3},{2,0},{3,5},{4,2},{5,7},{6,4},{7,9},{8,6},{9,11},{10,... | collective-permute-start | bytes 44 | tf_op jit(solution)/shard_map/ppermute | solution.py:824
  13.8 0.0 collective-permute-start.5
  13.8 1.5 %collective-permute-done.1 = s32[1,3]{1,0:T(1,128)S(1)} collective-permute-done((s32[1,3]{1,0:T(1,128)S(1)}, s32[1,3]{1,0:T(1,128)S(1)}, u32[]{:S(2)}, u32[]{:S(2)}) %collective-permute-start.1) | collective-permute-done | bytes 44 | tf_op jit(solution)/shard_map/ppermute | solution.py:824
  15.3 1.2 %collective-permute-start.6 = (f32[10,16,128]{2,1,0:T(8,128)}, f32[10,16,128]{2,1,0:T(8,128)S(1)}, u32[]{:S(2)}, u32[]{:S(2)}) collective-permute-start(f32[10,16,128]{2,1,0:T(8,128)} %get-tuple-element.25), channel_id=1, source_target_pairs={{0,225},{1,32},{2,227},{3,34},{4,229},{5,36},{6,231},{7,38},{8,233... | collective-permute-start | bytes 245768 | tf_op jit(solution)/shard_map/ppermute | solution.py:824
  16.5 0.0 collective-permute-done
  16.5 2.1 %collective-permute-start.4 = (f32[16,16,128]{2,1,0:T(8,128)}, f32[16,16,128]{2,1,0:T(8,128)S(1)}, u32[]{:S(2)}, u32[]{:S(2)}) collective-permute-start(f32[16,16,128]{2,1,0:T(8,128)} %get-tuple-element.23), channel_id=1, source_target_pairs={{0,1},{1,0},{2,3},{3,2},{4,5},{5,4},{6,7},{7,6},{8,9},{9,8},{10,11... | collective-permute-start | bytes 393224 | tf_op jit(solution)/shard_map/ppermute | solution.py:824
  18.6 0.1 add_subtract_fusion
  18.6 0.1 concatenate.9.sc
  18.7 0.0 collective-permute-done.5.strip1
  18.7 4.2 %collective-permute-done.6.strip2 = f32[10,16,128]{2,1,0:T(8,128)S(1)} collective-permute-done((f32[10,16,128]{2,1,0:T(8,128)}, f32[10,16,128]{2,1,0:T(8,128)S(1)}, u32[]{:S(2)}, u32[]{:S(2)}) %collective-permute-start.6) | collective-permute-done | bytes 81952 | tf_op jit(solution)/shard_map/ppermute | solution.py:824
  22.9 0.0 collective-permute-done.4.strip
  22.9 0.0 collective-permute-done.2.x1
  22.9 0.0 collective-permute-done.3.x2
  22.9 0.0 copy-done
  22.9 0.0 copy-done.1
  22.9 0.0 copy-done.2
  22.9 0.7 shard_map.61
  23.6 1.6 %collective-permute-start.9 = (f32[24,32,128]{2,1,0:T(8,128)S(1)}, f32[24,32,128]{2,1,0:T(8,128)S(1)}, u32[]{:S(2)}, u32[]{:S(2)}) collective-permute-start(f32[24,32,128]{2,1,0:T(8,128)S(1)} %get-tuple-element.30), channel_id=1, source_target_pairs={{0,2},{1,31},{2,4},{3,1},{4,6},{5,3},{6,8},{7,5},{8,10},{9,7},{10,... | collective-permute-start | bytes 1179656 | tf_op jit(solution)/shard_map/ppermute | solution.py:824
  25.2 3.9 %collective-permute-start.10 = (f32[24,32,128]{2,1,0:T(8,128)S(1)}, f32[24,32,128]{2,1,0:T(8,128)S(1)}, u32[]{:S(2)}, u32[]{:S(2)}) collective-permute-start(f32[24,32,128]{2,1,0:T(8,128)S(1)} %get-tuple-element.31), channel_id=1, source_target_pairs={{0,30},{1,3},{2,0},{3,5},{4,2},{5,7},{6,4},{7,9},{8,6},{9,11},{10,... | collective-permute-start | bytes 1179656 | tf_op jit(solution)/shard_map/ppermute | solution.py:824
  29.1 4.4 %shard_map.60 = (f32[30,16,128]{2,1,0:T(8,128)S(1)}, f32[30,16,128]{2,1,0:T(8,128)S(1)}, f32[15,40,128]{2,1,0:T(8,128)S(1)}, f32[15,40,128]{2,1,0:T(8,128)S(1)}) custom-call(s32[16]{0:T(128)S(1)} %concatenate.9.sc, f32[3,16,16,128]{3,2,1,0:T(8,128)S(1)} %copy-done, f32[3,16,16,128]{3,2,1,0:T(8,128)S(1)} %copy-done.1, f32[16,16,128]{2,1,0:T(8,128)S(1)} %copy-done.2, ...), custom_call_target="tpu_custom_call" | custom-call | flops 2147483648 | bytes 1048576 | tf_op jit(solution)/shard_map/pallas_call | solution.py:798
  33.5 0.1 collective-permute-start.7
  33.6 5.3 %collective-permute-start.8 = (f32[15,40,128]{2,1,0:T(8,128)S(1)}, f32[15,40,128]{2,1,0:T(8,128)S(1)}, u32[]{:S(2)}, u32[]{:S(2)}) collective-permute-start(f32[15,40,128]{2,1,0:T(8,128)S(1)} %get-tuple-element.29), channel_id=1, source_target_pairs={{0,30},{1,3},{2,0},{3,5},{4,2},{5,7},{6,4},{7,9},{8,6},{9,11},{10,... | collective-permute-start | bytes 921608 | tf_op jit(solution)/shard_map/ppermute | solution.py:824
  38.9 0.0 collective-permute-done.9.s1
  38.9 0.0 collective-permute-done.10.s2
  38.9 7.7 %shard_map.62 = f32[3,16,16,128]{3,2,1,0:T(8,128)} custom-call(s32[16]{0:T(128)S(1)} %concatenate.9.sc, f32[3,16,16,128]{3,2,1,0:T(8,128)S(1)} %copy-done, f32[3,16,16,128]{3,2,1,0:T(8,128)S(1)} %copy-done.1, f32[16,16,128]{2,1,0:T(8,128)S(1)} %copy-done.2, f32[67,16,128]{2,1,0:T(8,128)S(1)} %collective-permute-done.2.x1, ...), custom_call_target="tpu_custom_call" | custom-call | flops 4294967296 | bytes 1048576 | tf_op jit(solution)/shard_map/pallas_call | solution.py:798
  46.6 0.0 collective-permute-done.7.r1
  46.7 0.0 collective-permute-done.8.r2
  46.7 33.9 %shard_map.63 = f32[16,128]{1,0:T(8,128)S(1)} custom-call(s32[16]{0:T(128)S(1)} %concatenate.9.sc, f32[30,16,128]{2,1,0:T(8,128)S(1)} %get-tuple-element.33.own_u, f32[30,16,128]{2,1,0:T(8,128)S(1)} %get-tuple-element.34.own_f, f32[15,40,128]{2,1,0:T(8,128)S(1)} %collective-permute-done.7.r1, f32[15,40,128]{2,1,0:T(8,128)S(1)} %collective-permute-done.8.r2), custom_call_target="tpu_custom_call" | custom-call | flops 8589934592 | bytes 1048576 | tf_op jit(solution)/shard_map/pallas_call | solution.py:798
  80.5 0.3 collective-permute-start.11
  80.8 0.9 collective-permute-done.11
  81.8 3.2 %collective-permute-start.13 = (f32[2,16,128]{2,1,0:T(8,128)S(1)}, f32[2,16,128]{2,1,0:T(8,128)S(1)}, u32[]{:S(2)}, u32[]{:S(2)}) collective-permute-start(f32[2,16,128]{2,1,0:T(8,128)S(1)} %pad_maximum_fusion.1), channel_id=1, source_target_pairs={{0,30},{1,3},{2,0},{3,5},{4,2},{5,7},{6,4},{7,9},{8,6},{9,11},{10,... | collective-permute-start | bytes 49160 | tf_op jit(solution)/shard_map/ppermute | solution.py:824
  85.0 0.0 collective-permute-start.12
  85.0 1.4 %collective-permute-done.13 = f32[2,16,128]{2,1,0:T(8,128)S(1)} collective-permute-done((f32[2,16,128]{2,1,0:T(8,128)S(1)}, f32[2,16,128]{2,1,0:T(8,128)S(1)}, u32[]{:S(2)}, u32[]{:S(2)}) %collective-permute-start.13) | collective-permute-done | bytes 16416 | tf_op jit(solution)/shard_map/ppermute | solution.py:824
  86.5 5.6 %collective-permute-done.12 = f32[2,16,128]{2,1,0:T(8,128)S(1)} collective-permute-done((f32[2,16,128]{2,1,0:T(8,128)S(1)}, f32[2,16,128]{2,1,0:T(8,128)S(1)}, u32[]{:S(2)}, u32[]{:S(2)}) %collective-permute-start.12) | collective-permute-done | bytes 16416 | tf_op jit(solution)/shard_map/ppermute | solution.py:824
  92.1 3.0 %collective-permute-start.15 = (f32[6,16,128]{2,1,0:T(8,128)S(1)}, f32[6,16,128]{2,1,0:T(8,128)S(1)}, u32[]{:S(2)}, u32[]{:S(2)}) collective-permute-start(f32[6,16,128]{2,1,0:T(8,128)S(1)} %pad_maximum_fusion.parts), channel_id=1, source_target_pairs={{0,224},{1,33},{2,226},{3,35},{4,228},{5,37},{6,230},{7,39},{8,232... | collective-permute-start | bytes 147464 | tf_op jit(solution)/shard_map/ppermute | solution.py:824
  95.1 0.0 collective-permute-start.14
  95.1 2.0 %shard_map.64.near = f32[256,128]{1,0:T(8,128)S(1)} custom-call(s32[16]{0:T(128)S(1)} %concatenate.9.sc, f32[6,16,128]{2,1,0:T(8,128)S(1)} %pad_maximum_fusion.parts), custom_call_target="tpu_custom_call" | custom-call | flops 536870912 | bytes 1048576 | tf_op jit(solution)/shard_map/pallas_call | solution.py:798
  97.1 0.0 collective-permute-done.15.parts2
  97.1 3.3 %collective-permute-done.14.parts1 = f32[6,16,128]{2,1,0:T(8,128)S(1)} collective-permute-done((f32[6,16,128]{2,1,0:T(8,128)S(1)}, f32[6,16,128]{2,1,0:T(8,128)S(1)}, u32[]{:S(2)}, u32[]{:S(2)}) %collective-permute-start.14) | collective-permute-done | bytes 49184 | tf_op jit(solution)/shard_map/ppermute | solution.py:824
  100.4 2.8 %shard_map.65 = f32[16,16,128]{2,1,0:T(8,128)} custom-call(s32[16]{0:T(128)S(1)} %concatenate.9.sc, f32[16,16,128]{2,1,0:T(8,128)S(1)} %copy-done.2, f32[256,128]{1,0:T(8,128)S(1)} %shard_map.64.near, f32[6,16,128]{2,1,0:T(8,128)S(1)} %collective-permute-done.14.parts1, f32[6,16,128]{2,1,0:T(8,128)S(1)} %collective-permute-done.15.parts2), custom_call_target="tpu_custom_call" | custom-call | flops 16777216 | bytes 1048576 | tf_op jit(solution)/shard_map/pallas_call | solution.py:798
  (2 shorter events, 0.0 us)
Async XLA Ops:
  0.6 22.3 %copy-start = (f32[3,16,16,128]{3,2,1,0:T(8,128)S(1)}, f32[3,16,16,128]{3,2,1,0:T(8,128)}, u32[]{:S(2)}) copy-start(f32[3,16,16,128]{3,2,1,0:T(8,128)} %u.7) | copy-start | bytes 1179652
  0.6 22.3 %copy-start.1 = (f32[3,16,16,128]{3,2,1,0:T(8,128)S(1)}, f32[3,16,16,128]{3,2,1,0:T(8,128)}, u32[]{:S(2)}) copy-start(f32[3,16,16,128]{3,2,1,0:T(8,128)} %f.7) | copy-start | bytes 1179652
  0.7 22.3 %copy-start.2 = (f32[16,16,128]{2,1,0:T(8,128)S(1)}, f32[16,16,128]{2,1,0:T(8,128)}, u32[]{:S(2)}) copy-start(f32[16,16,128]{2,1,0:T(8,128)} %m.9) | copy-start | bytes 393220
  3.4 19.5 %collective-permute-start.2 = (f32[67,16,128]{2,1,0:T(8,128)}, f32[67,16,128]{2,1,0:T(8,128)S(1)}, u32[]{:S(2)}, u32[]{:S(2)}) collective-permute-start(f32[67,16,128]{2,1,0:T(8,128)} %get-tuple-element.21), channel_id=1, source_target_pairs={{0,32},{1,225},{2,34},{3,227},{4,36},{5,229},{6,38},{7,231},{8,40}... | collective-permute-start | bytes 1646600 | tf_op jit(solution)/shard_map/ppermute | solution.py:824
  3.7 19.2 %collective-permute-start.3 = (f32[67,16,128]{2,1,0:T(8,128)}, f32[67,16,128]{2,1,0:T(8,128)S(1)}, u32[]{:S(2)}, u32[]{:S(2)}) collective-permute-start(f32[67,16,128]{2,1,0:T(8,128)} %get-tuple-element.22), channel_id=1, source_target_pairs={{0,224},{1,33},{2,226},{3,35},{4,228},{5,37},{6,230},{7,39},{8,232... | collective-permute-start | bytes 1646600 | tf_op jit(solution)/shard_map/ppermute | solution.py:824
  7.7 0.7 copy-start.3
  8.4 6.9 %collective-permute-start.1 = (s32[1,3]{1,0:T(1,128)S(1)}, s32[1,3]{1,0:T(1,128)S(1)}, u32[]{:S(2)}, u32[]{:S(2)}) collective-permute-start(s32[1,3]{1,0:T(1,128)S(1)} %add_subtract_fusion.1), channel_id=1, source_target_pairs={{0,2},{1,31},{2,4},{3,1},{4,6},{5,3},{6,8},{7,5},{8,10},{9,7},{10,... | collective-permute-start | bytes 44 | tf_op jit(solution)/shard_map/ppermute | solution.py:824
  9.9 6.5 %collective-permute-start = (s32[1,3]{1,0:T(1,128)S(1)}, s32[1,3]{1,0:T(1,128)S(1)}, u32[]{:S(2)}, u32[]{:S(2)}) collective-permute-start(s32[1,3]{1,0:T(1,128)S(1)} %add_subtract_fusion.1), channel_id=1, source_target_pairs={{0,30},{1,3},{2,0},{3,5},{4,2},{5,7},{6,4},{7,9},{8,6},{9,11},{10,... | collective-permute-start | bytes 44 | tf_op jit(solution)/shard_map/ppermute | solution.py:824
  13.8 4.9 %collective-permute-start.5 = (f32[10,16,128]{2,1,0:T(8,128)}, f32[10,16,128]{2,1,0:T(8,128)S(1)}, u32[]{:S(2)}, u32[]{:S(2)}) collective-permute-start(f32[10,16,128]{2,1,0:T(8,128)} %get-tuple-element.24), channel_id=1, source_target_pairs={{0,33},{1,224},{2,35},{3,226},{4,37},{5,228},{6,39},{7,230},{8,41}... | collective-permute-start | bytes 245768 | tf_op jit(solution)/shard_map/ppermute | solution.py:824
  15.3 7.6 %collective-permute-start.6 = (f32[10,16,128]{2,1,0:T(8,128)}, f32[10,16,128]{2,1,0:T(8,128)S(1)}, u32[]{:S(2)}, u32[]{:S(2)}) collective-permute-start(f32[10,16,128]{2,1,0:T(8,128)} %get-tuple-element.25), channel_id=1, source_target_pairs={{0,225},{1,32},{2,227},{3,34},{4,229},{5,36},{6,231},{7,38},{8,233... | collective-permute-start | bytes 245768 | tf_op jit(solution)/shard_map/ppermute | solution.py:824
  16.5 6.4 %collective-permute-start.4 = (f32[16,16,128]{2,1,0:T(8,128)}, f32[16,16,128]{2,1,0:T(8,128)S(1)}, u32[]{:S(2)}, u32[]{:S(2)}) collective-permute-start(f32[16,16,128]{2,1,0:T(8,128)} %get-tuple-element.23), channel_id=1, source_target_pairs={{0,1},{1,0},{2,3},{3,2},{4,5},{5,4},{6,7},{7,6},{8,9},{9,8},{10,11... | collective-permute-start | bytes 393224 | tf_op jit(solution)/shard_map/ppermute | solution.py:824
  23.6 15.3 %collective-permute-start.9 = (f32[24,32,128]{2,1,0:T(8,128)S(1)}, f32[24,32,128]{2,1,0:T(8,128)S(1)}, u32[]{:S(2)}, u32[]{:S(2)}) collective-permute-start(f32[24,32,128]{2,1,0:T(8,128)S(1)} %get-tuple-element.30), channel_id=1, source_target_pairs={{0,2},{1,31},{2,4},{3,1},{4,6},{5,3},{6,8},{7,5},{8,10},{9,7},{10,... | collective-permute-start | bytes 1179656 | tf_op jit(solution)/shard_map/ppermute | solution.py:824
  25.2 13.7 %collective-permute-start.10 = (f32[24,32,128]{2,1,0:T(8,128)S(1)}, f32[24,32,128]{2,1,0:T(8,128)S(1)}, u32[]{:S(2)}, u32[]{:S(2)}) collective-permute-start(f32[24,32,128]{2,1,0:T(8,128)S(1)} %get-tuple-element.31), channel_id=1, source_target_pairs={{0,30},{1,3},{2,0},{3,5},{4,2},{5,7},{6,4},{7,9},{8,6},{9,11},{10,... | collective-permute-start | bytes 1179656 | tf_op jit(solution)/shard_map/ppermute | solution.py:824
  33.5 13.1 %collective-permute-start.7 = (f32[15,40,128]{2,1,0:T(8,128)S(1)}, f32[15,40,128]{2,1,0:T(8,128)S(1)}, u32[]{:S(2)}, u32[]{:S(2)}) collective-permute-start(f32[15,40,128]{2,1,0:T(8,128)S(1)} %get-tuple-element.28), channel_id=1, source_target_pairs={{0,2},{1,31},{2,4},{3,1},{4,6},{5,3},{6,8},{7,5},{8,10},{9,7},{10,... | collective-permute-start | bytes 921608 | tf_op jit(solution)/shard_map/ppermute | solution.py:824
  33.6 13.1 %collective-permute-start.8 = (f32[15,40,128]{2,1,0:T(8,128)S(1)}, f32[15,40,128]{2,1,0:T(8,128)S(1)}, u32[]{:S(2)}, u32[]{:S(2)}) collective-permute-start(f32[15,40,128]{2,1,0:T(8,128)S(1)} %get-tuple-element.29), channel_id=1, source_target_pairs={{0,30},{1,3},{2,0},{3,5},{4,2},{5,7},{6,4},{7,9},{8,6},{9,11},{10,... | collective-permute-start | bytes 921608 | tf_op jit(solution)/shard_map/ppermute | solution.py:824
  80.5 1.3 %collective-permute-start.11 = (f32[16,128]{1,0:T(8,128)S(1)}, f32[16,128]{1,0:T(8,128)S(1)}, u32[]{:S(2)}, u32[]{:S(2)}) collective-permute-start(f32[16,128]{1,0:T(8,128)S(1)} %shard_map.63), channel_id=1, source_target_pairs={{0,1},{1,0},{2,3},{3,2},{4,5},{5,4},{6,7},{7,6},{8,9},{9,8},{10,11... | collective-permute-start | bytes 24584 | tf_op jit(solution)/shard_map/ppermute | solution.py:824
  81.8 4.7 %collective-permute-start.13 = (f32[2,16,128]{2,1,0:T(8,128)S(1)}, f32[2,16,128]{2,1,0:T(8,128)S(1)}, u32[]{:S(2)}, u32[]{:S(2)}) collective-permute-start(f32[2,16,128]{2,1,0:T(8,128)S(1)} %pad_maximum_fusion.1), channel_id=1, source_target_pairs={{0,30},{1,3},{2,0},{3,5},{4,2},{5,7},{6,4},{7,9},{8,6},{9,11},{10,... | collective-permute-start | bytes 49160 | tf_op jit(solution)/shard_map/ppermute | solution.py:824
  85.0 7.1 %collective-permute-start.12 = (f32[2,16,128]{2,1,0:T(8,128)S(1)}, f32[2,16,128]{2,1,0:T(8,128)S(1)}, u32[]{:S(2)}, u32[]{:S(2)}) collective-permute-start(f32[2,16,128]{2,1,0:T(8,128)S(1)} %pad_maximum_fusion.1), channel_id=1, source_target_pairs={{0,2},{1,31},{2,4},{3,1},{4,6},{5,3},{6,8},{7,5},{8,10},{9,7},{10,... | collective-permute-start | bytes 49160 | tf_op jit(solution)/shard_map/ppermute | solution.py:824
  92.1 5.0 %collective-permute-start.15 = (f32[6,16,128]{2,1,0:T(8,128)S(1)}, f32[6,16,128]{2,1,0:T(8,128)S(1)}, u32[]{:S(2)}, u32[]{:S(2)}) collective-permute-start(f32[6,16,128]{2,1,0:T(8,128)S(1)} %pad_maximum_fusion.parts), channel_id=1, source_target_pairs={{0,224},{1,33},{2,226},{3,35},{4,228},{5,37},{6,230},{7,39},{8,232... | collective-permute-start | bytes 147464 | tf_op jit(solution)/shard_map/ppermute | solution.py:824
  95.1 5.3 %collective-permute-start.14 = (f32[6,16,128]{2,1,0:T(8,128)S(1)}, f32[6,16,128]{2,1,0:T(8,128)S(1)}, u32[]{:S(2)}, u32[]{:S(2)}) collective-permute-start(f32[6,16,128]{2,1,0:T(8,128)S(1)} %pad_maximum_fusion.parts), channel_id=1, source_target_pairs={{0,32},{1,225},{2,34},{3,227},{4,36},{5,229},{6,38},{7,231},{8,40}... | collective-permute-start | bytes 147464 | tf_op jit(solution)/shard_map/ppermute | solution.py:824

commit v5 on v4

--- a/solution.py
+++ b/solution.py
@@ -185,7 +185,7 @@
         own_u[i] = field
         own_f[i] = force
 
-    loop(0, WIN, own, 6)
+    loop(0, WIN, own, 10)
 
     sub = iota((8, 128), 0)
     for msg, base, upward in ((msg1, 4, low_first), (msg2, 7, gz != 0)):
@@ -204,7 +204,7 @@
                     number += 1
             msg[i, 32:40] = mixed
 
-        loop(0, WIN // 2, pair, 3)
+        loop(0, WIN // 2, pair, 5)
 
 
 def side_kernel(sc, u, f, m, x1, x2, strip, strip1, strip2, side1, side2):
@@ -350,7 +350,7 @@
                 else:
                     fo[2 * i + step] = tall
 
-    loop(0, WIN // 2, unpack, 3)
+    loop(0, WIN // 2, unpack, 5)
 
     def faces(i):
         here = m3[i]
@@ -435,7 +435,7 @@
                 piece = tall[n * WY : (n + 1) * WY, 128 * k : 128 * k + 128] * pick_y
                 rows[n, k, pl.ds(a, 1), :] = jnp.sum(piece, axis=0, keepdims=True)
 
-    loop(0, PC, layer, 5)
+    loop(0, PC, layer, PC)
 
     lane16 = iota((16, 128), 1)
     row16 = iota((16, 128), 0)
@@ -772,7 +772,7 @@
     def add(n):
         acc[...] += contribution(sc, parts[n], 0, BX)
 
-    loop(0, parts.shape[0], add, 3)
+    loop(0, parts.shape[0], add, 6)
 
 
 def final_kernel(sc, m, near, parts1, parts2, out, acc):
@@ -786,7 +786,7 @@
             where = pl.ds(pl.multiple_of(start * BY, BY), reach * BY)
             acc[where, :] += contribution(sc, parts[n], start, reach)
 
-    loop(0, parts1.shape[0], add, 3)
+    loop(0, parts1.shape[0], add, 6)
     for x in range(BX):
         out[x] = m[x] * (1.0 + acc[16 * x : 16 * x + 16, :])
 

time: 103 us -> 103 us (level)
  Pallas kernels: 54.3 us -> 53 us
    pallas_call x7, Pallas kernels: 54.3 us -> 53 us  [call(): pl.pallas_call(kernel, out_shape=outs, in_specs=specs, out_specs=[pl.Bloc...]
  transfers between devices with their start and end apart: 16 -> 16, of which waited for: 6 -> 7; matrix products, arithmetic and copies ran while one was open for 0% -> 0% of each run, Pallas kernels for 14% -> 13%
where the time goes in v5:
time: 103 us
  Pallas kernels  53 us (51%)
  starting transfers between devices  30.8 us (30%)
  waiting for transfers between devices  17.4 us (17%)
    pallas_call x7, Pallas kernels, call(): pl.pallas_call(kernel, out_shape=outs, in_specs=specs, out_specs=[pl.Bloc...  53 us
    ppermute x16, starting transfers between devices, send(): return lax.ppermute(values, AXES, pairs)  30.8 us
    ppermute x16, waiting for transfers between devices, send(): return lax.ppermute(values, AXES, pairs)  17.4 us
  transfers between devices with their start and end apart: 16, of which 7 were waited for; matrix products, arithmetic and copies ran while one was open for 0% of the time, Pallas kernels for 13%

profile of v5, /device:TPU:0, one launch (start us, length us, event | category | flops | bytes accessed | tf_op | source)
XLA Modules:
  0.0 102.8 jit_solution(353368052717242740)
XLA Ops:
  0.6 0.0 copy-start
  0.6 0.0 copy-start.1
  0.7 0.0 copy-start.2
  0.7 2.7 %shard_map.59 = (f32[67,16,128]{2,1,0:T(8,128)}, f32[67,16,128]{2,1,0:T(8,128)}, f32[16,16,128]{2,1,0:T(8,128)}, f32[10,16,128]{2,1,0:T(8,128)}, f32[10,16,128]{2,1,0:T(8,128)}) custom-call(s32[1]{0:T(128)} %bitcast.sc, f32[3,16,16,128]{3,2,1,0:T(8,128)} %u.7, f32[3,16,16,128]{3,2,1,0:T(8,128)} %f.7, f32[16,16,128]{2,1,0:T(8,128)} %m.9), custom_call_target="tpu_custom_call" | custom-call | flops 1048576 | bytes 1048576 | tf_op jit(solution)/shard_map/pallas_call | solution.py:798
  3.4 0.3 collective-permute-start.2
  3.7 4.0 %collective-permute-start.3 = (f32[67,16,128]{2,1,0:T(8,128)}, f32[67,16,128]{2,1,0:T(8,128)S(1)}, u32[]{:S(2)}, u32[]{:S(2)}) collective-permute-start(f32[67,16,128]{2,1,0:T(8,128)} %get-tuple-element.22), channel_id=1, source_target_pairs={{0,224},{1,33},{2,226},{3,35},{4,228},{5,37},{6,230},{7,39},{8,232... | collective-permute-start | bytes 1646600 | tf_op jit(solution)/shard_map/ppermute | solution.py:824
  7.7 0.0 copy-start.3
  7.7 0.7 copy-done.3
  8.3 0.1 add_subtract_fusion.1
  8.4 1.5 %collective-permute-start.1 = (s32[1,3]{1,0:T(1,128)S(1)}, s32[1,3]{1,0:T(1,128)S(1)}, u32[]{:S(2)}, u32[]{:S(2)}) collective-permute-start(s32[1,3]{1,0:T(1,128)S(1)} %add_subtract_fusion.1), channel_id=1, source_target_pairs={{0,2},{1,31},{2,4},{3,1},{4,6},{5,3},{6,8},{7,5},{8,10},{9,7},{10,... | collective-permute-start | bytes 44 | tf_op jit(solution)/shard_map/ppermute | solution.py:824
  9.9 3.9 %collective-permute-start = (s32[1,3]{1,0:T(1,128)S(1)}, s32[1,3]{1,0:T(1,128)S(1)}, u32[]{:S(2)}, u32[]{:S(2)}) collective-permute-start(s32[1,3]{1,0:T(1,128)S(1)} %add_subtract_fusion.1), channel_id=1, source_target_pairs={{0,30},{1,3},{2,0},{3,5},{4,2},{5,7},{6,4},{7,9},{8,6},{9,11},{10,... | collective-permute-start | bytes 44 | tf_op jit(solution)/shard_map/ppermute | solution.py:824
  13.8 0.0 collective-permute-start.5
  13.8 1.5 %collective-permute-done.1 = s32[1,3]{1,0:T(1,128)S(1)} collective-permute-done((s32[1,3]{1,0:T(1,128)S(1)}, s32[1,3]{1,0:T(1,128)S(1)}, u32[]{:S(2)}, u32[]{:S(2)}) %collective-permute-start.1) | collective-permute-done | bytes 44 | tf_op jit(solution)/shard_map/ppermute | solution.py:824
  15.3 1.2 %collective-permute-start.6 = (f32[10,16,128]{2,1,0:T(8,128)}, f32[10,16,128]{2,1,0:T(8,128)S(1)}, u32[]{:S(2)}, u32[]{:S(2)}) collective-permute-start(f32[10,16,128]{2,1,0:T(8,128)} %get-tuple-element.25), channel_id=1, source_target_pairs={{0,225},{1,32},{2,227},{3,34},{4,229},{5,36},{6,231},{7,38},{8,233... | collective-permute-start | bytes 245768 | tf_op jit(solution)/shard_map/ppermute | solution.py:824
  16.5 0.0 collective-permute-done
  16.5 2.1 %collective-permute-start.4 = (f32[16,16,128]{2,1,0:T(8,128)}, f32[16,16,128]{2,1,0:T(8,128)S(1)}, u32[]{:S(2)}, u32[]{:S(2)}) collective-permute-start(f32[16,16,128]{2,1,0:T(8,128)} %get-tuple-element.23), channel_id=1, source_target_pairs={{0,1},{1,0},{2,3},{3,2},{4,5},{5,4},{6,7},{7,6},{8,9},{9,8},{10,11... | collective-permute-start | bytes 393224 | tf_op jit(solution)/shard_map/ppermute | solution.py:824
  18.6 0.1 add_subtract_fusion
  18.6 0.1 concatenate.9.sc
  18.7 0.0 collective-permute-done.5.strip1
  18.7 4.2 %collective-permute-done.6.strip2 = f32[10,16,128]{2,1,0:T(8,128)S(1)} collective-permute-done((f32[10,16,128]{2,1,0:T(8,128)}, f32[10,16,128]{2,1,0:T(8,128)S(1)}, u32[]{:S(2)}, u32[]{:S(2)}) %collective-permute-start.6) | collective-permute-done | bytes 81952 | tf_op jit(solution)/shard_map/ppermute | solution.py:824
  22.9 0.0 collective-permute-done.4.strip
  22.9 0.0 collective-permute-done.2.x1
  22.9 0.0 collective-permute-done.3.x2
  22.9 0.0 copy-done
  22.9 0.0 copy-done.1
  22.9 0.0 copy-done.2
  22.9 0.7 shard_map.61
  23.6 1.6 %collective-permute-start.9 = (f32[24,32,128]{2,1,0:T(8,128)S(1)}, f32[24,32,128]{2,1,0:T(8,128)S(1)}, u32[]{:S(2)}, u32[]{:S(2)}) collective-permute-start(f32[24,32,128]{2,1,0:T(8,128)S(1)} %get-tuple-element.30), channel_id=1, source_target_pairs={{0,2},{1,31},{2,4},{3,1},{4,6},{5,3},{6,8},{7,5},{8,10},{9,7},{10,... | collective-permute-start | bytes 1179656 | tf_op jit(solution)/shard_map/ppermute | solution.py:824
  25.2 3.9 %collective-permute-start.10 = (f32[24,32,128]{2,1,0:T(8,128)S(1)}, f32[24,32,128]{2,1,0:T(8,128)S(1)}, u32[]{:S(2)}, u32[]{:S(2)}) collective-permute-start(f32[24,32,128]{2,1,0:T(8,128)S(1)} %get-tuple-element.31), channel_id=1, source_target_pairs={{0,30},{1,3},{2,0},{3,5},{4,2},{5,7},{6,4},{7,9},{8,6},{9,11},{10,... | collective-permute-start | bytes 1179656 | tf_op jit(solution)/shard_map/ppermute | solution.py:824
  29.1 4.0 %shard_map.60 = (f32[30,16,128]{2,1,0:T(8,128)S(1)}, f32[30,16,128]{2,1,0:T(8,128)S(1)}, f32[15,40,128]{2,1,0:T(8,128)S(1)}, f32[15,40,128]{2,1,0:T(8,128)S(1)}) custom-call(s32[16]{0:T(128)S(1)} %concatenate.9.sc, f32[3,16,16,128]{3,2,1,0:T(8,128)S(1)} %copy-done, f32[3,16,16,128]{3,2,1,0:T(8,128)S(1)} %copy-done.1, f32[16,16,128]{2,1,0:T(8,128)S(1)} %copy-done.2, ...), custom_call_target="tpu_custom_call" | custom-call | flops 2147483648 | bytes 1048576 | tf_op jit(solution)/shard_map/pallas_call | solution.py:798
  33.1 0.1 collective-permute-start.7
  33.2 5.3 %collective-permute-start.8 = (f32[15,40,128]{2,1,0:T(8,128)S(1)}, f32[15,40,128]{2,1,0:T(8,128)S(1)}, u32[]{:S(2)}, u32[]{:S(2)}) collective-permute-start(f32[15,40,128]{2,1,0:T(8,128)S(1)} %get-tuple-element.29), channel_id=1, source_target_pairs={{0,30},{1,3},{2,0},{3,5},{4,2},{5,7},{6,4},{7,9},{8,6},{9,11},{10,... | collective-permute-start | bytes 921608 | tf_op jit(solution)/shard_map/ppermute | solution.py:824
  38.5 0.0 collective-permute-done.9.s1
  38.5 0.0 collective-permute-done.10.s2
  38.5 7.7 %shard_map.62 = f32[3,16,16,128]{3,2,1,0:T(8,128)} custom-call(s32[16]{0:T(128)S(1)} %concatenate.9.sc, f32[3,16,16,128]{3,2,1,0:T(8,128)S(1)} %copy-done, f32[3,16,16,128]{3,2,1,0:T(8,128)S(1)} %copy-done.1, f32[16,16,128]{2,1,0:T(8,128)S(1)} %copy-done.2, f32[67,16,128]{2,1,0:T(8,128)S(1)} %collective-permute-done.2.x1, ...), custom_call_target="tpu_custom_call" | custom-call | flops 4294967296 | bytes 1048576 | tf_op jit(solution)/shard_map/pallas_call | solution.py:798
  46.2 0.0 collective-permute-done.7.r1
  46.2 0.0 collective-permute-done.8.r2
  46.2 33.6 %shard_map.63 = f32[16,128]{1,0:T(8,128)S(1)} custom-call(s32[16]{0:T(128)S(1)} %concatenate.9.sc, f32[30,16,128]{2,1,0:T(8,128)S(1)} %get-tuple-element.33.own_u, f32[30,16,128]{2,1,0:T(8,128)S(1)} %get-tuple-element.34.own_f, f32[15,40,128]{2,1,0:T(8,128)S(1)} %collective-permute-done.7.r1, f32[15,40,128]{2,1,0:T(8,128)S(1)} %collective-permute-done.8.r2), custom_call_target="tpu_custom_call" | custom-call | flops 8589934592 | bytes 1048576 | tf_op jit(solution)/shard_map/pallas_call | solution.py:798
  79.8 0.4 collective-permute-start.11
  80.2 0.8 collective-permute-done.11
  81.1 3.7 %collective-permute-start.13 = (f32[2,16,128]{2,1,0:T(8,128)S(1)}, f32[2,16,128]{2,1,0:T(8,128)S(1)}, u32[]{:S(2)}, u32[]{:S(2)}) collective-permute-start(f32[2,16,128]{2,1,0:T(8,128)S(1)} %pad_maximum_fusion.1), channel_id=1, source_target_pairs={{0,30},{1,3},{2,0},{3,5},{4,2},{5,7},{6,4},{7,9},{8,6},{9,11},{10,... | collective-permute-start | bytes 49160 | tf_op jit(solution)/shard_map/ppermute | solution.py:824
  84.7 0.0 collective-permute-start.12
  84.7 1.4 %collective-permute-done.13 = f32[2,16,128]{2,1,0:T(8,128)S(1)} collective-permute-done((f32[2,16,128]{2,1,0:T(8,128)S(1)}, f32[2,16,128]{2,1,0:T(8,128)S(1)}, u32[]{:S(2)}, u32[]{:S(2)}) %collective-permute-start.13) | collective-permute-done | bytes 16416 | tf_op jit(solution)/shard_map/ppermute | solution.py:824
  86.2 5.6 %collective-permute-done.12 = f32[2,16,128]{2,1,0:T(8,128)S(1)} collective-permute-done((f32[2,16,128]{2,1,0:T(8,128)S(1)}, f32[2,16,128]{2,1,0:T(8,128)S(1)}, u32[]{:S(2)}, u32[]{:S(2)}) %collective-permute-start.12) | collective-permute-done | bytes 16416 | tf_op jit(solution)/shard_map/ppermute | solution.py:824
  91.8 3.0 %collective-permute-start.15 = (f32[6,16,128]{2,1,0:T(8,128)S(1)}, f32[6,16,128]{2,1,0:T(8,128)S(1)}, u32[]{:S(2)}, u32[]{:S(2)}) collective-permute-start(f32[6,16,128]{2,1,0:T(8,128)S(1)} %pad_maximum_fusion.parts), channel_id=1, source_target_pairs={{0,224},{1,33},{2,226},{3,35},{4,228},{5,37},{6,230},{7,39},{8,232... | collective-permute-start | bytes 147464 | tf_op jit(solution)/shard_map/ppermute | solution.py:824
  94.8 0.0 collective-permute-start.14
  94.8 1.5 %shard_map.64.near = f32[256,128]{1,0:T(8,128)S(1)} custom-call(s32[16]{0:T(128)S(1)} %concatenate.9.sc, f32[6,16,128]{2,1,0:T(8,128)S(1)} %pad_maximum_fusion.parts), custom_call_target="tpu_custom_call" | custom-call | flops 536870912 | bytes 1048576 | tf_op jit(solution)/shard_map/pallas_call | solution.py:798
  96.3 0.3 collective-permute-done.15.parts2
  96.5 3.5 %collective-permute-done.14.parts1 = f32[6,16,128]{2,1,0:T(8,128)S(1)} collective-permute-done((f32[6,16,128]{2,1,0:T(8,128)S(1)}, f32[6,16,128]{2,1,0:T(8,128)S(1)}, u32[]{:S(2)}, u32[]{:S(2)}) %collective-permute-start.14) | collective-permute-done | bytes 49184 | tf_op jit(solution)/shard_map/ppermute | solution.py:824
  100.1 2.7 %shard_map.65 = f32[16,16,128]{2,1,0:T(8,128)} custom-call(s32[16]{0:T(128)S(1)} %concatenate.9.sc, f32[16,16,128]{2,1,0:T(8,128)S(1)} %copy-done.2, f32[256,128]{1,0:T(8,128)S(1)} %shard_map.64.near, f32[6,16,128]{2,1,0:T(8,128)S(1)} %collective-permute-done.14.parts1, f32[6,16,128]{2,1,0:T(8,128)S(1)} %collective-permute-done.15.parts2), custom_call_target="tpu_custom_call" | custom-call | flops 16777216 | bytes 1048576 | tf_op jit(solution)/shard_map/pallas_call | solution.py:798
  (2 shorter events, 0.0 us)
Async XLA Ops:
  0.6 22.3 %copy-start = (f32[3,16,16,128]{3,2,1,0:T(8,128)S(1)}, f32[3,16,16,128]{3,2,1,0:T(8,128)}, u32[]{:S(2)}) copy-start(f32[3,16,16,128]{3,2,1,0:T(8,128)} %u.7) | copy-start | bytes 1179652
  0.6 22.3 %copy-start.1 = (f32[3,16,16,128]{3,2,1,0:T(8,128)S(1)}, f32[3,16,16,128]{3,2,1,0:T(8,128)}, u32[]{:S(2)}) copy-start(f32[3,16,16,128]{3,2,1,0:T(8,128)} %f.7) | copy-start | bytes 1179652
  0.7 22.3 %copy-start.2 = (f32[16,16,128]{2,1,0:T(8,128)S(1)}, f32[16,16,128]{2,1,0:T(8,128)}, u32[]{:S(2)}) copy-start(f32[16,16,128]{2,1,0:T(8,128)} %m.9) | copy-start | bytes 393220
  3.4 19.5 %collective-permute-start.2 = (f32[67,16,128]{2,1,0:T(8,128)}, f32[67,16,128]{2,1,0:T(8,128)S(1)}, u32[]{:S(2)}, u32[]{:S(2)}) collective-permute-start(f32[67,16,128]{2,1,0:T(8,128)} %get-tuple-element.21), channel_id=1, source_target_pairs={{0,32},{1,225},{2,34},{3,227},{4,36},{5,229},{6,38},{7,231},{8,40}... | collective-permute-start | bytes 1646600 | tf_op jit(solution)/shard_map/ppermute | solution.py:824
  3.7 19.2 %collective-permute-start.3 = (f32[67,16,128]{2,1,0:T(8,128)}, f32[67,16,128]{2,1,0:T(8,128)S(1)}, u32[]{:S(2)}, u32[]{:S(2)}) collective-permute-start(f32[67,16,128]{2,1,0:T(8,128)} %get-tuple-element.22), channel_id=1, source_target_pairs={{0,224},{1,33},{2,226},{3,35},{4,228},{5,37},{6,230},{7,39},{8,232... | collective-permute-start | bytes 1646600 | tf_op jit(solution)/shard_map/ppermute | solution.py:824
  7.7 0.7 copy-start.3
  8.4 6.9 %collective-permute-start.1 = (s32[1,3]{1,0:T(1,128)S(1)}, s32[1,3]{1,0:T(1,128)S(1)}, u32[]{:S(2)}, u32[]{:S(2)}) collective-permute-start(s32[1,3]{1,0:T(1,128)S(1)} %add_subtract_fusion.1), channel_id=1, source_target_pairs={{0,2},{1,31},{2,4},{3,1},{4,6},{5,3},{6,8},{7,5},{8,10},{9,7},{10,... | collective-permute-start | bytes 44 | tf_op jit(solution)/shard_map/ppermute | solution.py:824
  9.9 6.5 %collective-permute-start = (s32[1,3]{1,0:T(1,128)S(1)}, s32[1,3]{1,0:T(1,128)S(1)}, u32[]{:S(2)}, u32[]{:S(2)}) collective-permute-start(s32[1,3]{1,0:T(1,128)S(1)} %add_subtract_fusion.1), channel_id=1, source_target_pairs={{0,30},{1,3},{2,0},{3,5},{4,2},{5,7},{6,4},{7,9},{8,6},{9,11},{10,... | collective-permute-start | bytes 44 | tf_op jit(solution)/shard_map/ppermute | solution.py:824
  13.8 4.9 %collective-permute-start.5 = (f32[10,16,128]{2,1,0:T(8,128)}, f32[10,16,128]{2,1,0:T(8,128)S(1)}, u32[]{:S(2)}, u32[]{:S(2)}) collective-permute-start(f32[10,16,128]{2,1,0:T(8,128)} %get-tuple-element.24), channel_id=1, source_target_pairs={{0,33},{1,224},{2,35},{3,226},{4,37},{5,228},{6,39},{7,230},{8,41}... | collective-permute-start | bytes 245768 | tf_op jit(solution)/shard_map/ppermute | solution.py:824
  15.3 7.6 %collective-permute-start.6 = (f32[10,16,128]{2,1,0:T(8,128)}, f32[10,16,128]{2,1,0:T(8,128)S(1)}, u32[]{:S(2)}, u32[]{:S(2)}) collective-permute-start(f32[10,16,128]{2,1,0:T(8,128)} %get-tuple-element.25), channel_id=1, source_target_pairs={{0,225},{1,32},{2,227},{3,34},{4,229},{5,36},{6,231},{7,38},{8,233... | collective-permute-start | bytes 245768 | tf_op jit(solution)/shard_map/ppermute | solution.py:824
  16.5 6.4 %collective-permute-start.4 = (f32[16,16,128]{2,1,0:T(8,128)}, f32[16,16,128]{2,1,0:T(8,128)S(1)}, u32[]{:S(2)}, u32[]{:S(2)}) collective-permute-start(f32[16,16,128]{2,1,0:T(8,128)} %get-tuple-element.23), channel_id=1, source_target_pairs={{0,1},{1,0},{2,3},{3,2},{4,5},{5,4},{6,7},{7,6},{8,9},{9,8},{10,11... | collective-permute-start | bytes 393224 | tf_op jit(solution)/shard_map/ppermute | solution.py:824
  23.6 14.9 %collective-permute-start.9 = (f32[24,32,128]{2,1,0:T(8,128)S(1)}, f32[24,32,128]{2,1,0:T(8,128)S(1)}, u32[]{:S(2)}, u32[]{:S(2)}) collective-permute-start(f32[24,32,128]{2,1,0:T(8,128)S(1)} %get-tuple-element.30), channel_id=1, source_target_pairs={{0,2},{1,31},{2,4},{3,1},{4,6},{5,3},{6,8},{7,5},{8,10},{9,7},{10,... | collective-permute-start | bytes 1179656 | tf_op jit(solution)/shard_map/ppermute | solution.py:824
  25.2 13.3 %collective-permute-start.10 = (f32[24,32,128]{2,1,0:T(8,128)S(1)}, f32[24,32,128]{2,1,0:T(8,128)S(1)}, u32[]{:S(2)}, u32[]{:S(2)}) collective-permute-start(f32[24,32,128]{2,1,0:T(8,128)S(1)} %get-tuple-element.31), channel_id=1, source_target_pairs={{0,30},{1,3},{2,0},{3,5},{4,2},{5,7},{6,4},{7,9},{8,6},{9,11},{10,... | collective-permute-start | bytes 1179656 | tf_op jit(solution)/shard_map/ppermute | solution.py:824
  33.1 13.1 %collective-permute-start.7 = (f32[15,40,128]{2,1,0:T(8,128)S(1)}, f32[15,40,128]{2,1,0:T(8,128)S(1)}, u32[]{:S(2)}, u32[]{:S(2)}) collective-permute-start(f32[15,40,128]{2,1,0:T(8,128)S(1)} %get-tuple-element.28), channel_id=1, source_target_pairs={{0,2},{1,31},{2,4},{3,1},{4,6},{5,3},{6,8},{7,5},{8,10},{9,7},{10,... | collective-permute-start | bytes 921608 | tf_op jit(solution)/shard_map/ppermute | solution.py:824
  33.2 13.1 %collective-permute-start.8 = (f32[15,40,128]{2,1,0:T(8,128)S(1)}, f32[15,40,128]{2,1,0:T(8,128)S(1)}, u32[]{:S(2)}, u32[]{:S(2)}) collective-permute-start(f32[15,40,128]{2,1,0:T(8,128)S(1)} %get-tuple-element.29), channel_id=1, source_target_pairs={{0,30},{1,3},{2,0},{3,5},{4,2},{5,7},{6,4},{7,9},{8,6},{9,11},{10,... | collective-permute-start | bytes 921608 | tf_op jit(solution)/shard_map/ppermute | solution.py:824
  79.8 1.3 %collective-permute-start.11 = (f32[16,128]{1,0:T(8,128)S(1)}, f32[16,128]{1,0:T(8,128)S(1)}, u32[]{:S(2)}, u32[]{:S(2)}) collective-permute-start(f32[16,128]{1,0:T(8,128)S(1)} %shard_map.63), channel_id=1, source_target_pairs={{0,1},{1,0},{2,3},{3,2},{4,5},{5,4},{6,7},{7,6},{8,9},{9,8},{10,11... | collective-permute-start | bytes 24584 | tf_op jit(solution)/shard_map/ppermute | solution.py:824
  81.1 5.1 %collective-permute-start.13 = (f32[2,16,128]{2,1,0:T(8,128)S(1)}, f32[2,16,128]{2,1,0:T(8,128)S(1)}, u32[]{:S(2)}, u32[]{:S(2)}) collective-permute-start(f32[2,16,128]{2,1,0:T(8,128)S(1)} %pad_maximum_fusion.1), channel_id=1, source_target_pairs={{0,30},{1,3},{2,0},{3,5},{4,2},{5,7},{6,4},{7,9},{8,6},{9,11},{10,... | collective-permute-start | bytes 49160 | tf_op jit(solution)/shard_map/ppermute | solution.py:824
  84.7 7.1 %collective-permute-start.12 = (f32[2,16,128]{2,1,0:T(8,128)S(1)}, f32[2,16,128]{2,1,0:T(8,128)S(1)}, u32[]{:S(2)}, u32[]{:S(2)}) collective-permute-start(f32[2,16,128]{2,1,0:T(8,128)S(1)} %pad_maximum_fusion.1), channel_id=1, source_target_pairs={{0,2},{1,31},{2,4},{3,1},{4,6},{5,3},{6,8},{7,5},{8,10},{9,7},{10,... | collective-permute-start | bytes 49160 | tf_op jit(solution)/shard_map/ppermute | solution.py:824
  91.8 4.8 %collective-permute-start.15 = (f32[6,16,128]{2,1,0:T(8,128)S(1)}, f32[6,16,128]{2,1,0:T(8,128)S(1)}, u32[]{:S(2)}, u32[]{:S(2)}) collective-permute-start(f32[6,16,128]{2,1,0:T(8,128)S(1)} %pad_maximum_fusion.parts), channel_id=1, source_target_pairs={{0,224},{1,33},{2,226},{3,35},{4,228},{5,37},{6,230},{7,39},{8,232... | collective-permute-start | bytes 147464 | tf_op jit(solution)/shard_map/ppermute | solution.py:824
  94.8 5.3 %collective-permute-start.14 = (f32[6,16,128]{2,1,0:T(8,128)S(1)}, f32[6,16,128]{2,1,0:T(8,128)S(1)}, u32[]{:S(2)}, u32[]{:S(2)}) collective-permute-start(f32[6,16,128]{2,1,0:T(8,128)S(1)} %pad_maximum_fusion.parts), channel_id=1, source_target_pairs={{0,32},{1,225},{2,34},{3,227},{4,36},{5,229},{6,38},{7,231},{8,40}... | collective-permute-start | bytes 147464 | tf_op jit(solution)/shard_map/ppermute | solution.py:824

commit v6 on v5

--- a/solution.py
+++ b/solution.py
@@ -881,10 +881,11 @@
         [scalar, own_u, own_f, r1, r2],
         1 << 33,
     )
-    plane = jnp.stack([delta, send(delta, lambda x, y, z: (x, y, 1 - z))])
-    right = send(plane, lambda x, y, z: (x, y + turn(z), z))
-    left = send(plane, lambda x, y, z: (x, y - turn(z), z))
-    plane = jnp.concatenate([plane, right, left])
+    beside = [delta, send(delta, lambda x, y, z: (x, y, 1 - z))]
+    for step in (1, -1):
+        beside.append(send(delta, lambda x, y, z, step=step: (x, y + step * turn(z), z)))
+        beside.append(send(delta, lambda x, y, z, step=step: (x, y + step * turn(z), 1 - z)))
+    plane = jnp.stack(beside)
     after = send(plane, lambda x, y, z: (x + turn(z), y, z))
     before = send(plane, lambda x, y, z: (x - turn(z), y, z))
     near = call(near_kernel, (BX * BY, 128), [], [scalar, plane], 1 << 29)

time: 103 us -> 102 us (level)
  waiting for transfers between devices: 17.4 us -> 14.1 us
  starting transfers between devices: 30.8 us -> 33 us
    ppermute x16 -> x18, waiting for transfers between devices: 17.4 us -> 14.1 us  [send(): return lax.ppermute(values, AXES, pairs)]
    ppermute x16 -> x18, starting transfers between devices: 30.8 us -> 33 us  [send(): return lax.ppermute(values, AXES, pairs)]
  transfers between devices with their start and end apart: 16 -> 18, of which waited for: 7 -> 6; matrix products, arithmetic and copies ran while one was open for 0% -> 0% of each run, Pallas kernels for 13% -> 13%
where the time goes in v6:
time: 102 us
  Pallas kernels  53 us (52%)
  starting transfers between devices  33 us (32%)
  waiting for transfers between devices  14.1 us (14%)
    pallas_call x7, Pallas kernels, call(): pl.pallas_call(kernel, out_shape=outs, in_specs=specs, out_specs=[pl.Bloc...  53 us
    ppermute x18, starting transfers between devices, send(): return lax.ppermute(values, AXES, pairs)  33 us
    ppermute x18, waiting for transfers between devices, send(): return lax.ppermute(values, AXES, pairs)  14.1 us
  transfers between devices with their start and end apart: 18, of which 6 were waited for; matrix products, arithmetic and copies ran while one was open for 0% of the time, Pallas kernels for 13%

profile of v6, /device:TPU:0, one launch (start us, length us, event | category | flops | bytes accessed | tf_op | source)
XLA Modules:
  0.0 101.8 jit_solution(12681735150554983697)
XLA Ops:
  0.6 0.0 copy-start
  0.6 0.0 copy-start.1
  0.7 0.0 copy-start.2
  0.7 2.7 %shard_map.59 = (f32[67,16,128]{2,1,0:T(8,128)}, f32[67,16,128]{2,1,0:T(8,128)}, f32[16,16,128]{2,1,0:T(8,128)}, f32[10,16,128]{2,1,0:T(8,128)}, f32[10,16,128]{2,1,0:T(8,128)}) custom-call(s32[1]{0:T(128)} %bitcast.sc, f32[3,16,16,128]{3,2,1,0:T(8,128)} %u.7, f32[3,16,16,128]{3,2,1,0:T(8,128)} %f.7, f32[16,16,128]{2,1,0:T(8,128)} %m.9), custom_call_target="tpu_custom_call" | custom-call | flops 1048576 | bytes 1048576 | tf_op jit(solution)/shard_map/pallas_call | solution.py:798
  3.4 0.3 collective-permute-start.2
  3.7 4.0 %collective-permute-start.3 = (f32[67,16,128]{2,1,0:T(8,128)}, f32[67,16,128]{2,1,0:T(8,128)S(1)}, u32[]{:S(2)}, u32[]{:S(2)}) collective-permute-start(f32[67,16,128]{2,1,0:T(8,128)} %get-tuple-element.22), channel_id=1, source_target_pairs={{0,224},{1,33},{2,226},{3,35},{4,228},{5,37},{6,230},{7,39},{8,232... | collective-permute-start | bytes 1646600 | tf_op jit(solution)/shard_map/ppermute | solution.py:824
  7.7 0.0 copy-start.3
  7.7 0.7 copy-done.3
  8.3 0.1 add_subtract_fusion.1
  8.4 1.5 %collective-permute-start.1 = (s32[1,3]{1,0:T(1,128)S(1)}, s32[1,3]{1,0:T(1,128)S(1)}, u32[]{:S(2)}, u32[]{:S(2)}) collective-permute-start(s32[1,3]{1,0:T(1,128)S(1)} %add_subtract_fusion.1), channel_id=1, source_target_pairs={{0,2},{1,31},{2,4},{3,1},{4,6},{5,3},{6,8},{7,5},{8,10},{9,7},{10,... | collective-permute-start | bytes 44 | tf_op jit(solution)/shard_map/ppermute | solution.py:824
  9.9 3.9 %collective-permute-start = (s32[1,3]{1,0:T(1,128)S(1)}, s32[1,3]{1,0:T(1,128)S(1)}, u32[]{:S(2)}, u32[]{:S(2)}) collective-permute-start(s32[1,3]{1,0:T(1,128)S(1)} %add_subtract_fusion.1), channel_id=1, source_target_pairs={{0,30},{1,3},{2,0},{3,5},{4,2},{5,7},{6,4},{7,9},{8,6},{9,11},{10,... | collective-permute-start | bytes 44 | tf_op jit(solution)/shard_map/ppermute | solution.py:824
  13.8 0.0 collective-permute-start.5
  13.8 1.5 %collective-permute-done.1 = s32[1,3]{1,0:T(1,128)S(1)} collective-permute-done((s32[1,3]{1,0:T(1,128)S(1)}, s32[1,3]{1,0:T(1,128)S(1)}, u32[]{:S(2)}, u32[]{:S(2)}) %collective-permute-start.1) | collective-permute-done | bytes 44 | tf_op jit(solution)/shard_map/ppermute | solution.py:824
  15.3 1.2 %collective-permute-start.6 = (f32[10,16,128]{2,1,0:T(8,128)}, f32[10,16,128]{2,1,0:T(8,128)S(1)}, u32[]{:S(2)}, u32[]{:S(2)}) collective-permute-start(f32[10,16,128]{2,1,0:T(8,128)} %get-tuple-element.25), channel_id=1, source_target_pairs={{0,225},{1,32},{2,227},{3,34},{4,229},{5,36},{6,231},{7,38},{8,233... | collective-permute-start | bytes 245768 | tf_op jit(solution)/shard_map/ppermute | solution.py:824
  16.4 0.0 collective-permute-done
  16.4 2.1 %collective-permute-start.4 = (f32[16,16,128]{2,1,0:T(8,128)}, f32[16,16,128]{2,1,0:T(8,128)S(1)}, u32[]{:S(2)}, u32[]{:S(2)}) collective-permute-start(f32[16,16,128]{2,1,0:T(8,128)} %get-tuple-element.23), channel_id=1, source_target_pairs={{0,1},{1,0},{2,3},{3,2},{4,5},{5,4},{6,7},{7,6},{8,9},{9,8},{10,11... | collective-permute-start | bytes 393224 | tf_op jit(solution)/shard_map/ppermute | solution.py:824
  18.5 0.1 add_subtract_fusion
  18.6 0.1 concatenate.5.sc
  18.7 0.0 collective-permute-done.5.strip1
  18.7 4.2 %collective-permute-done.6.strip2 = f32[10,16,128]{2,1,0:T(8,128)S(1)} collective-permute-done((f32[10,16,128]{2,1,0:T(8,128)}, f32[10,16,128]{2,1,0:T(8,128)S(1)}, u32[]{:S(2)}, u32[]{:S(2)}) %collective-permute-start.6) | collective-permute-done | bytes 81952 | tf_op jit(solution)/shard_map/ppermute | solution.py:824
  22.9 0.0 collective-permute-done.4.strip
  22.9 0.0 collective-permute-done.2.x1
  22.9 0.0 collective-permute-done.3.x2
  22.9 0.0 copy-done
  22.9 0.0 copy-done.1
  22.9 0.0 copy-done.2
  22.9 0.7 shard_map.61
  23.6 1.6 %collective-permute-start.9 = (f32[24,32,128]{2,1,0:T(8,128)S(1)}, f32[24,32,128]{2,1,0:T(8,128)S(1)}, u32[]{:S(2)}, u32[]{:S(2)}) collective-permute-start(f32[24,32,128]{2,1,0:T(8,128)S(1)} %get-tuple-element.30), channel_id=1, source_target_pairs={{0,2},{1,31},{2,4},{3,1},{4,6},{5,3},{6,8},{7,5},{8,10},{9,7},{10,... | collective-permute-start | bytes 1179656 | tf_op jit(solution)/shard_map/ppermute | solution.py:824
  25.2 3.9 %collective-permute-start.10 = (f32[24,32,128]{2,1,0:T(8,128)S(1)}, f32[24,32,128]{2,1,0:T(8,128)S(1)}, u32[]{:S(2)}, u32[]{:S(2)}) collective-permute-start(f32[24,32,128]{2,1,0:T(8,128)S(1)} %get-tuple-element.31), channel_id=1, source_target_pairs={{0,30},{1,3},{2,0},{3,5},{4,2},{5,7},{6,4},{7,9},{8,6},{9,11},{10,... | collective-permute-start | bytes 1179656 | tf_op jit(solution)/shard_map/ppermute | solution.py:824
  29.1 4.0 %shard_map.60 = (f32[30,16,128]{2,1,0:T(8,128)S(1)}, f32[30,16,128]{2,1,0:T(8,128)S(1)}, f32[15,40,128]{2,1,0:T(8,128)S(1)}, f32[15,40,128]{2,1,0:T(8,128)S(1)}) custom-call(s32[16]{0:T(128)S(1)} %concatenate.5.sc, f32[3,16,16,128]{3,2,1,0:T(8,128)S(1)} %copy-done, f32[3,16,16,128]{3,2,1,0:T(8,128)S(1)} %copy-done.1, f32[16,16,128]{2,1,0:T(8,128)S(1)} %copy-done.2, ...), custom_call_target="tpu_custom_call" | custom-call | flops 2147483648 | bytes 1048576 | tf_op jit(solution)/shard_map/pallas_call | solution.py:798
  33.1 0.1 collective-permute-start.7
  33.2 5.3 %collective-permute-start.8 = (f32[15,40,128]{2,1,0:T(8,128)S(1)}, f32[15,40,128]{2,1,0:T(8,128)S(1)}, u32[]{:S(2)}, u32[]{:S(2)}) collective-permute-start(f32[15,40,128]{2,1,0:T(8,128)S(1)} %get-tuple-element.29), channel_id=1, source_target_pairs={{0,30},{1,3},{2,0},{3,5},{4,2},{5,7},{6,4},{7,9},{8,6},{9,11},{10,... | collective-permute-start | bytes 921608 | tf_op jit(solution)/shard_map/ppermute | solution.py:824
  38.5 0.0 collective-permute-done.9.s1
  38.5 0.0 collective-permute-done.10.s2
  38.5 7.7 %shard_map.62 = f32[3,16,16,128]{3,2,1,0:T(8,128)} custom-call(s32[16]{0:T(128)S(1)} %concatenate.5.sc, f32[3,16,16,128]{3,2,1,0:T(8,128)S(1)} %copy-done, f32[3,16,16,128]{3,2,1,0:T(8,128)S(1)} %copy-done.1, f32[16,16,128]{2,1,0:T(8,128)S(1)} %copy-done.2, f32[67,16,128]{2,1,0:T(8,128)S(1)} %collective-permute-done.2.x1, ...), custom_call_target="tpu_custom_call" | custom-call | flops 4294967296 | bytes 1048576 | tf_op jit(solution)/shard_map/pallas_call | solution.py:798
  46.2 0.0 collective-permute-done.7.r1
  46.2 0.0 collective-permute-done.8.r2
  46.2 33.6 %shard_map.63 = f32[16,128]{1,0:T(8,128)S(1)} custom-call(s32[16]{0:T(128)S(1)} %concatenate.5.sc, f32[30,16,128]{2,1,0:T(8,128)S(1)} %get-tuple-element.33.own_u, f32[30,16,128]{2,1,0:T(8,128)S(1)} %get-tuple-element.34.own_f, f32[15,40,128]{2,1,0:T(8,128)S(1)} %collective-permute-done.7.r1, f32[15,40,128]{2,1,0:T(8,128)S(1)} %collective-permute-done.8.r2), custom_call_target="tpu_custom_call" | custom-call | flops 8589934592 | bytes 1048576 | tf_op jit(solution)/shard_map/pallas_call | solution.py:798
  79.8 2.7 %collective-permute-start.15 = (f32[16,128]{1,0:T(8,128)S(1)}, f32[16,128]{1,0:T(8,128)S(1)}, u32[]{:S(2)}, u32[]{:S(2)}) collective-permute-start(f32[16,128]{1,0:T(8,128)S(1)} %shard_map.63), channel_id=1, source_target_pairs={{0,31},{1,2},{2,1},{3,4},{4,3},{5,6},{6,5},{7,8},{8,7},{9,10},{10,... | collective-permute-start | bytes 24584 | tf_op jit(solution)/shard_map/ppermute | solution.py:824
  82.5 1.2 %collective-permute-start.14 = (f32[16,128]{1,0:T(8,128)S(1)}, f32[16,128]{1,0:T(8,128)S(1)}, u32[]{:S(2)}, u32[]{:S(2)}) collective-permute-start(f32[16,128]{1,0:T(8,128)S(1)} %shard_map.63), channel_id=1, source_target_pairs={{0,30},{1,3},{2,0},{3,5},{4,2},{5,7},{6,4},{7,9},{8,6},{9,11},{10,... | collective-permute-start | bytes 24584 | tf_op jit(solution)/shard_map/ppermute | solution.py:824
  83.6 0.0 collective-permute-start.13
  83.6 0.9 collective-permute-start.12
  84.5 1.5 %collective-permute-start.11 = (f32[16,128]{1,0:T(8,128)S(1)}, f32[16,128]{1,0:T(8,128)S(1)}, u32[]{:S(2)}, u32[]{:S(2)}) collective-permute-start(f32[16,128]{1,0:T(8,128)S(1)} %shard_map.63), channel_id=1, source_target_pairs={{0,1},{1,0},{2,3},{3,2},{4,5},{5,4},{6,7},{7,6},{8,9},{9,8},{10,11... | collective-permute-start | bytes 24584 | tf_op jit(solution)/shard_map/ppermute | solution.py:824
  86.0 0.8 collective-permute-done.11
  86.8 3.8 %collective-permute-done.12 = f32[16,128]{1,0:T(8,128)S(1)} collective-permute-done((f32[16,128]{1,0:T(8,128)S(1)}, f32[16,128]{1,0:T(8,128)S(1)}, u32[]{:S(2)}, u32[]{:S(2)}) %collective-permute-start.12) | collective-permute-done | bytes 8224 | tf_op jit(solution)/shard_map/ppermute | solution.py:824
  90.6 0.0 collective-permute-done.13
  90.6 0.0 collective-permute-done.14
  90.6 0.0 collective-permute-done.15
  90.7 3.1 %collective-permute-start.17 = (f32[6,16,128]{2,1,0:T(8,128)S(1)}, f32[6,16,128]{2,1,0:T(8,128)S(1)}, u32[]{:S(2)}, u32[]{:S(2)}) collective-permute-start(f32[6,16,128]{2,1,0:T(8,128)S(1)} %constant_dynamic-update-slice_fusion.parts), channel_id=1, source_target_pairs={{0,224},{1,33},{2,226},{3,35},{4,228},{5,37},{6,230},{7,39},{8,232... | collective-permute-start | bytes 147464 | tf_op jit(solution)/shard_map/ppermute | solution.py:824
  93.7 0.0 collective-permute-start.16
  93.7 1.5 %shard_map.64.near = f32[256,128]{1,0:T(8,128)S(1)} custom-call(s32[16]{0:T(128)S(1)} %concatenate.5.sc, f32[6,16,128]{2,1,0:T(8,128)S(1)} %constant_dynamic-update-slice_fusion.parts), custom_call_target="tpu_custom_call" | custom-call | flops 536870912 | bytes 1048576 | tf_op jit(solution)/shard_map/pallas_call | solution.py:798
  95.2 0.3 collective-permute-done.17.parts2
  95.5 3.5 %collective-permute-done.16.parts1 = f32[6,16,128]{2,1,0:T(8,128)S(1)} collective-permute-done((f32[6,16,128]{2,1,0:T(8,128)S(1)}, f32[6,16,128]{2,1,0:T(8,128)S(1)}, u32[]{:S(2)}, u32[]{:S(2)}) %collective-permute-start.16) | collective-permute-done | bytes 49184 | tf_op jit(solution)/shard_map/ppermute | solution.py:824
  99.0 2.8 %shard_map.65 = f32[16,16,128]{2,1,0:T(8,128)} custom-call(s32[16]{0:T(128)S(1)} %concatenate.5.sc, f32[16,16,128]{2,1,0:T(8,128)S(1)} %copy-done.2, f32[256,128]{1,0:T(8,128)S(1)} %shard_map.64.near, f32[6,16,128]{2,1,0:T(8,128)S(1)} %collective-permute-done.16.parts1, f32[6,16,128]{2,1,0:T(8,128)S(1)} %collective-permute-done.17.parts2), custom_call_target="tpu_custom_call" | custom-call | flops 16777216 | bytes 1048576 | tf_op jit(solution)/shard_map/pallas_call | solution.py:798
  (6 shorter events, 0.0 us)
Async XLA Ops:
  0.6 22.2 %copy-start = (f32[3,16,16,128]{3,2,1,0:T(8,128)S(1)}, f32[3,16,16,128]{3,2,1,0:T(8,128)}, u32[]{:S(2)}) copy-start(f32[3,16,16,128]{3,2,1,0:T(8,128)} %u.7) | copy-start | bytes 1179652
  0.6 22.2 %copy-start.1 = (f32[3,16,16,128]{3,2,1,0:T(8,128)S(1)}, f32[3,16,16,128]{3,2,1,0:T(8,128)}, u32[]{:S(2)}) copy-start(f32[3,16,16,128]{3,2,1,0:T(8,128)} %f.7) | copy-start | bytes 1179652
  0.7 22.2 %copy-start.2 = (f32[16,16,128]{2,1,0:T(8,128)S(1)}, f32[16,16,128]{2,1,0:T(8,128)}, u32[]{:S(2)}) copy-start(f32[16,16,128]{2,1,0:T(8,128)} %m.9) | copy-start | bytes 393220
  3.4 19.5 %collective-permute-start.2 = (f32[67,16,128]{2,1,0:T(8,128)}, f32[67,16,128]{2,1,0:T(8,128)S(1)}, u32[]{:S(2)}, u32[]{:S(2)}) collective-permute-start(f32[67,16,128]{2,1,0:T(8,128)} %get-tuple-element.21), channel_id=1, source_target_pairs={{0,32},{1,225},{2,34},{3,227},{4,36},{5,229},{6,38},{7,231},{8,40}... | collective-permute-start | bytes 1646600 | tf_op jit(solution)/shard_map/ppermute | solution.py:824
  3.7 19.2 %collective-permute-start.3 = (f32[67,16,128]{2,1,0:T(8,128)}, f32[67,16,128]{2,1,0:T(8,128)S(1)}, u32[]{:S(2)}, u32[]{:S(2)}) collective-permute-start(f32[67,16,128]{2,1,0:T(8,128)} %get-tuple-element.22), channel_id=1, source_target_pairs={{0,224},{1,33},{2,226},{3,35},{4,228},{5,37},{6,230},{7,39},{8,232... | collective-permute-start | bytes 1646600 | tf_op jit(solution)/shard_map/ppermute | solution.py:824
  7.7 0.7 copy-start.3
  8.4 6.9 %collective-permute-start.1 = (s32[1,3]{1,0:T(1,128)S(1)}, s32[1,3]{1,0:T(1,128)S(1)}, u32[]{:S(2)}, u32[]{:S(2)}) collective-permute-start(s32[1,3]{1,0:T(1,128)S(1)} %add_subtract_fusion.1), channel_id=1, source_target_pairs={{0,2},{1,31},{2,4},{3,1},{4,6},{5,3},{6,8},{7,5},{8,10},{9,7},{10,... | collective-permute-start | bytes 44 | tf_op jit(solution)/shard_map/ppermute | solution.py:824
  9.9 6.5 %collective-permute-start = (s32[1,3]{1,0:T(1,128)S(1)}, s32[1,3]{1,0:T(1,128)S(1)}, u32[]{:S(2)}, u32[]{:S(2)}) collective-permute-start(s32[1,3]{1,0:T(1,128)S(1)} %add_subtract_fusion.1), channel_id=1, source_target_pairs={{0,30},{1,3},{2,0},{3,5},{4,2},{5,7},{6,4},{7,9},{8,6},{9,11},{10,... | collective-permute-start | bytes 44 | tf_op jit(solution)/shard_map/ppermute | solution.py:824
  13.8 4.9 %collective-permute-start.5 = (f32[10,16,128]{2,1,0:T(8,128)}, f32[10,16,128]{2,1,0:T(8,128)S(1)}, u32[]{:S(2)}, u32[]{:S(2)}) collective-permute-start(f32[10,16,128]{2,1,0:T(8,128)} %get-tuple-element.24), channel_id=1, source_target_pairs={{0,33},{1,224},{2,35},{3,226},{4,37},{5,228},{6,39},{7,230},{8,41}... | collective-permute-start | bytes 245768 | tf_op jit(solution)/shard_map/ppermute | solution.py:824
  15.3 7.6 %collective-permute-start.6 = (f32[10,16,128]{2,1,0:T(8,128)}, f32[10,16,128]{2,1,0:T(8,128)S(1)}, u32[]{:S(2)}, u32[]{:S(2)}) collective-permute-start(f32[10,16,128]{2,1,0:T(8,128)} %get-tuple-element.25), channel_id=1, source_target_pairs={{0,225},{1,32},{2,227},{3,34},{4,229},{5,36},{6,231},{7,38},{8,233... | collective-permute-start | bytes 245768 | tf_op jit(solution)/shard_map/ppermute | solution.py:824
  16.4 6.4 %collective-permute-start.4 = (f32[16,16,128]{2,1,0:T(8,128)}, f32[16,16,128]{2,1,0:T(8,128)S(1)}, u32[]{:S(2)}, u32[]{:S(2)}) collective-permute-start(f32[16,16,128]{2,1,0:T(8,128)} %get-tuple-element.23), channel_id=1, source_target_pairs={{0,1},{1,0},{2,3},{3,2},{4,5},{5,4},{6,7},{7,6},{8,9},{9,8},{10,11... | collective-permute-start | bytes 393224 | tf_op jit(solution)/shard_map/ppermute | solution.py:824
  23.6 14.9 %collective-permute-start.9 = (f32[24,32,128]{2,1,0:T(8,128)S(1)}, f32[24,32,128]{2,1,0:T(8,128)S(1)}, u32[]{:S(2)}, u32[]{:S(2)}) collective-permute-start(f32[24,32,128]{2,1,0:T(8,128)S(1)} %get-tuple-element.30), channel_id=1, source_target_pairs={{0,2},{1,31},{2,4},{3,1},{4,6},{5,3},{6,8},{7,5},{8,10},{9,7},{10,... | collective-permute-start | bytes 1179656 | tf_op jit(solution)/shard_map/ppermute | solution.py:824
  25.2 13.3 %collective-permute-start.10 = (f32[24,32,128]{2,1,0:T(8,128)S(1)}, f32[24,32,128]{2,1,0:T(8,128)S(1)}, u32[]{:S(2)}, u32[]{:S(2)}) collective-permute-start(f32[24,32,128]{2,1,0:T(8,128)S(1)} %get-tuple-element.31), channel_id=1, source_target_pairs={{0,30},{1,3},{2,0},{3,5},{4,2},{5,7},{6,4},{7,9},{8,6},{9,11},{10,... | collective-permute-start | bytes 1179656 | tf_op jit(solution)/shard_map/ppermute | solution.py:824
  33.1 13.1 %collective-permute-start.7 = (f32[15,40,128]{2,1,0:T(8,128)S(1)}, f32[15,40,128]{2,1,0:T(8,128)S(1)}, u32[]{:S(2)}, u32[]{:S(2)}) collective-permute-start(f32[15,40,128]{2,1,0:T(8,128)S(1)} %get-tuple-element.28), channel_id=1, source_target_pairs={{0,2},{1,31},{2,4},{3,1},{4,6},{5,3},{6,8},{7,5},{8,10},{9,7},{10,... | collective-permute-start | bytes 921608 | tf_op jit(solution)/shard_map/ppermute | solution.py:824
  33.2 13.1 %collective-permute-start.8 = (f32[15,40,128]{2,1,0:T(8,128)S(1)}, f32[15,40,128]{2,1,0:T(8,128)S(1)}, u32[]{:S(2)}, u32[]{:S(2)}) collective-permute-start(f32[15,40,128]{2,1,0:T(8,128)S(1)} %get-tuple-element.29), channel_id=1, source_target_pairs={{0,30},{1,3},{2,0},{3,5},{4,2},{5,7},{6,4},{7,9},{8,6},{9,11},{10,... | collective-permute-start | bytes 921608 | tf_op jit(solution)/shard_map/ppermute | solution.py:824
  79.8 10.8 %collective-permute-start.15 = (f32[16,128]{1,0:T(8,128)S(1)}, f32[16,128]{1,0:T(8,128)S(1)}, u32[]{:S(2)}, u32[]{:S(2)}) collective-permute-start(f32[16,128]{1,0:T(8,128)S(1)} %shard_map.63), channel_id=1, source_target_pairs={{0,31},{1,2},{2,1},{3,4},{4,3},{5,6},{6,5},{7,8},{8,7},{9,10},{10,... | collective-permute-start | bytes 24584 | tf_op jit(solution)/shard_map/ppermute | solution.py:824
  82.5 8.1 %collective-permute-start.14 = (f32[16,128]{1,0:T(8,128)S(1)}, f32[16,128]{1,0:T(8,128)S(1)}, u32[]{:S(2)}, u32[]{:S(2)}) collective-permute-start(f32[16,128]{1,0:T(8,128)S(1)} %shard_map.63), channel_id=1, source_target_pairs={{0,30},{1,3},{2,0},{3,5},{4,2},{5,7},{6,4},{7,9},{8,6},{9,11},{10,... | collective-permute-start | bytes 24584 | tf_op jit(solution)/shard_map/ppermute | solution.py:824
  83.6 7.0 %collective-permute-start.13 = (f32[16,128]{1,0:T(8,128)S(1)}, f32[16,128]{1,0:T(8,128)S(1)}, u32[]{:S(2)}, u32[]{:S(2)}) collective-permute-start(f32[16,128]{1,0:T(8,128)S(1)} %shard_map.63), channel_id=1, source_target_pairs={{0,3},{1,30},{2,5},{3,0},{4,7},{5,2},{6,9},{7,4},{8,11},{9,6},{10,... | collective-permute-start | bytes 24584 | tf_op jit(solution)/shard_map/ppermute | solution.py:824
  83.6 7.0 %collective-permute-start.12 = (f32[16,128]{1,0:T(8,128)S(1)}, f32[16,128]{1,0:T(8,128)S(1)}, u32[]{:S(2)}, u32[]{:S(2)}) collective-permute-start(f32[16,128]{1,0:T(8,128)S(1)} %shard_map.63), channel_id=1, source_target_pairs={{0,2},{1,31},{2,4},{3,1},{4,6},{5,3},{6,8},{7,5},{8,10},{9,7},{10,... | collective-permute-start | bytes 24584 | tf_op jit(solution)/shard_map/ppermute | solution.py:824
  84.5 2.3 %collective-permute-start.11 = (f32[16,128]{1,0:T(8,128)S(1)}, f32[16,128]{1,0:T(8,128)S(1)}, u32[]{:S(2)}, u32[]{:S(2)}) collective-permute-start(f32[16,128]{1,0:T(8,128)S(1)} %shard_map.63), channel_id=1, source_target_pairs={{0,1},{1,0},{2,3},{3,2},{4,5},{5,4},{6,7},{7,6},{8,9},{9,8},{10,11... | collective-permute-start | bytes 24584 | tf_op jit(solution)/shard_map/ppermute | solution.py:824
  90.7 4.8 %collective-permute-start.17 = (f32[6,16,128]{2,1,0:T(8,128)S(1)}, f32[6,16,128]{2,1,0:T(8,128)S(1)}, u32[]{:S(2)}, u32[]{:S(2)}) collective-permute-start(f32[6,16,128]{2,1,0:T(8,128)S(1)} %constant_dynamic-update-slice_fusion.parts), channel_id=1, source_target_pairs={{0,224},{1,33},{2,226},{3,35},{4,228},{5,37},{6,230},{7,39},{8,232... | collective-permute-start | bytes 147464 | tf_op jit(solution)/shard_map/ppermute | solution.py:824
  93.7 5.3 %collective-permute-start.16 = (f32[6,16,128]{2,1,0:T(8,128)S(1)}, f32[6,16,128]{2,1,0:T(8,128)S(1)}, u32[]{:S(2)}, u32[]{:S(2)}) collective-permute-start(f32[6,16,128]{2,1,0:T(8,128)S(1)} %constant_dynamic-update-slice_fusion.parts), channel_id=1, source_target_pairs={{0,32},{1,225},{2,34},{3,227},{4,36},{5,229},{6,38},{7,231},{8,40}... | collective-permute-start | bytes 147464 | tf_op jit(solution)/shard_map/ppermute | solution.py:824
